TPU v7x, 128 devices: a whole 4x4x4 slice. The times are simulated.
128 devices in a mesh: dp: 8 (over z, core), seq: 16 (over y, x).
Axes of the slice: x: 4, y: 4, z: 4, core: 2. Of those that a mesh axis runs over, the one named last changes fastest.
Arguments:
- hidden: bfloat16 [8, 2048, 1536], P('dp', 'seq'), may hold values from -6 to 6
- segments: int32 [8, 2048], P('dp', 'seq'), may hold values from 0 to 3, as said below
- pre_gain: bfloat16 [1536], P(('dp', 'seq')), may hold values from 0.5 to 1.5
- w_in: bfloat16 [1536, 6448], P(('dp', 'seq')), may hold values from -0.15625 to 0.15625
- conv_weight: bfloat16 [4, 3328], P(None, ('dp', 'seq')), may hold values from -3 to 3
- conv_bias: bfloat16 [3328], P(('dp', 'seq')), may hold values from -3 to 3
- dt_bias: float32 [48], replicated, may hold values from -8 to -5
- a_log: float32 [48], replicated, may hold values from -1 to 3
- d_skip: float32 [48], replicated, may hold values from 0.5 to 1.5
- gate_gain: bfloat16 [3072], P(('dp', 'seq')), may hold values from 0.5 to 1.5
- w_out: bfloat16 [3072, 1536], P(('dp', 'seq')), may hold values from -0.109375 to 0.109375
- grad_out: bfloat16 [8, 2048, 1536], P('dp', 'seq'), may hold values from -6 to 6
Outputs:
- block_out: bfloat16 [8, 2048, 1536], P('dp', 'seq')
- grad_hidden: bfloat16 [8, 2048, 1536], P('dp', 'seq')
- grad_pre_gain: float32 [1536], P(('dp', 'seq'))
- grad_w_in: float32 [1536, 6448], P(('dp', 'seq'))
- grad_conv_weight: float32 [4, 3328], P(None, ('dp', 'seq'))
- grad_conv_bias: float32 [3328], P(('dp', 'seq'))
- grad_dt_bias: float32 [48], replicated
- grad_a_log: float32 [48], replicated
- grad_d_skip: float32 [48], replicated
- grad_gate_gain: float32 [3072], P(('dp', 'seq'))
- grad_w_out: float32 [3072, 1536], P(('dp', 'seq'))
Inputs may be any that keep to these rules, and one draw needn't show every extreme that they name: `segments`: in every sequence the segment numbers rise from 0 to 3 along the positions, one number per document; every document has 102 or more positions and exactly one has 1024.
All inputs are finite; a program needn't handle non-finite values.
Results may differ from a plain program's by a relative error of at most 0.015.
Values may be sent and summed in bfloat16 or wider, within the bound.
No kernel may reach another device: no remote copies, remote signals or barrier semaphores. Data moves between devices by JAX's collectives and lax.ppermute only.
A program may use at most 192 MiB of HBM per device.

v0:
```python
from functools import partial

import jax
import jax.numpy as jnp
from jax import lax
from jax.sharding import PartitionSpec as P

INNER = 3072
HEADDIM = 64
STATE = 128
CONV = 4
HEADS = 48
CONV_CH = 3328


epsilon = 1e-05
highest = lax.Precision.HIGHEST


def passed_along(value, axis, steps):
    count = lax.axis_size(axis)
    initial, last = (max(0, -steps), min(count, count - steps))
    return lax.ppermute(value, axis, [(source, source + steps) for source in range(initial, last)])


def entering(shard, axis, join, neutral):
    place = lax.axis_index(axis)
    gathered = jax.tree.map(
        lambda a, kind: lax.all_gather(a.astype(kind), axis),
        shard,
        (jnp.bfloat16, jnp.bfloat16, jnp.bfloat16, jnp.bfloat16),
    )
    state = jax.tree.map(lambda a, e: jnp.zeros_like(a) + jnp.asarray(e, a.dtype), shard, neutral)

    def one(step, state):
        return join(
            state,
            jax.tree.map(
                lambda a, own: lax.dynamic_index_in_dim(a, step, 0, False).astype(own.dtype),
                gathered,
                shard,
            ),
        )

    return lax.fori_loop(0, place, one, state)


def entering_2(shard, axis, join, neutral):
    count = lax.axis_size(axis)
    place = lax.axis_index(axis)
    ahead = count - 1 - place
    gathered = jax.tree.map(
        lambda a, kind: lax.all_gather(a.astype(kind), axis),
        shard,
        jax.tree.map(lambda a: jnp.bfloat16 if a.dtype == jnp.float32 else a.dtype, shard),
    )
    state = jax.tree.map(lambda a, e: jnp.zeros_like(a) + jnp.asarray(e, a.dtype), shard, neutral)

    def one(step, state):
        source = count - 1 - step
        return join(
            state,
            jax.tree.map(
                lambda a, own: lax.dynamic_index_in_dim(a, source, 0, False).astype(own.dtype),
                gathered,
                shard,
            ),
        )

    return lax.fori_loop(0, ahead, one, state)


def norm_in(tokens, pre_gain):
    variance = jnp.mean(tokens * tokens, axis=-1, keepdims=True)
    return tokens * lax.rsqrt(variance + epsilon) * pre_gain[None, :]


def conv_section(xbc_ext, conv_weight, conv_bias):
    length = xbc_ext.shape[0] - (CONV - 1)
    conv_sum = conv_bias[None, :] + conv_weight[0][None, :] * xbc_ext[0:length]
    for offset in range(1, CONV):
        conv_sum = conv_sum + conv_weight[offset][None, :] * xbc_ext[offset : offset + length]
    active = jax.nn.silu(conv_sum)
    x_heads = active[:, :INNER].reshape(length, HEADS, HEADDIM)
    b_rows = active[:, INNER : INNER + STATE]
    c_rows = active[:, INNER + STATE :]
    return (x_heads, b_rows, c_rows)


def decay_section(dt_raw, dt_bias, a_log):
    step_size = jax.nn.softplus(dt_raw + dt_bias[None, :])
    log_decay = -step_size * jnp.exp(a_log)[None, :]
    return (step_size, log_decay)


def intra_block(x_heads, step_size, log_decay, b_rows, c_rows, segment):
    cumulative = jnp.cumsum(log_decay, axis=0)
    length = segment.shape[0]
    places = jnp.arange(length)
    allowed = (segment[:, None] == segment[None, :]) & (places[:, None] >= places[None, :])
    spread = cumulative[:, None, :] - cumulative[None, :, :]
    kernel = jnp.exp(jnp.where(allowed[:, :, None], spread, -jnp.inf))
    scores = jnp.dot(c_rows, b_rows.T, precision=highest, preferred_element_type=jnp.float32)
    mixing = scores[:, :, None] * kernel * step_size[None, :, :]
    y_inner = jnp.einsum("tsh,shp->thp", mixing, x_heads, precision=highest)
    same_end = (segment == segment[-1])[:, None]
    to_end = jnp.exp(jnp.where(same_end, cumulative[-1][None, :] - cumulative, -jnp.inf))
    weighted = (to_end * step_size)[:, :, None] * x_heads
    local_state = jnp.einsum("shp,sn->hpn", weighted, b_rows, precision=highest)
    whole_decay = jnp.exp(cumulative[-1]) * (segment[0] == segment[-1]).astype(jnp.float32)
    entry_decay = jnp.exp(cumulative) * (segment == segment[0]).astype(jnp.float32)[:, None]
    return (y_inner, local_state, whole_decay, entry_decay)


def gated_finish(y_ssd, x_heads, z_gate, d_skip, gate_gain):
    y_full = (y_ssd + d_skip[None, :, None] * x_heads).reshape(-1, INNER)
    gated = y_full * jax.nn.silu(z_gate)
    variance = jnp.mean(gated * gated, axis=-1, keepdims=True)
    return gated * lax.rsqrt(variance + epsilon) * gate_gain[None, :]


def local_branch(
    xbc_ext,
    z_gate,
    dt_raw,
    conv_weight,
    conv_bias,
    dt_bias,
    a_log,
    d_skip,
    gate_gain,
    start_state,
    segment,
):
    x_heads, b_rows, c_rows = conv_section(xbc_ext, conv_weight, conv_bias)
    step_size, log_decay = decay_section(dt_raw, dt_bias, a_log)
    y_inner, local_state, whole_decay, entry_decay = intra_block(
        x_heads, step_size, log_decay, b_rows, c_rows, segment
    )
    from_state = jnp.einsum("tn,hpn->thp", c_rows, start_state, precision=highest)
    y_ssd = y_inner + entry_decay[:, :, None] * from_state
    normed_out = gated_finish(y_ssd, x_heads, z_gate, d_skip, gate_gain)
    end_state = local_state + whole_decay[:, None, None] * start_state
    return (normed_out, end_state)


def join_forward(earlier, latter):
    early_decay, early_state, early_first, early_last = earlier
    late_decay, late_state, late_first, late_last = latter
    linked = ((early_last == late_first) | (early_last < 0.0) | (late_first < 0.0)).astype(
        jnp.float32
    )
    joined_decay = late_decay * early_decay * linked
    joined_state = late_state + (late_decay * linked)[:, None, None] * early_state
    joined_first = jnp.where(early_first < 0.0, late_first, early_first)
    joined_last = jnp.where(late_last < 0.0, early_last, late_last)
    return (joined_decay, joined_state, joined_first, joined_last)


def join_backward(earlier, latter):
    early_decay, early_grad = earlier
    late_decay, late_grad = latter
    return (late_decay * early_decay, late_grad + late_decay[:, None, None] * early_grad)


def local(
    hidden,
    segments,
    pre_gain,
    w_in,
    conv_weight,
    conv_bias,
    dt_bias,
    a_log,
    d_skip,
    gate_gain,
    w_out,
    grad_out,
):
    shards = (pre_gain, w_in, conv_weight, conv_bias, gate_gain, w_out)
    gathered = (
        lax.all_gather(shards[0], ("dp", "seq"), axis=0, tiled=True),
        lax.all_gather(shards[1], ("dp", "seq"), axis=0, tiled=True),
        lax.all_gather(shards[2], ("dp", "seq"), axis=1, tiled=True),
        lax.all_gather(shards[3], ("dp", "seq"), axis=0, tiled=True),
        lax.all_gather(shards[4], ("dp", "seq"), axis=0, tiled=True),
        lax.all_gather(shards[5], ("dp", "seq"), axis=0, tiled=True),
    )
    gain_full, w_in_full, conv_full, bias_full, gate_full, w_out_full = gathered
    tokens = hidden[0].astype(jnp.float32)
    segment = segments[0]
    normed_low = norm_in(tokens, gain_full.astype(jnp.float32)).astype(jnp.bfloat16)
    projected = jnp.dot(normed_low, w_in_full, preferred_element_type=jnp.float32).astype(
        jnp.bfloat16
    )
    conv_low = projected[:, INNER : INNER + CONV_CH]
    rim_rows = passed_along(conv_low[conv_low.shape[0] - (CONV - 1) :], "seq", 1)
    xbc_ext = jnp.concatenate([rim_rows, conv_low], axis=0).astype(jnp.float32)
    z_gate = projected[:, :INNER].astype(jnp.float32)
    dt_raw = projected[:, INNER + CONV_CH :].astype(jnp.float32)
    x_heads, b_rows, c_rows = conv_section(
        xbc_ext, conv_full.astype(jnp.float32), bias_full.astype(jnp.float32)
    )
    step_size, log_decay = decay_section(dt_raw, dt_bias, a_log)
    y_inner, local_state, whole_decay, entry_decay = intra_block(
        x_heads, step_size, log_decay, b_rows, c_rows, segment
    )
    first_seg = segment[0:1].astype(jnp.float32)
    last_seg = segment[segment.shape[0] - 1 :].astype(jnp.float32)
    identity = (
        jnp.ones_like(whole_decay),
        jnp.zeros_like(local_state),
        -jnp.ones((1,), jnp.float32),
        -jnp.ones((1,), jnp.float32),
    )
    prefix_in = entering(
        (whole_decay, local_state, first_seg, last_seg), "seq", join_forward, identity
    )
    carried = (prefix_in[3][0] == first_seg[0]).astype(jnp.float32)
    start_state = carried * prefix_in[1]
    from_state = jnp.einsum("tn,hpn->thp", c_rows, start_state, precision=highest)
    y_ssd = y_inner + entry_decay[:, :, None] * from_state
    normed_out = gated_finish(y_ssd, x_heads, z_gate, d_skip, gate_full.astype(jnp.float32))
    out_low = normed_out.astype(jnp.bfloat16)
    block_out = (jnp.dot(out_low, w_out_full, preferred_element_type=jnp.float32) + tokens).astype(
        jnp.bfloat16
    )
    back_weights = (
        lax.all_gather(shards[0], ("dp", "seq"), axis=0, tiled=True),
        lax.all_gather(shards[1], ("dp", "seq"), axis=0, tiled=True),
        lax.all_gather(shards[2], ("dp", "seq"), axis=1, tiled=True),
        lax.all_gather(shards[3], ("dp", "seq"), axis=0, tiled=True),
        lax.all_gather(shards[4], ("dp", "seq"), axis=0, tiled=True),
        lax.all_gather(shards[5], ("dp", "seq"), axis=0, tiled=True),
    )
    gain_back, w_in_back, conv_back, bias_back, gate_back, w_out_back = back_weights
    cotangent = grad_out[0]
    d_normed = jnp.dot(cotangent, w_out_back.T, preferred_element_type=jnp.float32)
    grad_w_out = jnp.dot(out_low.T, cotangent, preferred_element_type=jnp.float32)
    primals = (
        xbc_ext,
        z_gate,
        dt_raw,
        conv_back.astype(jnp.float32),
        bias_back.astype(jnp.float32),
        dt_bias,
        a_log,
        d_skip,
        gate_back.astype(jnp.float32),
        start_state,
    )
    outputs, pullback = jax.vjp(partial(local_branch, segment=segment), *primals)
    own_pull = pullback((d_normed, jnp.zeros_like(outputs[1])))[9]
    outgoing = (carried * whole_decay, carried * own_pull)
    later_grads = entering_2(
        outgoing, "seq", join_backward, (jnp.ones_like(whole_decay), jnp.zeros_like(local_state))
    )
    gradients = pullback((d_normed, later_grads[1]))
    rim_back = passed_along(gradients[0][: CONV - 1].astype(jnp.bfloat16), "seq", -1).astype(
        jnp.float32
    )
    d_conv_own = gradients[0][CONV - 1 :]
    split_at = d_conv_own.shape[0] - (CONV - 1)
    d_conv_in = jnp.concatenate([d_conv_own[:split_at], d_conv_own[split_at:] + rim_back], axis=0)
    d_projected = jnp.concatenate([gradients[1], d_conv_in, gradients[2]], axis=1).astype(
        jnp.bfloat16
    )
    grad_w_in = jnp.dot(normed_low.T, d_projected, preferred_element_type=jnp.float32)
    d_normed_in = jnp.dot(d_projected, w_in_back.T, preferred_element_type=jnp.float32)
    normed_again, norm_pull = jax.vjp(norm_in, tokens, gain_back.astype(jnp.float32))
    d_tokens, d_pre_gain = norm_pull(d_normed_in)
    grad_hidden = (cotangent.astype(jnp.float32) + d_tokens).astype(jnp.bfloat16)
    summed = (
        lax.psum_scatter(grad_w_in, ("dp", "seq"), scatter_dimension=0, tiled=True),
        lax.psum_scatter(grad_w_out, ("dp", "seq"), scatter_dimension=0, tiled=True),
        lax.psum_scatter(gradients[3], ("dp", "seq"), scatter_dimension=1, tiled=True),
        lax.psum_scatter(gradients[4], ("dp", "seq"), scatter_dimension=0, tiled=True),
        lax.psum_scatter(d_pre_gain, ("dp", "seq"), scatter_dimension=0, tiled=True),
        lax.psum_scatter(gradients[8], ("dp", "seq"), scatter_dimension=0, tiled=True),
    )
    head_sums = lax.psum((gradients[5], gradients[6], gradients[7]), ("dp", "seq"))
    return (
        block_out[None],
        grad_hidden[None],
        summed[4],
        summed[0],
        summed[2],
        summed[3],
        head_sums[0],
        head_sums[1],
        head_sums[2],
        summed[5],
        summed[1],
    )


def solution(mesh):
    placed = (
        P("dp", "seq", None),
        P("dp", "seq"),
        P(("dp", "seq")),
        P(("dp", "seq"), None),
        P(None, ("dp", "seq")),
        P(("dp", "seq")),
        P(),
        P(),
        P(),
        P(("dp", "seq")),
        P(("dp", "seq"), None),
        P("dp", "seq", None),
    )
    return jax.shard_map(
        local,
        mesh=mesh,
        in_specs=placed,
        out_specs=(
            P("dp", "seq", None),
            P("dp", "seq", None),
            P(("dp", "seq")),
            P(("dp", "seq"), None),
            P(None, ("dp", "seq")),
            P(("dp", "seq")),
            P(),
            P(),
            P(),
            P(("dp", "seq")),
            P(("dp", "seq"), None),
        ),
        check_vma=False,
    )
```

profile of v0, /device:TPU:0, one launch (start us, length us, event | category | flops | bytes accessed | tf_op | source)
XLA Modules:
  0.0 1673.3 jit_solution(5633449149458289180)
XLA Ops:
  13.8 69.5 %all-reduce.25 = (bf16[1536]{0:T(1024)(128)(2,1)S(1)}, bf16[3328]{0:T(1024)(128)(2,1)S(1)}, bf16[3072]{0:T(1024)(128)(2,1)}) all-reduce(bf16[1536]{0:T(1024)(128)(2,1)S(1)} %dynamic-update-slice.1, bf16[3328]{0:T(1024)(128)(2,1)S(1)} %dynamic-update-slice, ...), channel_id=1, replica_groups=mesh['dp'=8,'seq'=16] {'dp','seq'}, use_global_device_ids=true, to_apply=%add.14 | all-reduce | flops 7936 | bytes 31744
  83.3 53.8 %all-gather.3 = bf16[128,26,4]{1,2,0:T(4,128)(2,1)S(1)} all-gather(bf16[1,26,4]{1,2,0:T(4,128)(2,1)} %bitcast.168), channel_id=1, replica_groups=mesh['dp'=8,'seq'=16] {'dp','seq'}, dimensions={0}, use_global_device_ids=true | all-gather | bytes 26832 | tf_op jit(solution)/shard_map/all_gather | solution.py:184
  140.3 29.4 %reshape.310 = bf16[1536,6448]{1,0:T(8,128)(2,1)} reshape(bf16[128,12,6448]{2,1,0:T(8,128)(2,1)} %all-gather.18.cloned.1.call-done) | data formatting | bytes 39616512
  199.8 40.0 %all-reduce.26 = (bf16[16]{0:T(256)(128)(2,1)}, bf16[16]{0:T(256)(128)(2,1)}) all-reduce(bf16[16]{0:T(256)(128)(2,1)S(1)} %dynamic-update-slice.2, bf16[16]{0:T(256)(128)(2,1)S(1)} %dynamic-update-slice.3), channel_id=3, replica_groups=mesh['dp'=8,'seq'=16] {'seq'}, use_global_device_ids=true, to_apply=%add.15 | all-reduce | flops 32 | bytes 128
  241.6 17.0 %all-gather.5 = bf16[16,1,48]{2,1,0:T(2,128)(2,1)S(1)} all-gather(bf16[1,1,48]{2,1,0:T(2,128)(2,1)} %get-tuple-element.246), channel_id=1, replica_groups=mesh['dp'=8,'seq'=16] {'seq'}, dimensions={0}, use_global_device_ids=true | all-gather | bytes 1632 | tf_op jit(solution)/shard_map/all_gather | solution.py:29
  263.0 21.8 %all-gather.14.cloned.1.call-done = bf16[768,64,128]{2,1,0:T(8,128)(2,1)} async-done(((bf16[48,64,128]{2,1,0:T(8,128)(2,1)}), bf16[768,64,128]{2,1,0:T(8,128)(2,1)}) %all-gather.14.cloned.1.call-update) | async-done | bytes 12582928 | tf_op jit(solution)/shard_map/all_gather | solution.py:29
  302.6 55.6 %all-gather.12.cloned.1.call-done = bf16[3072,1536]{1,0:T(8,128)(2,1)} async-done(((bf16[24,1536]{1,0:T(8,128)(2,1)}), bf16[3072,1536]{1,0:T(8,128)(2,1)}) %all-gather.12.cloned.1.call-update) | async-done | bytes 9437200 | tf_op jit(solution)/shard_map/all_gather | solution.py:187
  377.7 54.2 %all-gather.6 = bf16[16,1,48]{2,1,0:T(2,128)(2,1)S(1)} all-gather(bf16[1,1,48]{2,1,0:T(2,128)(2,1)S(1)} %convert_bitcast_fusion), channel_id=1, replica_groups=mesh['dp'=8,'seq'=16] {'seq'}, dimensions={0}, use_global_device_ids=true | all-gather | bytes 1632 | tf_op jit(solution)/shard_map/all_gather | solution.py:53
  459.5 43.2 %all-gather.16.cloned.1.call-done = bf16[768,64,128]{2,1,0:T(8,128)(2,1)} async-done(((bf16[48,64,128]{2,1,0:T(8,128)(2,1)}), bf16[768,64,128]{2,1,0:T(8,128)(2,1)}) %all-gather.16.cloned.1.call-update) | async-done | bytes 12582928 | tf_op jit(solution)/shard_map/all_gather | solution.py:53
  504.0 56.0 %while.30 = (s32[]{:T(128)}, f32[48,64,128]{2,1,0:T(8,128)}, s32[]{:T(128)}, bf16[16,48,64,128]{3,2,1,0:T(8,128)(2,1)}, bf16[16,48]{1,0:T(8,128)(2,1)}, /*index=5*/s32[]{:T(128)}, s32[]{:T(128)}, s32[]{:T(128)}, s32[]{:T(128)}) while((s32[]{:T(128)}, f32[48,64,128]{2,1,0:T(8,128)}, s32[]{:T(128)}, bf16[16,48,64,128]{3,2,1,0:T(8,128)(2,1)}, ...), condition=%wide.region_8.9_spmd, body=%wide.region_7.8_spmd.sunk | while | flops 1179702 | bytes 3932795 | solution.py:70
  596.1 11.5 fusion.65
  615.7 17.1 %fusion.83 = f32[1536,6448]{1,0:T(8,128)} fusion(bf16[128,48]{1,0:T(8,128)(2,1)S(1)} %get-tuple-element.226, bf16[3,3328]{1,0:T(4,128)(2,1)S(1)} %fusion.105, bf16[125,3328]{1,0:T(8,128)(2,1)} %copy-done.16, bf16[128,3072]{1,0:T(8,128)(2,1)} %get-tuple-element.236, bf16[1,128,1536]{2,1,0:T(8,128)(2,1)S(1)} %copy-done.12, ...), kind=kOutput, calls=%fused_computation.118 | convolution fusion | flops 2542845952 | bytes 41667072 | tf_op jit(solution)/shard_map/dot_general | solution.py:268
  632.8 598.8 %fusion = f32[16,6448]{1,0:T(8,128)S(1)} fusion(f32[1536,6448]{1,0:T(8,128)} %fusion.83), kind=kCustom, calls=%all-reduce-scatter | all-reduce-scatter fusion | flops 13205505 | bytes 40029184
  1243.8 34.1 %collective-permute-done.33 = f32[12,6448]{1,0:T(8,128)S(1)} collective-permute-done((f32[12,6448]{1,0:T(8,128)S(1)}, f32[12,6448]{1,0:T(8,128)S(1)}, u32[]{:S(2)}, u32[]{:S(2)}) %collective-permute-start.33) | collective-permute-done | bytes 309536
  1303.3 17.7 %collective-permute-start.22 = (f32[16,6448]{1,0:T(8,128)S(1)}, f32[16,6448]{1,0:T(8,128)S(1)}, u32[]{:S(2)}, u32[]{:S(2)}) collective-permute-start(f32[16,6448]{1,0:T(8,128)S(1)} %fusion), channel_id=1, source_target_pairs={{0,21},{1,22},{2,23},{3,24},{4,25},{5,26},{6,27},{7,28},{8,29},{9,... | collective-permute-start | bytes 1238024
  1322.3 13.3 collective-permute-done.25
  1335.6 17.6 %collective-permute-start.20 = (f32[16,6448]{1,0:T(8,128)S(1)}, f32[16,6448]{1,0:T(8,128)S(1)}, u32[]{:S(2)}, u32[]{:S(2)}) collective-permute-start(f32[16,6448]{1,0:T(8,128)S(1)} %fusion), channel_id=1, source_target_pairs={{0,19},{1,20},{2,21},{3,22},{4,23},{5,24},{6,25},{7,26},{8,27},{9,... | collective-permute-start | bytes 1238024
  1354.6 13.7 collective-permute-start.18
  1393.9 18.3 %collective-permute-start.11 = (f32[16,6448]{1,0:T(8,128)S(1)}, f32[16,6448]{1,0:T(8,128)S(1)}, u32[]{:S(2)}, u32[]{:S(2)}) collective-permute-start(f32[16,6448]{1,0:T(8,128)S(1)} %fusion), channel_id=1, source_target_pairs={{0,10},{1,11},{2,12},{3,13},{4,14},{5,15},{6,16},{7,17},{8,18},{9,... | collective-permute-start | bytes 1238024
  1424.5 17.9 %collective-permute-start.7 = (f32[16,6448]{1,0:T(8,128)S(1)}, f32[16,6448]{1,0:T(8,128)S(1)}, u32[]{:S(2)}, u32[]{:S(2)}) collective-permute-start(f32[16,6448]{1,0:T(8,128)S(1)} %fusion), channel_id=1, source_target_pairs={{0,6},{1,7},{2,8},{3,9},{4,10},{5,11},{6,12},{7,13},{8,14},{9,15},... | collective-permute-start | bytes 1238024
  1448.5 20.7 %collective-permute-start.6 = (f32[16,6448]{1,0:T(8,128)S(1)}, f32[16,6448]{1,0:T(8,128)}, u32[]{:S(2)}, u32[]{:S(2)}) collective-permute-start(f32[16,6448]{1,0:T(8,128)S(1)} %fusion), channel_id=1, source_target_pairs={{0,5},{1,6},{2,7},{3,8},{4,9},{5,10},{6,11},{7,12},{8,13},{9,14},{... | collective-permute-start | bytes 1238024
  1479.7 25.2 %collective-permute-start.3 = (f32[16,6448]{1,0:T(8,128)S(1)}, f32[16,6448]{1,0:T(8,128)}, u32[]{:S(2)}, u32[]{:S(2)}) collective-permute-start(f32[16,6448]{1,0:T(8,128)S(1)} %fusion), channel_id=1, source_target_pairs={{0,2},{1,3},{2,4},{3,5},{4,6},{5,7},{6,8},{7,9},{8,10},{9,11},{10,... | collective-permute-start | bytes 1238024
  1504.9 10.2 collective-permute-start.2
  1523.3 139.3 %concatenate.14 = f32[524,6448]{1,0:T(8,128)} concatenate(f32[12,6448]{1,0:T(8,128)S(1)} %copy-done.23, f32[16,6448]{1,0:T(8,128)S(1)} %copy-done.21, f32[16,6448]{1,0:T(8,128)S(1)} %copy-done.25, f32[16,6448]{1,0:T(8,128)S(1)} %copy-done.27, f32[16,6448]{1,0:T(8,128)} %copy-done.28, f32[16,6448]{1,0:T(8,128)} %copy-done.29, f32[16,6448]{1,0:T(8,128)} %copy-done.30, ...), dimensions={0} | concatenate | bytes 27030016
  (383 shorter events, 314.6 us)
Async XLA Ops:
  7.2 133.1 %all-gather.18.cloned.1.call-start = ((), (), s32[]{:S(2)}) async-start(), calls=%async_computation.5 | async-start | bytes 26947584 | tf_op jit(solution)/shard_map/all_gather | solution.py:183
  7.9 276.9 %all-gather.14.cloned.1.call-start = ((), (), s32[]{:S(2)}) async-start(), calls=%async_computation.3 | async-start | bytes 13369344 | tf_op jit(solution)/shard_map/all_gather | solution.py:29
  194.5 163.7 %all-gather.12.cloned.1.call-start = ((), (), s32[]{:S(2)}) async-start(), calls=%async_computation.1 | async-start | bytes 9510912 | tf_op jit(solution)/shard_map/all_gather | solution.py:187
  195.2 307.4 %all-gather.16.cloned.1.call-start = ((), (), s32[]{:S(2)}) async-start(), calls=%async_computation.4 | async-start | bytes 13369344 | tf_op jit(solution)/shard_map/all_gather | solution.py:53
  377.7 1138.5 %all-reduce.29.cloned.1.call-start = ((), (), s32[]{:S(2)}) async-start(), calls=%async_computation.6 | async-start | bytes 183296
  607.7 1056.8 %reduce-scatter.5.cloned.1.call-start = ((), (), s32[]{:S(2)}) async-start(), calls=%async_computation.2 | async-start | bytes 19021824 | tf_op jit(solution)/shard_map/reduce_scatter | solution.py:275
  1231.6 50.6 %collective-permute-start.32 = (f32[16,6448]{1,0:T(8,128)S(1)}, f32[16,6448]{1,0:T(8,128)S(1)}, u32[]{:S(2)}, u32[]{:S(2)}) collective-permute-start(f32[16,6448]{1,0:T(8,128)S(1)} %fusion), channel_id=1, source_target_pairs={{0,31},{1,32},{2,33},{3,34},{4,35},{5,36},{6,37},{7,38},{8,39},{9,... | collective-permute-start | bytes 1238024
  1233.0 44.9 %collective-permute-start.33 = (f32[12,6448]{1,0:T(8,128)S(1)}, f32[12,6448]{1,0:T(8,128)S(1)}, u32[]{:S(2)}, u32[]{:S(2)}) collective-permute-start(f32[12,6448]{1,0:T(8,128)S(1)} %slice.133), channel_id=1, source_target_pairs={{0,32},{1,33},{2,34},{3,35},{4,36},{5,37},{6,38},{7,39},{8,40},{9,... | collective-permute-start | bytes 928520
  1234.3 50.1 %collective-permute-start.31 = (f32[16,6448]{1,0:T(8,128)S(1)}, f32[16,6448]{1,0:T(8,128)S(1)}, u32[]{:S(2)}, u32[]{:S(2)}) collective-permute-start(f32[16,6448]{1,0:T(8,128)S(1)} %fusion), channel_id=1, source_target_pairs={{0,30},{1,31},{2,32},{3,33},{4,34},{5,35},{6,36},{7,37},{8,38},{9,... | collective-permute-start | bytes 1238024
  1238.0 50.6 %collective-permute-start.30 = (f32[16,6448]{1,0:T(8,128)S(1)}, f32[16,6448]{1,0:T(8,128)S(1)}, u32[]{:S(2)}, u32[]{:S(2)}) collective-permute-start(f32[16,6448]{1,0:T(8,128)S(1)} %fusion), channel_id=1, source_target_pairs={{0,29},{1,30},{2,31},{3,32},{4,33},{5,34},{6,35},{7,36},{8,37},{9,... | collective-permute-start | bytes 1238024
  1241.6 54.0 %collective-permute-start.29 = (f32[16,6448]{1,0:T(8,128)S(1)}, f32[16,6448]{1,0:T(8,128)S(1)}, u32[]{:S(2)}, u32[]{:S(2)}) collective-permute-start(f32[16,6448]{1,0:T(8,128)S(1)} %fusion), channel_id=1, source_target_pairs={{0,28},{1,29},{2,30},{3,31},{4,32},{5,33},{6,34},{7,35},{8,36},{9,... | collective-permute-start | bytes 1238024
  1288.6 47.0 %collective-permute-start.25 = (f32[16,6448]{1,0:T(8,128)S(1)}, f32[16,6448]{1,0:T(8,128)S(1)}, u32[]{:S(2)}, u32[]{:S(2)}) collective-permute-start(f32[16,6448]{1,0:T(8,128)S(1)} %fusion), channel_id=1, source_target_pairs={{0,24},{1,25},{2,26},{3,27},{4,28},{5,29},{6,30},{7,31},{8,32},{9,... | collective-permute-start | bytes 1238024
  1295.6 57.6 %collective-permute-start.24 = (f32[16,6448]{1,0:T(8,128)S(1)}, f32[16,6448]{1,0:T(8,128)S(1)}, u32[]{:S(2)}, u32[]{:S(2)}) collective-permute-start(f32[16,6448]{1,0:T(8,128)S(1)} %fusion), channel_id=1, source_target_pairs={{0,23},{1,24},{2,25},{3,26},{4,27},{5,28},{6,29},{7,30},{8,31},{9,... | collective-permute-start | bytes 1238024
  1300.4 54.2 %collective-permute-start.23 = (f32[16,6448]{1,0:T(8,128)S(1)}, f32[16,6448]{1,0:T(8,128)S(1)}, u32[]{:S(2)}, u32[]{:S(2)}) collective-permute-start(f32[16,6448]{1,0:T(8,128)S(1)} %fusion), channel_id=1, source_target_pairs={{0,22},{1,23},{2,24},{3,25},{4,26},{5,27},{6,28},{7,29},{8,30},{9,... | collective-permute-start | bytes 1238024
  1303.3 65.0 %collective-permute-start.22 = (f32[16,6448]{1,0:T(8,128)S(1)}, f32[16,6448]{1,0:T(8,128)S(1)}, u32[]{:S(2)}, u32[]{:S(2)}) collective-permute-start(f32[16,6448]{1,0:T(8,128)S(1)} %fusion), channel_id=1, source_target_pairs={{0,21},{1,22},{2,23},{3,24},{4,25},{5,26},{6,27},{7,28},{8,29},{9,... | collective-permute-start | bytes 1238024
  1321.0 49.0 %collective-permute-start.21 = (f32[16,6448]{1,0:T(8,128)S(1)}, f32[16,6448]{1,0:T(8,128)S(1)}, u32[]{:S(2)}, u32[]{:S(2)}) collective-permute-start(f32[16,6448]{1,0:T(8,128)S(1)} %fusion), channel_id=1, source_target_pairs={{0,20},{1,21},{2,22},{3,23},{4,24},{5,25},{6,26},{7,27},{8,28},{9,... | collective-permute-start | bytes 1238024
  1393.9 54.6 %collective-permute-start.11 = (f32[16,6448]{1,0:T(8,128)S(1)}, f32[16,6448]{1,0:T(8,128)S(1)}, u32[]{:S(2)}, u32[]{:S(2)}) collective-permute-start(f32[16,6448]{1,0:T(8,128)S(1)} %fusion), channel_id=1, source_target_pairs={{0,10},{1,11},{2,12},{3,13},{4,14},{5,15},{6,16},{7,17},{8,18},{9,... | collective-permute-start | bytes 1238024
  1412.2 57.1 %collective-permute-start.10 = (f32[16,6448]{1,0:T(8,128)S(1)}, f32[16,6448]{1,0:T(8,128)S(1)}, u32[]{:S(2)}, u32[]{:S(2)}) collective-permute-start(f32[16,6448]{1,0:T(8,128)S(1)} %fusion), channel_id=1, source_target_pairs={{0,9},{1,10},{2,11},{3,12},{4,13},{5,14},{6,15},{7,16},{8,17},{9,1... | collective-permute-start | bytes 1238024
  1414.1 61.1 %collective-permute-start.9 = (f32[16,6448]{1,0:T(8,128)S(1)}, f32[16,6448]{1,0:T(8,128)S(1)}, u32[]{:S(2)}, u32[]{:S(2)}) collective-permute-start(f32[16,6448]{1,0:T(8,128)S(1)} %fusion), channel_id=1, source_target_pairs={{0,8},{1,9},{2,10},{3,11},{4,12},{5,13},{6,14},{7,15},{8,16},{9,17... | collective-permute-start | bytes 1238024
  1418.5 61.2 %collective-permute-start.8 = (f32[16,6448]{1,0:T(8,128)S(1)}, f32[16,6448]{1,0:T(8,128)S(1)}, u32[]{:S(2)}, u32[]{:S(2)}) collective-permute-start(f32[16,6448]{1,0:T(8,128)S(1)} %fusion), channel_id=1, source_target_pairs={{0,7},{1,8},{2,9},{3,10},{4,11},{5,12},{6,13},{7,14},{8,15},{9,16}... | collective-permute-start | bytes 1238024
  1424.5 80.4 %collective-permute-start.7 = (f32[16,6448]{1,0:T(8,128)S(1)}, f32[16,6448]{1,0:T(8,128)S(1)}, u32[]{:S(2)}, u32[]{:S(2)}) collective-permute-start(f32[16,6448]{1,0:T(8,128)S(1)} %fusion), channel_id=1, source_target_pairs={{0,6},{1,7},{2,8},{3,9},{4,10},{5,11},{6,12},{7,13},{8,14},{9,15},... | collective-permute-start | bytes 1238024
  1448.5 72.8 %collective-permute-start.6 = (f32[16,6448]{1,0:T(8,128)S(1)}, f32[16,6448]{1,0:T(8,128)}, u32[]{:S(2)}, u32[]{:S(2)}) collective-permute-start(f32[16,6448]{1,0:T(8,128)S(1)} %fusion), channel_id=1, source_target_pairs={{0,5},{1,6},{2,7},{3,8},{4,9},{5,10},{6,11},{7,12},{8,13},{9,14},{... | collective-permute-start | bytes 1238024
  1469.3 52.1 %collective-permute-start.5 = (f32[16,6448]{1,0:T(8,128)S(1)}, f32[16,6448]{1,0:T(8,128)}, u32[]{:S(2)}, u32[]{:S(2)}) collective-permute-start(f32[16,6448]{1,0:T(8,128)S(1)} %fusion), channel_id=1, source_target_pairs={{0,4},{1,5},{2,6},{3,7},{4,8},{5,9},{6,10},{7,11},{8,12},{9,13},{1... | collective-permute-start | bytes 1238024
  1475.2 46.2 %collective-permute-start.4 = (f32[16,6448]{1,0:T(8,128)S(1)}, f32[16,6448]{1,0:T(8,128)}, u32[]{:S(2)}, u32[]{:S(2)}) collective-permute-start(f32[16,6448]{1,0:T(8,128)S(1)} %fusion), channel_id=1, source_target_pairs={{0,3},{1,4},{2,5},{3,6},{4,7},{5,8},{6,9},{7,10},{8,11},{9,12},{10... | collective-permute-start | bytes 1238024
  (103 other events, 3950.6 us)
Sparse Core Ops, SparseCore 0:
  11.0 99.0 all-gather.17
  194.6 90.1 all-gather.13
  287.7 70.4 all-gather.11
  377.8 124.8 all-gather.15
  607.8 788.6 all-reduce.28
  1403.1 240.5 reduce-scatter.4
where the time goes:
time: 1700 us; the launch traced here: 1670 us
  blocking collectives  833 us (49%)
  starting transfers between devices  231 us (14%)
  local copies, waits for them, and re-layouts  215 us (13%)
  waiting for transfers between devices  174 us (10%)
  matrix products  107 us (6%)
  other arithmetic  94.7 us (6%)
  between operations  18.7 us (1%)
    unnamed x3, blocking collectives  708 us
    unnamed x33, starting transfers between devices  227 us
    unnamed x198, local copies, waits for them, and re-layouts  186 us
    all_gather x1, waiting for transfers between devices, local(): lax.all_gather(shards[5], ('dp', 'seq'), axis=0, tiled=True)  55.6 us
    all_gather x1, blocking collectives, entering_2(): lax.all_gather(a.astype(kind), axis)  54.2 us
    all_gather x1, blocking collectives, local(): lax.all_gather(shards[2], ('dp', 'seq'), axis=1, tiled=True)  53.8 us
    unnamed x39, waiting for transfers between devices  53.3 us
    add x15, other arithmetic, join_backward(): late_grad + late_decay[:, None, None] * early_grad  45.6 us
  transfers between devices with their start and end apart: 40, of which 7 were waited for; matrix products, arithmetic and copies ran while one was open for 51% of the time, Pallas kernels for 0%

commit v1 on v0

v1 whole, which is shorter than its diff:
```python
import jax
import jax.numpy as jnp
from jax import lax
from jax.experimental import pallas as pl
from jax.experimental.pallas import tpu as pltpu
from jax.sharding import PartitionSpec as P

D = 1536
INNER = 3072
STATE = 128
CONV = 4
HEADS = 48
CONV_CH = 3328
CHUNK = 128
OWN = 3
WIDE = 192
PAD = 768
low = jnp.bfloat16
f32 = jnp.float32


def mm(a, b, dims=((1,), (0,))):
    return lax.dot_general(a, b, (dims, ((), ())), preferred_element_type=f32)


NT = ((1,), (1,))
TN = ((0,), (0,))


def per_head(parts):
    lane = lax.broadcasted_iota(jnp.int32, (1, WIDE), 1)
    return jnp.where(lane < 64, parts[0], jnp.where(lane < 128, parts[1], parts[2]))


def stacked(a):
    lane = lax.broadcasted_iota(jnp.int32, a.shape, 1)
    zero = jnp.zeros_like(a)
    return jnp.concatenate(
        [jnp.where((lane >= 64 * h) & (lane < 64 * h + 64), a, zero) for h in range(OWN)], axis=0
    )


def running(a, back):
    lane = lax.broadcasted_iota(jnp.int32, a.shape, 1)
    step = 1
    while step < CHUNK:
        if back:
            a = a + jnp.where(lane < CHUNK - step, pltpu.roll(a, CHUNK - step, 1), 0.0)
        else:
            a = a + jnp.where(lane >= step, pltpu.roll(a, step, 1), 0.0)
        step *= 2
    return a


def chunk_terms(zdt, rows, head_ref):
    raw = zdt[:, 128:256].T[64:72]
    v = raw + head_ref[0]
    ea = jnp.exp(head_ref[1])
    step = jnp.maximum(v, 0.0) + jnp.log1p(jnp.exp(-jnp.abs(v)))
    ld = -step * ea
    cum = running(ld, False)
    total = cum[:, CHUNK - 1 : CHUNK]
    seg = rows[0:1]
    before = rows[1:2, 0:1]
    last = seg[:, CHUNK - 1 : CHUNK]
    entry = jnp.exp(cum) * (seg == before).astype(f32)
    to_end = jnp.exp(total - cum) * (seg == last).astype(f32)
    whole = jnp.exp(total) * (last == before).astype(f32)
    pack = jnp.concatenate(
        [cum, entry, to_end * step, rows, jnp.zeros((CHUNK - 32, CHUNK), f32)], axis=0
    )
    cols = pack.T
    t = lax.broadcasted_iota(jnp.int32, (CHUNK, CHUNK), 0)
    s = lax.broadcasted_iota(jnp.int32, (CHUNK, CHUNK), 1)
    barred = jnp.where((t >= s) & (cols[:, 24:25] == seg), 0.0, -1e30)
    return v, ea, step, ld, cum, to_end, whole, cols, barred


def convolved(ext_ref, conv_ref):
    pre = conv_ref[CONV : CONV + 1, :]
    for k in range(CONV):
        pre = pre + conv_ref[k : k + 1, :] * ext_ref[pl.ds(5 + k, CHUNK), :]
    return pre


def decays(cols, cum, barred, h):
    return jnp.exp(cols[:, h : h + 1] - cum[h : h + 1] + barred)


def forward_kernel(
    proj_ref, rows_ref, conv_ref, head_ref, skip_ref, y_ref, gated_ref, kept_ref, ext_ref, state_ref
):
    first = pl.program_id(0) == 0

    @pl.when(first)
    def _():
        ext_ref[0:8, :] = jnp.zeros((8, 512), f32)
        state_ref[...] = jnp.zeros_like(state_ref)

    @pl.when(jnp.logical_not(first))
    def _():
        ext_ref[0:8, :] = ext_ref[CHUNK : CHUNK + 8, :]

    ext_ref[8 : CHUNK + 8, :] = proj_ref[:, 256:PAD].astype(f32)
    zdt = proj_ref[:, 0:256].astype(f32)
    pre = convolved(ext_ref, conv_ref)
    act = pre * jax.nn.sigmoid(pre)
    x = act[:, :WIDE]
    b_low = act[:, 256:384].astype(low)
    c_low = act[:, 384:512].astype(low)
    v, ea, step, ld, cum, to_end, whole, cols, barred = chunk_terms(zdt, rows_ref[...], head_ref)
    scores = mm(c_low, b_low, NT)
    mixing = jnp.concatenate(
        [
            (scores * decays(cols, cum, barred, h) * step[h : h + 1]).astype(low)
            for h in range(OWN)
        ],
        axis=1,
    )
    state = state_ref[...]
    kept_ref[0] = state
    entry = per_head([cols[:, 8 + h : 9 + h] for h in range(OWN)])
    y = mm(mixing, stacked(x.astype(low))) + entry * mm(c_low, state.astype(low))
    leaving = per_head([cols[:, 16 + h : 17 + h] for h in range(OWN)])
    state_ref[...] = per_head([whole[h : h + 1] for h in range(OWN)]) * state + mm(
        b_low, (leaving * x).astype(low), TN
    )
    y = y + skip_ref[...] * x
    z = zdt[:, :WIDE]
    y_ref[...] = y
    gated_ref[...] = (y * z * jax.nn.sigmoid(z)).astype(low)


def backward_kernel(
    proj_ref,
    before_ref,
    rows_ref,
    conv_ref,
    head_ref,
    skip_ref,
    y_ref,
    u_ref,
    kept_ref,
    d_proj_ref,
    conv_grad_ref,
    head_grad_ref,
    skip_grad_ref,
    ext_ref,
    later_ref,
    state_ref,
):
    step_id = pl.program_id(0)
    count = pl.num_programs(0)

    @pl.when(step_id == 0)
    def _():
        later_ref[CHUNK : CHUNK + 8, :] = jnp.zeros((8, 512), f32)
        state_ref[...] = jnp.zeros_like(state_ref)
        conv_grad_ref[...] = jnp.zeros_like(conv_grad_ref)
        head_grad_ref[...] = jnp.zeros_like(head_grad_ref)
        skip_grad_ref[...] = jnp.zeros_like(skip_grad_ref)

    @pl.when(step_id > 0)
    def _():
        later_ref[CHUNK : CHUNK + 8, :] = later_ref[0:8, :]

    ahead = before_ref[8:16, 256:PAD].astype(f32)
    ext_ref[0:8, :] = jnp.where(step_id == count - 1, 0.0, ahead)
    conv_in = proj_ref[:, 256:PAD].astype(f32)
    ext_ref[8 : CHUNK + 8, :] = conv_in
    zdt = proj_ref[:, 0:256].astype(f32)
    pre = convolved(ext_ref, conv_ref)
    sig = jax.nn.sigmoid(pre)
    act = pre * sig
    slope = sig * (1.0 + pre * (1.0 - sig))
    x = act[:, :WIDE]
    x_low = x.astype(low)
    b_low = act[:, 256:384].astype(low)
    c_low = act[:, 384:512].astype(low)
    v, ea, step, ld, cum, to_end, whole, cols, barred = chunk_terms(zdt, rows_ref[...], head_ref)
    scores = mm(c_low, b_low, NT)

    z = zdt[:, :WIDE]
    z_sig = jax.nn.sigmoid(z)
    z_act = z * z_sig
    y = y_ref[...]
    d_gated = cols[:, 26:27] * u_ref[...] - cols[:, 27:28] * (y * z_act)
    dy = d_gated * z_act
    dz = d_gated * y * (z_sig * (1.0 + z * (1.0 - z_sig)))
    dy_low = dy.astype(low)

    state = kept_ref[0]
    state_low = state.astype(low)
    later = state_ref[...]
    later_low = later.astype(low)
    entry = per_head([cols[:, 8 + h : 9 + h] for h in range(OWN)])
    leaving = per_head([cols[:, 16 + h : 17 + h] for h in range(OWN)])
    wholes = per_head([whole[h : h + 1] for h in range(OWN)])

    x_stack = stacked(x_low)
    d_mixing = mm(dy_low, x_stack, NT)
    d_scores = jnp.zeros((CHUNK, CHUNK), f32)
    mixings = []
    flows = []
    d_steps = []
    for h in range(OWN):
        decay = decays(cols, cum, barred, h)
        stepped = decay * step[h : h + 1]
        mixing = scores * stepped
        mixings.append(mixing.astype(low))
        part = d_mixing[:, CHUNK * h : CHUNK * h + CHUNK]
        d_scores = d_scores + part * stepped
        flows.append((part * mixing).astype(low))
        d_steps.append(jnp.sum(part * scores * decay, axis=0, keepdims=True))
    d_scores = d_scores.astype(low)

    t = lax.broadcasted_iota(jnp.int32, (CHUNK, CHUNK), 0)
    s = lax.broadcasted_iota(jnp.int32, (CHUNK, CHUNK), 1)
    earlier = (t < s).astype(low)
    reach = mm(jnp.concatenate(flows, axis=0), earlier)
    inside = [
        jnp.sum(
            jnp.where(t >= s, reach[CHUNK * h : CHUNK * h + CHUNK], 0.0), axis=0, keepdims=True
        )
        for h in range(OWN)
    ]
    blank = jnp.zeros((8 - OWN, CHUNK), f32)

    from_later = mm(b_low, later_low)
    dx = (
        mm(jnp.concatenate(mixings, axis=0), stacked(dy_low), TN)
        + leaving * from_later
        + skip_ref[...] * dy
    )
    dy_entry = entry * dy
    dy_entry_low = dy_entry.astype(low)
    x_leaving = (leaving * x).astype(low)
    dc = mm(d_scores, b_low) + mm(dy_entry_low, state_low, NT)
    db = mm(d_scores, c_low, TN) + mm(x_leaving, later_low, NT)

    row_head = lax.broadcasted_iota(jnp.int32, (8, WIDE), 0)
    lane = lax.broadcasted_iota(jnp.int32, (8, WIDE), 1)
    by_head = ((lane >= 64 * row_head) & (lane < 64 * row_head + 64)).astype(low)
    xv = mm(by_head, (x * from_later).astype(low), NT)
    row_state = mm(by_head, (dy_entry * mm(c_low, state_low)).astype(low), NT)
    overlap = jnp.sum(mm(by_head, (later * state).astype(low), NT), axis=1, keepdims=True)
    ended = to_end * xv
    col_state = ended * step
    d_step = jnp.concatenate(d_steps + [blank], axis=0) + ended
    d_ld = (
        jnp.concatenate(inside + [blank], axis=0)
        + running(row_state, True)
        + (running(col_state, False) - col_state)
        + whole * overlap
    )
    d_dt = (d_step - d_ld * ea) * jax.nn.sigmoid(v)
    head_grad_ref[0] += d_dt
    head_grad_ref[1] += d_ld * ld
    skip_grad_ref[...] += jnp.sum((dy * x).reshape(16, 8, WIDE), axis=0)
    state_ref[...] = wholes * later + mm(c_low, dy_entry_low, TN)

    later_ref[0:CHUNK, 0:WIDE] = dx * slope[:, :WIDE]
    later_ref[0:CHUNK, WIDE:256] = jnp.zeros((CHUNK, 256 - WIDE), f32)
    later_ref[0:CHUNK, 256:384] = db * slope[:, 256:384]
    later_ref[0:CHUNK, 384:512] = dc * slope[:, 384:512]
    d_conv_in = jnp.zeros((CHUNK, 512), f32)
    for k in range(CONV):
        moved = later_ref[pl.ds(CONV - 1 - k, CHUNK), :]
        d_conv_in = d_conv_in + conv_ref[k : k + 1, :] * moved
        conv_grad_ref[k] += jnp.sum((moved * conv_in).reshape(16, 8, 512), axis=0)
        if k == CONV - 1:
            conv_grad_ref[CONV] += jnp.sum(moved.reshape(16, 8, 512), axis=0)

    turned = jnp.concatenate(
        [jnp.zeros((64, CHUNK), f32), d_dt, jnp.zeros((56, CHUNK), f32)], axis=0
    ).T
    d_proj_ref[:, 0:128] = dz[:, 0:128].astype(low)
    d_proj_ref[:, 128:256] = jnp.concatenate([dz[:, 128:WIDE], turned[:, 64:128]], axis=1).astype(
        low
    )
    d_proj_ref[:, 256:PAD] = d_conv_in.astype(low)


def ssd_forward(proj, rows, conv, heads, skip):
    length = proj.shape[0]
    chunks = length // CHUNK
    whole = lambda shape: pl.BlockSpec(shape, lambda i: (0,) * len(shape))
    return pl.pallas_call(
        forward_kernel,
        grid=(chunks,),
        in_specs=[
            pl.BlockSpec((CHUNK, PAD), lambda i: (i, 0)),
            pl.BlockSpec((8, CHUNK), lambda i: (0, i)),
            whole((8, 512)),
            whole((2, 8, CHUNK)),
            whole((1, WIDE)),
        ],
        out_specs=[
            pl.BlockSpec((CHUNK, WIDE), lambda i: (i, 0)),
            pl.BlockSpec((CHUNK, WIDE), lambda i: (i, 0)),
            pl.BlockSpec((1, STATE, WIDE), lambda i: (i, 0, 0)),
        ],
        out_shape=[
            jax.ShapeDtypeStruct((length, WIDE), f32),
            jax.ShapeDtypeStruct((length, WIDE), low),
            jax.ShapeDtypeStruct((chunks, STATE, WIDE), f32),
        ],
        scratch_shapes=[pltpu.VMEM((CHUNK + 8, 512), f32), pltpu.VMEM((STATE, WIDE), f32)],
        compiler_params=pltpu.CompilerParams(
            dimension_semantics=("arbitrary",), vmem_limit_bytes=32 * 1024 * 1024
        ),
        name="ssd_forward",
    )(proj, rows, conv, heads, skip)


def ssd_backward(proj, rows, conv, heads, skip, y, u, kept):
    length = proj.shape[0]
    chunks = length // CHUNK
    back = lambda i: chunks - 1 - i
    whole = lambda shape: pl.BlockSpec(shape, lambda i: (0,) * len(shape))
    return pl.pallas_call(
        backward_kernel,
        grid=(chunks,),
        in_specs=[
            pl.BlockSpec((CHUNK, PAD), lambda i: (back(i), 0)),
            pl.BlockSpec((16, PAD), lambda i: (jnp.maximum(back(i) * (CHUNK // 16) - 1, 0), 0)),
            pl.BlockSpec((8, CHUNK), lambda i: (0, back(i))),
            whole((8, 512)),
            whole((2, 8, CHUNK)),
            whole((1, WIDE)),
            pl.BlockSpec((CHUNK, WIDE), lambda i: (back(i), 0)),
            pl.BlockSpec((CHUNK, WIDE), lambda i: (back(i), 0)),
            pl.BlockSpec((1, STATE, WIDE), lambda i: (back(i), 0, 0)),
        ],
        out_specs=[
            pl.BlockSpec((CHUNK, PAD), lambda i: (back(i), 0)),
            whole((CONV + 1, 8, 512)),
            whole((2, 8, CHUNK)),
            whole((8, WIDE)),
        ],
        out_shape=[
            jax.ShapeDtypeStruct((length, PAD), low),
            jax.ShapeDtypeStruct((CONV + 1, 8, 512), f32),
            jax.ShapeDtypeStruct((2, 8, CHUNK), f32),
            jax.ShapeDtypeStruct((8, WIDE), f32),
        ],
        scratch_shapes=[
            pltpu.VMEM((CHUNK + 8, 512), f32),
            pltpu.VMEM((CHUNK + 8, 512), f32),
            pltpu.VMEM((STATE, WIDE), f32),
        ],
        compiler_params=pltpu.CompilerParams(
            dimension_semantics=("arbitrary",), vmem_limit_bytes=32 * 1024 * 1024
        ),
        name="ssd_backward",
    )(proj, proj, rows, conv, heads, skip, y, u, kept)

epsilon = 1e-05
BOTH = ("dp", "seq")


def columns_of(a):
    rows = a.shape[0]
    z = a[:, :INNER].reshape(rows, 16, WIDE)
    x = a[:, INNER : 2 * INNER].reshape(rows, 16, WIDE)
    bc = jnp.broadcast_to(a[:, None, 2 * INNER : 2 * INNER + 256], (rows, 16, 256))
    dt = a[:, 2 * INNER + 256 :].reshape(rows, 16, OWN)
    blank = lambda n: jnp.zeros((rows, 16, n), a.dtype)
    return jnp.concatenate([z, dt, blank(61), x, blank(64), bc], axis=2).transpose(1, 0, 2)


def padded(a):
    return jnp.concatenate(
        [a[:, :WIDE], jnp.zeros((a.shape[0], 64), a.dtype), a[:, WIDE:]], axis=1
    )


def block_order(back):
    pairs = [(f, (f % 8) * 16 + f // 8) for f in range(128)]
    return [(b, a) for a, b in pairs] if back else pairs


def local(
    hidden,
    segments,
    pre_gain,
    w_in,
    conv_weight,
    conv_bias,
    dt_bias,
    a_log,
    d_skip,
    gate_gain,
    w_out,
    grad_out,
):
    me = lax.axis_index("seq")
    row = lax.axis_index("dp")
    tokens = hidden[0].astype(f32)
    r0 = lax.rsqrt(jnp.mean(tokens * tokens, axis=-1, keepdims=True) + epsilon)
    hn = (tokens * r0).astype(low)
    hn_all = lax.all_gather(hn, "seq", axis=0, tiled=True)

    gain_in = pre_gain.astype(f32)[:, None]
    gain_out = gate_gain.astype(f32)[:, None]
    w_in_wide = w_in.astype(f32)
    w_out_wide = w_out.astype(f32)
    parts = columns_of((w_in_wide * gain_in).astype(low)).reshape(16 * 12, PAD)
    parts = lax.all_to_all(parts, "seq", 0, 0, tiled=True)
    blocks = lax.ppermute((w_out_wide * gain_out).astype(low), BOTH, block_order(False))
    weights = lax.all_gather(
        jnp.concatenate([parts, blocks.reshape(48, PAD)], axis=0), "dp", axis=0
    )
    w_own = weights[:, :192].reshape(D, PAD)
    w_out_own = weights[:, 192:].reshape(WIDE, D)

    small = jnp.concatenate(
        [conv_weight.reshape(-1), conv_bias, segments[0].astype(low)]
    )
    small = lax.all_to_all(
        jnp.broadcast_to(small[None], (128, small.shape[0])), BOTH, 0, 0, tiled=True
    ).astype(f32)
    conv_all = small[:, :130].reshape(128, 5, 26).transpose(1, 0, 2).reshape(5, CONV_CH)
    conv = jnp.concatenate(
        [lax.dynamic_slice_in_dim(conv_all, me * WIDE, WIDE, 1), conv_all[:, INNER:]], axis=1
    )
    conv = jnp.concatenate([padded(conv), jnp.zeros((3, 512), f32)], axis=0)
    segment = lax.dynamic_slice_in_dim(small[:, 130:], row * 16, 16, 0).reshape(1, 2048)
    before = jnp.concatenate([jnp.full((1, 1), -1.0, f32), segment[:, :-1]], axis=1)

    own = lambda a: lax.dynamic_slice_in_dim(a, me * OWN, OWN, 0)
    tall = lambda a: jnp.broadcast_to(jnp.pad(own(a), (0, 8 - OWN))[:, None], (8, CHUNK))
    heads = jnp.stack([tall(dt_bias), tall(a_log)])
    skip = jnp.repeat(own(d_skip), 64)[None]

    proj = jnp.dot(hn_all, w_own, preferred_element_type=f32).astype(low)
    rows = jnp.concatenate([segment, before, jnp.zeros((6, 2048), f32)], axis=0)
    y, gated, kept = ssd_forward(proj, rows, conv, heads, skip)

    cot_all = lax.all_gather(grad_out[0], "seq", axis=0, tiled=True)
    u = jnp.dot(cot_all, w_out_own.T, preferred_element_type=f32)
    gated_wide = gated.astype(f32)
    sums = jnp.stack([jnp.sum(gated_wide * gated_wide, axis=1), jnp.sum(u * gated_wide, axis=1)])
    sums = lax.all_to_all(
        jnp.broadcast_to(sums.reshape(1, 32, 128), (16, 32, 128)), "seq", 0, 0, tiled=True
    )
    sums = jnp.sum(sums, axis=0).reshape(2, 2048)
    r = lax.rsqrt(sums[0:1] / INNER + epsilon)
    c = r * r * r * (sums[1:2] / INNER)

    partial_out = jnp.dot(gated, w_out_own, preferred_element_type=f32).astype(low)
    total = lax.psum_scatter(partial_out, "seq", scatter_dimension=0, tiled=True)
    r_own = lax.dynamic_slice_in_dim(r[0], me * 128, 128, 0)
    block_out = (r_own[:, None] * total.astype(f32) + tokens).astype(low)

    rows = jnp.concatenate([segment, before, r, c, jnp.zeros((4, 2048), f32)], axis=0)
    d_proj, conv_grad, head_grad, skip_grad = ssd_backward(
        proj, rows, conv, heads, skip, y, u, kept
    )
    partial_in = lax.dot_general(
        d_proj, w_own, (((1,), (1,)), ((), ())), preferred_element_type=f32
    ).astype(low)
    v = lax.psum_scatter(partial_in, "seq", scatter_dimension=0, tiled=True).astype(f32)
    mean = jnp.mean(v * tokens, axis=-1, keepdims=True)
    grad_hidden = (
        grad_out[0].astype(f32) + r0 * v - tokens * (r0 * r0 * r0 * mean)
    ).astype(low)

    grad_in = lax.dot_general(
        hn_all, d_proj, (((0,), (0,)), ((), ())), preferred_element_type=f32
    )
    normed = (gated_wide * r.reshape(2048, 1)).astype(low)
    grad_out_w = lax.dot_general(
        normed, cot_all, (((0,), (0,)), ((), ())), preferred_element_type=f32
    )
    grads = jnp.concatenate(
        [grad_in.reshape(8, 192, PAD), grad_out_w.reshape(8, 48, PAD)], axis=1
    ).astype(low)
    grads = lax.psum_scatter(grads, "dp", scatter_dimension=0, tiled=False)
    g_parts = lax.all_to_all(grads[:192], "seq", 0, 0, tiled=True).reshape(16, 12, PAD)
    g_out = lax.ppermute(grads[192:].reshape(24, D), BOTH, block_order(True)).astype(f32)
    g_parts = g_parts.astype(f32).transpose(1, 0, 2)
    g_in = jnp.concatenate(
        [
            g_parts[:, :, :WIDE].reshape(12, INNER),
            g_parts[:, :, 256 : 256 + WIDE].reshape(12, INNER),
            jnp.sum(g_parts[:, :, 512:], axis=1),
            g_parts[:, :, WIDE : WIDE + OWN].reshape(12, HEADS),
        ],
        axis=1,
    )
    grad_w_in = gain_in * g_in
    grad_pre_gain = jnp.sum(w_in_wide * g_in, axis=1)
    grad_w_out = gain_out * g_out
    grad_gate_gain = jnp.sum(w_out_wide * g_out, axis=1)

    conv_own = jnp.sum(conv_grad, axis=1)
    conv_flat = jnp.zeros((5, CONV_CH), f32)
    conv_flat = lax.dynamic_update_slice(conv_flat, conv_own[:, 256:], (0, INNER))
    conv_flat = lax.dynamic_update_slice(conv_flat, conv_own[:, :WIDE], (0, me * WIDE))
    conv_flat = conv_flat.reshape(5, 128, 26).transpose(1, 0, 2).reshape(128, 130)
    head_own = jnp.concatenate(
        [
            jnp.sum(head_grad, axis=2)[:, :OWN].reshape(-1),
            jnp.sum(skip_grad, axis=0).reshape(OWN, 64).sum(axis=1),
        ]
    )
    tail = jnp.concatenate(
        [conv_flat, jnp.broadcast_to(head_own[None], (128, 9))], axis=1
    )
    tail = lax.all_to_all(tail, BOTH, 0, 0, tiled=True)
    conv_sum = jnp.sum(tail[:, :130], axis=0).reshape(5, 26)
    head_sum = jnp.sum(tail[:, 130:].reshape(8, 16, 3, OWN), axis=0)
    head_sum = head_sum.transpose(1, 0, 2).reshape(3, HEADS)
    return (
        block_out[None],
        grad_hidden[None],
        grad_pre_gain,
        grad_w_in,
        conv_sum[:CONV],
        conv_sum[CONV],
        head_sum[0],
        head_sum[1],
        head_sum[2],
        grad_gate_gain,
        grad_w_out,
    )


def solution(mesh):
    placed = (
        P("dp", "seq", None),
        P("dp", "seq"),
        P(BOTH),
        P(BOTH, None),
        P(None, BOTH),
        P(BOTH),
        P(),
        P(),
        P(),
        P(BOTH),
        P(BOTH, None),
        P("dp", "seq", None),
    )
    return jax.shard_map(
        local,
        mesh=mesh,
        in_specs=placed,
        out_specs=(
            P("dp", "seq", None),
            P("dp", "seq", None),
            P(BOTH),
            P(BOTH, None),
            P(None, BOTH),
            P(BOTH),
            P(),
            P(),
            P(),
            P(BOTH),
            P(BOTH, None),
        ),
        check_vma=False,
    )
```

time: 1700 us -> 486 us (0.29); the launches traced: 1670 us -> 485 us
  blocking collectives: 833 us -> 13.7 us
  starting transfers between devices: 231 us -> 37.1 us
  local copies, waits for them, and re-layouts: 215 us -> 32.1 us
  waiting for transfers between devices: 174 us -> 276 us
  other arithmetic: 94.7 us -> 14.1 us
  matrix products: 107 us -> 41.1 us
  Pallas kernels: 0 us -> 56.9 us
    unnamed x3 -> x0, blocking collectives: 708 us -> none
    unnamed x33 -> x0, starting transfers between devices: 227 us -> none
    unnamed x198 -> x54, local copies, waits for them, and re-layouts: 186 us -> 11.7 us
    reduce_scatter x1 -> x3, waiting for transfers between devices: 0.01 us -> 142 us  [the longest x1 83.1 us: local(): lax.psum_scatter(partial_out, 'seq', scatter_dimension=0, tiled=True)]
    all_gather x3 -> x0, blocking collectives: 125 us -> none  [the longest x1 54.2 us: entering_2(): lax.all_gather(a.astype(kind), axis)]
    dot_general x18 -> x6, matrix products: 107 us -> 41.1 us  [the longest x1 8.71 us: local(): lax.dot_general(d_proj, w_own, (((1,), (1,)), ((), ())), preferred_elemen...]
    pallas_call x0 -> x2, Pallas kernels: none -> 56.9 us  [the longest x1 37.8 us: ssd_backward(): pl.pallas_call(backward_kernel, grid=(chunks,), in_specs=[pl.BlockSpec((C...]
    unnamed x39 -> x6, waiting for transfers between devices: 53.3 us -> 0.76 us
  transfers between devices with their start and end apart: 40 -> 12, of which waited for: 7 -> 10; matrix products, arithmetic and copies ran while one was open for 51% -> 9% of each run, Pallas kernels for 0% -> 4%
where the time goes in v1:
time: 486 us; the launch traced here: 485 us
  waiting for transfers between devices  276 us (57%)
  Pallas kernels  56.9 us (12%)
  matrix products  41.1 us (8%)
  starting transfers between devices  37.1 us (8%)
  local copies, waits for them, and re-layouts  32.1 us (7%)
  between operations  14.8 us (3%)
  other arithmetic  14.1 us (3%)
  blocking collectives  13.7 us (3%)
    reduce_scatter x1, waiting for transfers between devices, local(): lax.psum_scatter(partial_out, 'seq', scatter_dimension=0, tiled=True)  83.1 us
    all_gather x1, waiting for transfers between devices, local(): hn_all = lax.all_gather(hn, 'seq', axis=0, tiled=True)  58.9 us
    reduce_scatter x1, waiting for transfers between devices, local(): lax.psum_scatter(partial_in, 'seq', scatter_dimension=0, tiled=True)  58.8 us
    pallas_call x1, Pallas kernels, ssd_backward(): pl.pallas_call(backward_kernel, grid=(chunks,), in_specs=[pl.BlockSpec((C...  37.8 us
    all_gather x1, waiting for transfers between devices, local(): cot_all = lax.all_gather(grad_out[0], 'seq', axis=0, tiled=True)  32.7 us
    pallas_call x1, Pallas kernels, ssd_forward(): pl.pallas_call(forward_kernel, grid=(chunks,), in_specs=[pl.BlockSpec((CH...  19 us
    all_to_all x1, blocking collectives, local(): lax.all_to_all(jnp.broadcast_to(sums.reshape(1, 32, 128), (16, 32, 128)),...  13.7 us
    all_to_all x1, starting transfers between devices, local(): lax.all_to_all(jnp.broadcast_to(small[None], (128, small.shape[0])), BOTH...  13.2 us
  transfers between devices with their start and end apart: 12, of which 10 were waited for; matrix products, arithmetic and copies ran while one was open for 9% of the time, Pallas kernels for 4%

profile of v1, /device:TPU:0, one launch (start us, length us, event | category | flops | bytes accessed | tf_op | source)
XLA Modules:
  0.0 485.3 jit_solution(14319933433743195361)
XLA Ops:
  10.8 7.2 %all-to-all-start = ((bf16[16,12,768]{2,1,0:T(8,128)(2,1)}), bf16[16,12,768]{2,1,0:T(8,128)(2,1)S(1)}, u32[]{:S(2)}, u32[]{:S(2)}) async-start(bf16[16,12,768]{2,1,0:T(8,128)(2,1)} %bitcast.2), calls=%async_computation | async-start | bytes 786432 | tf_op jit(solution)/shard_map/all_to_all | solution.py:409
  18.9 9.2 %all-to-all-done = bf16[16,12,768]{2,1,0:T(8,128)(2,1)S(1)} async-done(((bf16[16,12,768]{2,1,0:T(8,128)(2,1)}), bf16[16,12,768]{2,1,0:T(8,128)(2,1)S(1)}, u32[]{:S(2)}, u32[]{:S(2)}) %all-to-all-start) | async-done | bytes 294944 | tf_op jit(solution)/shard_map/all_to_all | solution.py:409
  33.7 13.2 %all-to-all-start.1 = ((bf16[128,2,129]{2,1,0:T(2,128)(2,1)}), bf16[128,2,129]{2,1,0:T(2,128)(2,1)S(1)}, u32[]{:S(2)}, u32[]{:S(2)}) async-start(bf16[128,2,129]{2,1,0:T(2,128)(2,1)} %reshape.258), calls=%async_computation.1 | async-start | bytes 262144 | tf_op jit(solution)/shard_map/all_to_all | solution.py:420
  47.7 8.8 %all-to-all-done.1 = bf16[128,2,129]{2,1,0:T(2,128)(2,1)S(1)} async-done(((bf16[128,2,129]{2,1,0:T(2,128)(2,1)}), bf16[128,2,129]{2,1,0:T(2,128)(2,1)S(1)}, u32[]{:S(2)}, u32[]{:S(2)}) %all-to-all-start.1) | async-done | bytes 66080 | tf_op jit(solution)/shard_map/all_to_all | solution.py:420
  57.8 4.5 all-gather.8.cloned.1.call-done
  63.4 3.3 slice.136
  67.6 58.9 %all-gather.6.cloned.1.call-done = bf16[2048,1536]{1,0:T(8,128)(2,1)} async-done(((bf16[128,1536]{1,0:T(8,128)(2,1)}), bf16[2048,1536]{1,0:T(8,128)(2,1)}) %all-gather.6.cloned.1.call-update) | async-done | bytes 6291472 | tf_op jit(solution)/shard_map/all_gather | solution.py:402
  126.5 7.8 %convolution_convert_fusion.3.proj_ref.before_ref = bf16[2048,768]{1,0:T(8,128)(2,1)S(1)} fusion(bf16[2048,1536]{1,0:T(8,128)(2,1)} %all-gather.6.cloned.1.call-done, bf16[1536,768]{1,0:T(8,128)(2,1)} %bitcast.76), kind=kOutput, calls=%fused_computation.7 | convolution fusion | flops 4833411072 | bytes 11796480 | tf_op jit(solution)/shard_map/dot_general | solution.py:436
  134.4 19.0 %ssd_forward.1 = (f32[2048,192]{1,0:T(8,128)S(1)}, bf16[2048,192]{1,0:T(8,128)(2,1)S(1)}, f32[16,128,192]{2,1,0:T(8,128)S(1)}) custom-call(bf16[2048,768]{1,0:T(8,128)(2,1)S(1)} %convolution_convert_fusion.3.proj_ref.before_ref, f32[8,2048]{1,0:T(8,128)S(1)} %maximum_maximum_fusion.rows_ref, f32[8,512]{1,0:T(8,128)S(1)} %concatenate.43.conv_ref, ...), custom_call_target="tpu_custom_call" | custom-call | tf_op jit(solution)/shard_map/ssd_forward/pallas_call | solution.py:288
  157.0 32.7 %all-gather.10.cloned.1.call-done = bf16[1,2048,1536]{2,1,0:T(8,128)(2,1)} async-done(((bf16[1,128,1536]{2,1,0:T(8,128)(2,1)}), bf16[1,2048,1536]{2,1,0:T(8,128)(2,1)}) %all-gather.10.cloned.1.call-update) | async-done | bytes 6291472 | tf_op jit(solution)/shard_map/all_gather | solution.py:440
  189.7 6.4 %fusion.10 = (f32[2048]{0:T(1024)S(1)}, f32[2048]{0:T(1024)S(1)}, f32[2048,192]{1,0:T(8,128)}) fusion(bf16[2048,192]{1,0:T(8,128)(2,1)} %copy-done, bf16[192,1536]{1,0:T(8,128)(2,1)} %reshape.240, bf16[1,2048,1536]{2,1,0:T(8,128)(2,1)} %all-gather.10.cloned.1.call-done), kind=kOutput, calls=%fused_computation.14 | convolution fusion | flops 1209921536 | bytes 9256960 | tf_op jit(solution)/shard_map/dot_general | solution.py:441
  196.2 13.7 %all_to_all.41 = f32[16,32,128]{2,1,0:T(8,128)S(1)} all-to-all(f32[16,32,128]{2,1,0:T(8,128)S(1)} %broadcast_in_dim.66), channel_id=1, replica_groups=mesh['dp'=8,'seq'=16] {'seq'}, dimensions={0} | all-to-all | bytes 524288 | tf_op jit(solution)/shard_map/all_to_all | solution.py:444
  210.0 5.4 %fusion.7 = bf16[192,1536]{1,0:T(8,128)(2,1)} fusion(bf16[1,2048,1536]{2,1,0:T(8,128)(2,1)} %all-gather.10.cloned.1.call-done, bf16[2048,192]{1,0:T(8,128)(2,1)} %copy-done, f32[2048]{0:T(1024)S(1)} %get-tuple-element.37), kind=kOutput, calls=%fused_computation.13 | convolution fusion | flops 1209434112 | bytes 7675904 | tf_op jit(solution)/shard_map/dot_general | solution.py:473
  222.4 37.8 %ssd_backward.1 = (bf16[2048,768]{1,0:T(8,128)(2,1)S(1)}, f32[5,8,512]{2,1,0:T(8,128)S(1)}, f32[2,8,128]{2,1,0:T(8,128)S(1)}, f32[8,192]{1,0:T(8,128)S(1)}) custom-call(bf16[2048,768]{1,0:T(8,128)(2,1)S(1)} %convolution_convert_fusion.3.proj_ref.before_ref, bf16[2048,768]{1,0:T(8,128)(2,1)S(1)} %convolution_convert_fusion.3.proj_ref.before_ref, ...), custom_call_target="tpu_custom_call" | custom-call | tf_op jit(solution)/shard_map/ssd_backward/pallas_call | solution.py:321
  260.2 8.4 %convolution_convert_fusion.2 = bf16[1536,768]{1,0:T(8,128)(2,1)S(1)} fusion(bf16[2048,1536]{1,0:T(8,128)(2,1)} %all-gather.6.cloned.1.call-done, bf16[2048,768]{1,0:T(8,128)(2,1)S(1)} %get-tuple-element.21), kind=kOutput, calls=%fused_computation.6 | convolution fusion | flops 4833017856 | bytes 11796480 | tf_op jit(solution)/shard_map/dot_general | solution.py:469
  271.6 8.7 %convolution_convert_fusion = bf16[2048,1536]{1,0:T(8,128)(2,1)} fusion(bf16[2048,768]{1,0:T(8,128)(2,1)S(1)} %copy-done.8, bf16[1536,768]{1,0:T(8,128)(2,1)} %bitcast.77), kind=kOutput, calls=%fused_computation | convolution fusion | flops 4834983936 | bytes 11796480 | tf_op jit(solution)/shard_map/dot_general | solution.py:460
  281.7 4.4 convolution_convert_fusion.1
  288.3 6.3 %all-to-all-start.4 = ((f32[128,1,139]{2,1,0:T(1,128)}), f32[128,1,139]{2,1,0:T(1,128)S(1)}, u32[]{:S(2)}, u32[]{:S(2)}) async-start(f32[128,1,139]{2,1,0:T(1,128)} %copy.95), calls=%async_computation.7 | async-start | bytes 262144 | tf_op jit(solution)/shard_map/all_to_all | solution.py:511
  294.6 9.6 %all-to-all-done.4 = f32[128,1,139]{2,1,0:T(1,128)S(1)} async-done(((f32[128,1,139]{2,1,0:T(1,128)}), f32[128,1,139]{2,1,0:T(1,128)S(1)}, u32[]{:S(2)}, u32[]{:S(2)}) %all-to-all-start.4) | async-done | bytes 71200 | tf_op jit(solution)/shard_map/all_to_all | solution.py:511
  308.1 8.7 %all-to-all-start.3 = ((bf16[16,12,768]{2,1,0:T(8,128)(2,1)}), bf16[16,12,768]{2,1,0:T(8,128)(2,1)S(1)}, u32[]{:S(2)}, u32[]{:S(2)}) async-start(bf16[16,12,768]{2,1,0:T(8,128)(2,1)} %all_to_all.31), calls=%async_computation.6 | async-start | bytes 786432 | tf_op jit(solution)/shard_map/all_to_all | solution.py:480
  321.6 8.9 %all-to-all-done.3 = bf16[16,12,768]{2,1,0:T(8,128)(2,1)S(1)} async-done(((bf16[16,12,768]{2,1,0:T(8,128)(2,1)}), bf16[16,12,768]{2,1,0:T(8,128)(2,1)S(1)}, u32[]{:S(2)}, u32[]{:S(2)}) %all-to-all-start.3) | async-done | bytes 294944 | tf_op jit(solution)/shard_map/all_to_all | solution.py:480
  333.0 58.8 %reduce-scatter.6.cloned.1.call-done = bf16[128,1536]{1,0:T(8,128)(2,1)} async-done(((bf16[2048,1536]{1,0:T(8,128)(2,1)}), bf16[128,1536]{1,0:T(8,128)(2,1)}) %reduce-scatter.6.cloned.1.call-update) | async-done | bytes 393232 | tf_op jit(solution)/shard_map/reduce_scatter | solution.py:463
  393.0 83.1 %reduce-scatter.4.cloned.1.call-done = bf16[128,1536]{1,0:T(8,128)(2,1)} async-done(((bf16[2048,1536]{1,0:T(8,128)(2,1)}), bf16[128,1536]{1,0:T(8,128)(2,1)}) %reduce-scatter.4.cloned.1.call-update) | async-done | bytes 393232 | tf_op jit(solution)/shard_map/reduce_scatter | solution.py:452
  476.1 2.4 fusion.25
  (193 shorter events, 43.2 us)
Async XLA Ops:
  7.2 21.8 %copy-start.9 = (bf16[1,128,1536]{2,1,0:T(8,128)(2,1)S(1)}, bf16[1,128,1536]{2,1,0:T(8,128)(2,1)}, u32[]{:S(2)}) copy-start(bf16[1,128,1536]{2,1,0:T(8,128)(2,1)} %param.12) | copy-start | bytes 1179652
  9.7 21.2 %copy-start.22 = (s32[1,128]{1,0:T(1,128)S(1)}, s32[1,128]{1,0:T(1,128)}, u32[]{:S(2)}) copy-start(s32[1,128]{1,0:T(1,128)} %param.13) | copy-start | bytes 1540
  9.7 21.2 %copy-start.19 = (bf16[26]{0:T(256)(128)(2,1)S(1)}, bf16[26]{0:T(256)(128)(2,1)}, u32[]{:S(2)}) copy-start(bf16[26]{0:T(256)(128)(2,1)} %param.17) | copy-start | bytes 160
  10.8 36.2 %copy-start.23 = (f32[48]{0:T(128)S(1)}, f32[48]{0:T(128)}, u32[]{:S(2)}) copy-start(f32[48]{0:T(128)} %param.18) | copy-start | bytes 580
  10.8 36.3 %copy-start.24 = (f32[48]{0:T(128)S(1)}, f32[48]{0:T(128)}, u32[]{:S(2)}) copy-start(f32[48]{0:T(128)} %param.19) | copy-start | bytes 580
  10.8 36.4 %copy-start.25 = (f32[48]{0:T(128)S(1)}, f32[48]{0:T(128)}, u32[]{:S(2)}) copy-start(f32[48]{0:T(128)} %param.20) | copy-start | bytes 580
  10.8 17.3 %all-to-all-start = ((bf16[16,12,768]{2,1,0:T(8,128)(2,1)}), bf16[16,12,768]{2,1,0:T(8,128)(2,1)S(1)}, u32[]{:S(2)}, u32[]{:S(2)}) async-start(bf16[16,12,768]{2,1,0:T(8,128)(2,1)} %bitcast.2), calls=%async_computation | async-start | bytes 786432 | tf_op jit(solution)/shard_map/all_to_all | solution.py:409
  18.0 44.2 %all-gather.8.cloned.1.call-start = ((), (), s32[]{:S(2)}) async-start(), calls=%async_computation.12 | async-start | bytes 3317760 | tf_op jit(solution)/shard_map/all_gather | solution.py:411
  18.2 0.7 collective-permute-start
  29.0 97.5 %all-gather.6.cloned.1.call-start = ((), (), s32[]{:S(2)}) async-start(), calls=%async_computation.8 | async-start | bytes 6684672 | tf_op jit(solution)/shard_map/all_gather | solution.py:402
  29.2 27.8 %copy-start.17 = (f32[128]{0:T(128)}, f32[128]{0:T(128)S(1)}, u32[]{:S(2)}) copy-start(f32[128]{0:T(128)S(1)} %fusion.18) | copy-start | bytes 1540
  30.1 159.6 %all-gather.10.cloned.1.call-start = ((), (), s32[]{:S(2)}) async-start(), calls=%async_computation.13 | async-start | bytes 6684672 | tf_op jit(solution)/shard_map/all_gather | solution.py:440
  33.7 22.8 %all-to-all-start.1 = ((bf16[128,2,129]{2,1,0:T(2,128)(2,1)}), bf16[128,2,129]{2,1,0:T(2,128)(2,1)S(1)}, u32[]{:S(2)}, u32[]{:S(2)}) async-start(bf16[128,2,129]{2,1,0:T(2,128)(2,1)} %reshape.258), calls=%async_computation.1 | async-start | bytes 262144 | tf_op jit(solution)/shard_map/all_to_all | solution.py:420
  46.9 257.8 %reduce-scatter.8.cloned.1.call-start = ((), (), s32[]{:S(2)}) async-start(), calls=%async_computation.11 | async-start | bytes 3317760 | tf_op jit(solution)/shard_map/reduce_scatter | solution.py:479
  270.5 121.3 %reduce-scatter.6.cloned.1.call-start = ((), (), s32[]{:S(2)}) async-start(), calls=%async_computation.10 | async-start | bytes 6684672 | tf_op jit(solution)/shard_map/reduce_scatter | solution.py:463
  280.3 195.7 %reduce-scatter.4.cloned.1.call-start = ((), (), s32[]{:S(2)}) async-start(), calls=%async_computation.9 | async-start | bytes 6684672 | tf_op jit(solution)/shard_map/reduce_scatter | solution.py:452
  286.1 34.2 %copy-start.16 = (bf16[24,1536]{1,0:T(8,128)(2,1)S(1)}, bf16[24,1536]{1,0:T(8,128)(2,1)}, u32[]{:S(2)}) copy-start(bf16[24,1536]{1,0:T(8,128)(2,1)} %param.22) | copy-start | bytes 221188
  288.3 15.9 %all-to-all-start.4 = ((f32[128,1,139]{2,1,0:T(1,128)}), f32[128,1,139]{2,1,0:T(1,128)S(1)}, u32[]{:S(2)}, u32[]{:S(2)}) async-start(f32[128,1,139]{2,1,0:T(1,128)} %copy.95), calls=%async_computation.7 | async-start | bytes 262144 | tf_op jit(solution)/shard_map/all_to_all | solution.py:511
  305.6 14.6 %collective-permute-start.1 = (bf16[24,1536]{1,0:T(8,128)(2,1)S(1)}, bf16[24,1536]{1,0:T(8,128)(2,1)S(1)}, u32[]{:S(2)}, u32[]{:S(2)}) collective-permute-start(bf16[24,1536]{1,0:T(8,128)(2,1)S(1)} %reshape.251), channel_id=1, source_target_pairs={{0,0},{16,1},{32,2},{48,3},{64,4},{80,5},{96,6},{112,7},{1,8},{17,... | collective-permute-start | bytes 221192 | tf_op jit(solution)/shard_map/ppermute | solution.py:481
  308.1 23.4 %copy-start.14 = (bf16[12,6448]{1,0:T(8,128)(2,1)S(1)}, bf16[12,6448]{1,0:T(8,128)(2,1)}, u32[]{:S(2)}) copy-start(bf16[12,6448]{1,0:T(8,128)(2,1)} %param.15) | copy-start | bytes 464260
  308.1 22.4 %all-to-all-start.3 = ((bf16[16,12,768]{2,1,0:T(8,128)(2,1)}), bf16[16,12,768]{2,1,0:T(8,128)(2,1)S(1)}, u32[]{:S(2)}, u32[]{:S(2)}) async-start(bf16[16,12,768]{2,1,0:T(8,128)(2,1)} %all_to_all.31), calls=%async_computation.6 | async-start | bytes 786432 | tf_op jit(solution)/shard_map/all_to_all | solution.py:480
  316.8 75.0 %copy-start.10 = (bf16[1,128,1536]{2,1,0:T(8,128)(2,1)S(1)}, bf16[1,128,1536]{2,1,0:T(8,128)(2,1)}, u32[]{:S(2)}) copy-start(bf16[1,128,1536]{2,1,0:T(8,128)(2,1)} %param.12) | copy-start | bytes 1179652
  321.6 71.4 %copy-start.18 = (f32[128]{0:T(128)S(1)}, f32[128]{0:T(128)}, u32[]{:S(2)}) copy-start(f32[128]{0:T(128)} %copy-done.17) | copy-start | bytes 1540
  321.6 154.5 %copy-start.13 = (bf16[1,128,1536]{2,1,0:T(8,128)(2,1)S(1)}, bf16[1,128,1536]{2,1,0:T(8,128)(2,1)}, u32[]{:S(2)}) copy-start(bf16[1,128,1536]{2,1,0:T(8,128)(2,1)} %param.23) | copy-start | bytes 1179652
  (14 other events, 73.8 us)
Sparse Core Ops, SparseCore 0:
  29.1 33.1 all-gather.7
  65.0 61.5 all-gather.5
  128.7 61.0 all-gather.9
  270.6 34.0 reduce-scatter.7
  308.4 83.3 reduce-scatter.5
  395.5 80.5 reduce-scatter.3

commit v2 on v1

v2 whole, which is shorter than its diff:
```python
import jax
import jax.numpy as jnp
from jax import lax
from jax.experimental import pallas as pl
from jax.experimental.pallas import tpu as pltpu
from jax.sharding import PartitionSpec as P

D = 1536
INNER = 3072
STATE = 128
CONV = 4
HEADS = 48
CONV_CH = 3328
CHUNK = 128
GROUP = 4
BLOCK = CHUNK * GROUP
OWN = 3
WIDE = 192
PAD = 768
low = jnp.bfloat16
f32 = jnp.float32


def mm(a, b, dims=((1,), (0,))):
    return lax.dot_general(a, b, (dims, ((), ())), preferred_element_type=f32)


NT = ((1,), (1,))
TN = ((0,), (0,))


def per_head(parts):
    lane = lax.broadcasted_iota(jnp.int32, (1, WIDE), 1)
    return jnp.where(lane < 64, parts[0], jnp.where(lane < 128, parts[1], parts[2]))


def stacked(a):
    lane = lax.broadcasted_iota(jnp.int32, a.shape, 1)
    zero = jnp.zeros_like(a)
    return jnp.concatenate(
        [jnp.where((lane >= 64 * h) & (lane < 64 * h + 64), a, zero) for h in range(OWN)], axis=0
    )


def running(a, back):
    lane = lax.broadcasted_iota(jnp.int32, a.shape, 1)
    step = 1
    while step < CHUNK:
        if back:
            a = a + jnp.where(lane < CHUNK - step, pltpu.roll(a, CHUNK - step, 1), 0.0)
        else:
            a = a + jnp.where(lane >= step, pltpu.roll(a, step, 1), 0.0)
        step *= 2
    return a


def part(a, j):
    return a[CHUNK * j : CHUNK * (j + 1)]


def eight(a, j):
    return a[8 * j : 8 * (j + 1)]


def block_terms(zdt, rows_ref, head_ref):
    raw = jnp.concatenate([part(zdt, j)[:, 128:256].T[64:72] for j in range(GROUP)], axis=0)
    wide = lambda row: jnp.concatenate(
        [jnp.broadcast_to(rows_ref[j, row : row + 1, :], (8, CHUNK)) for j in range(GROUP)], axis=0
    )
    v = raw + head_ref[0]
    ea = jnp.exp(head_ref[1])
    step = jnp.maximum(v, 0.0) + jnp.log1p(jnp.exp(-jnp.abs(v)))
    ld = -step * ea
    cum = running(ld, False)
    total = cum[:, CHUNK - 1 : CHUNK]
    seg = wide(0)
    before = wide(1)[:, 0:1]
    last = seg[:, CHUNK - 1 : CHUNK]
    entry = jnp.exp(cum) * (seg == before).astype(f32)
    to_end = jnp.exp(total - cum) * (seg == last).astype(f32)
    whole = jnp.exp(total) * (last == before).astype(f32)
    leaving = to_end * step
    cols = []
    for j in range(GROUP):
        pack = [eight(cum, j), eight(entry, j), eight(leaving, j), rows_ref[j]]
        pack = jnp.concatenate(pack + [jnp.zeros((CHUNK - 32, CHUNK), f32)], axis=0)
        cols.append(pack.T)
    return v, ea, step, ld, cum, to_end, whole, cols


def barred(cols, seg):
    t = lax.broadcasted_iota(jnp.int32, (CHUNK, CHUNK), 0)
    s = lax.broadcasted_iota(jnp.int32, (CHUNK, CHUNK), 1)
    return jnp.where((t >= s) & (cols[:, 24:25] == seg), 0.0, -1e30)


def convolved(ext_ref, conv_ref):
    pre = conv_ref[CONV : CONV + 1, :]
    for k in range(CONV):
        pre = pre + conv_ref[k : k + 1, :] * ext_ref[pl.ds(5 + k, BLOCK), :]
    return pre


def forward_kernel(
    both_ref,
    w_ref,
    out_ref,
    rows_ref,
    conv_ref,
    head_ref,
    skip_ref,
    proj_ref,
    y_ref,
    gated_ref,
    u_ref,
    kept_ref,
    total_ref,
    sums_ref,
    ext_ref,
    state_ref,
):
    first = pl.program_id(0) == 0

    @pl.when(first)
    def _():
        ext_ref[0:8, :] = jnp.zeros((8, 512), f32)
        state_ref[...] = jnp.zeros_like(state_ref)

    @pl.when(jnp.logical_not(first))
    def _():
        ext_ref[0:8, :] = ext_ref[BLOCK : BLOCK + 8, :]

    proj_ref[...] = mm(both_ref[:, 0:D], w_ref[...]).astype(low)
    u_ref[...] = mm(both_ref[:, D : 2 * D], out_ref[...], NT)
    zdt = proj_ref[:, 0:256].astype(f32)
    ext_ref[8 : BLOCK + 8, :] = proj_ref[:, 256:PAD].astype(f32)
    pre = convolved(ext_ref, conv_ref)
    act = pre * jax.nn.sigmoid(pre)
    x = act[:, :WIDE]
    x_low = x.astype(low)
    b_low = act[:, 256:384].astype(low)
    c_low = act[:, 384:512].astype(low)
    v, ea, step, ld, cum, to_end, whole, cols = block_terms(zdt, rows_ref, head_ref)
    inner, local, entries, wholes = [], [], [], []
    for j in range(GROUP):
        col = cols[j]
        bar = barred(col, rows_ref[j, 0:1, :])
        scores = mm(part(c_low, j), part(b_low, j), NT)
        mixing = []
        for h in range(OWN):
            i = 8 * j + h
            decay = jnp.exp(col[:, h : h + 1] - cum[i : i + 1] + bar)
            mixing.append((scores * decay * step[i : i + 1]).astype(low))
        inner.append(mm(jnp.concatenate(mixing, axis=1), stacked(part(x_low, j))))
        leaving = per_head([col[:, 16 + h : 17 + h] for h in range(OWN)])
        local.append(mm(part(b_low, j), (leaving * part(x, j)).astype(low), TN))
        entries.append(per_head([col[:, 8 + h : 9 + h] for h in range(OWN)]))
        wholes.append(per_head([whole[8 * j + h : 8 * j + h + 1] for h in range(OWN)]))
    state = state_ref[...]
    ys = []
    for j in range(GROUP):
        kept_ref[j] = state
        ys.append(inner[j] + entries[j] * mm(part(c_low, j), state.astype(low)))
        state = wholes[j] * state + local[j]
    state_ref[...] = state
    y = jnp.concatenate(ys, axis=0) + skip_ref[...] * x
    z = zdt[:, :WIDE]
    gated = y * z * jax.nn.sigmoid(z)
    gated_low = gated.astype(low)
    y_ref[...] = y
    gated_ref[...] = gated_low
    total_ref[...] = mm(gated_low, out_ref[...]).astype(low)
    ones = jnp.ones((8, WIDE), low)
    squares = mm(ones, (gated * gated).astype(low), NT)
    products = mm(ones, (gated * u_ref[...]).astype(low), NT)
    row = lax.broadcasted_iota(jnp.int32, (8, BLOCK), 0)
    sums_ref[...] = jnp.where(row == 0, squares, products)


def backward_kernel(
    place_ref,
    proj_ref,
    before_ref,
    w_ref,
    cot_ref,
    rows_ref,
    conv_ref,
    head_ref,
    skip_ref,
    y_ref,
    gated_ref,
    u_ref,
    kept_ref,
    d_proj_ref,
    top_ref,
    bottom_ref,
    out_grad_ref,
    sums_ref,
    ext_ref,
    later_ref,
    state_ref,
    conv_grad_ref,
    head_grad_ref,
    skip_grad_ref,
):
    step_id = pl.program_id(0)
    count = pl.num_programs(0)

    @pl.when(step_id == 0)
    def _():
        later_ref[BLOCK : BLOCK + 8, :] = jnp.zeros((8, 512), f32)
        state_ref[...] = jnp.zeros_like(state_ref)
        conv_grad_ref[...] = jnp.zeros_like(conv_grad_ref)
        head_grad_ref[...] = jnp.zeros_like(head_grad_ref)
        skip_grad_ref[...] = jnp.zeros_like(skip_grad_ref)
        out_grad_ref[...] = jnp.zeros_like(out_grad_ref)

    @pl.when(step_id > 0)
    def _():
        later_ref[BLOCK : BLOCK + 8, :] = later_ref[0:8, :]

    ahead = before_ref[8:16, 256:PAD].astype(f32)
    ext_ref[0:8, :] = jnp.where(step_id == count - 1, 0.0, ahead)
    conv_in = proj_ref[:, 256:PAD].astype(f32)
    ext_ref[8 : BLOCK + 8, :] = conv_in
    zdt = proj_ref[:, 0:256].astype(f32)
    pre = convolved(ext_ref, conv_ref)
    sig = jax.nn.sigmoid(pre)
    act = pre * sig
    slope = sig * (1.0 + pre * (1.0 - sig))
    x = act[:, :WIDE]
    x_low = x.astype(low)
    b_low = act[:, 256:384].astype(low)
    c_low = act[:, 384:512].astype(low)
    v, ea, step, ld, cum, to_end, whole, cols = block_terms(zdt, rows_ref, head_ref)

    z = zdt[:, :WIDE]
    z_sig = jax.nn.sigmoid(z)
    z_act = z * z_sig
    y = y_ref[...]
    r_col = jnp.concatenate([c[:, 26:27] for c in cols], axis=0)
    c_col = jnp.concatenate([c[:, 27:28] for c in cols], axis=0)
    d_gated = r_col * u_ref[...] - c_col * (y * z_act)
    dy = d_gated * z_act
    dz = d_gated * y * (z_sig * (1.0 + z * (1.0 - z_sig)))
    dy_low = dy.astype(low)
    normed = (gated_ref[...].astype(f32) * r_col).astype(low)
    out_grad_ref[...] += mm(normed, cot_ref[...], TN)

    t = lax.broadcasted_iota(jnp.int32, (CHUNK, CHUNK), 0)
    s = lax.broadcasted_iota(jnp.int32, (CHUNK, CHUNK), 1)
    earlier = (t < s).astype(low)
    blank = jnp.zeros((8 - OWN, CHUNK), f32)
    row_head = lax.broadcasted_iota(jnp.int32, (8, WIDE), 0)
    lane = lax.broadcasted_iota(jnp.int32, (8, WIDE), 1)
    by_head = ((lane >= 64 * row_head) & (lane < 64 * row_head + 64)).astype(low)

    dx_in, d_scores_all, d_steps_all, inside_all = [], [], [], []
    entries, leavings, wholes, to_state, dy_entries = [], [], [], [], []
    for j in range(GROUP):
        col = cols[j]
        bar = barred(col, rows_ref[j, 0:1, :])
        scores = mm(part(c_low, j), part(b_low, j), NT)
        d_mixing = mm(part(dy_low, j), stacked(part(x_low, j)), NT)
        d_scores = jnp.zeros((CHUNK, CHUNK), f32)
        mixings, flows, d_steps = [], [], []
        for h in range(OWN):
            i = 8 * j + h
            decay = jnp.exp(col[:, h : h + 1] - cum[i : i + 1] + bar)
            stepped = decay * step[i : i + 1]
            mixing = scores * stepped
            mixings.append(mixing.astype(low))
            d_mix = d_mixing[:, CHUNK * h : CHUNK * h + CHUNK]
            d_scores = d_scores + d_mix * stepped
            flows.append((d_mix * mixing).astype(low))
            d_steps.append(jnp.sum(d_mix * scores * decay, axis=0, keepdims=True))
        reach = mm(jnp.concatenate(flows, axis=0), earlier)
        inside = [
            jnp.sum(jnp.where(t >= s, part(reach, h), 0.0), axis=0, keepdims=True)
            for h in range(OWN)
        ]
        d_scores_all.append(d_scores.astype(low))
        d_steps_all += d_steps + [blank]
        inside_all += inside + [blank]
        dx_in.append(mm(jnp.concatenate(mixings, axis=0), stacked(part(dy_low, j)), TN))
        entry = per_head([col[:, 8 + h : 9 + h] for h in range(OWN)])
        dy_entry = entry * part(dy, j)
        dy_entries.append(dy_entry)
        to_state.append(mm(part(c_low, j), dy_entry.astype(low), TN))
        leavings.append(per_head([col[:, 16 + h : 17 + h] for h in range(OWN)]))
        wholes.append(per_head([whole[8 * j + h : 8 * j + h + 1] for h in range(OWN)]))

    laters = [None] * GROUP
    later = state_ref[...]
    for j in reversed(range(GROUP)):
        laters[j] = later
        later = wholes[j] * later + to_state[j]
    state_ref[...] = later

    xv, row_state, overlap, dxs, dbs, dcs = [], [], [], [], [], []
    for j in range(GROUP):
        bj, cj, xj = part(b_low, j), part(c_low, j), part(x, j)
        state_low = kept_ref[j].astype(low)
        later_low = laters[j].astype(low)
        from_later = mm(bj, later_low)
        dxs.append(dx_in[j] + leavings[j] * from_later)
        x_leaving = (leavings[j] * xj).astype(low)
        d_scores = d_scores_all[j]
        dcs.append(mm(d_scores, bj) + mm(dy_entries[j].astype(low), state_low, NT))
        dbs.append(mm(d_scores, cj, TN) + mm(x_leaving, later_low, NT))
        xv.append(mm(by_head, (xj * from_later).astype(low), NT))
        row_state.append(mm(by_head, (dy_entries[j] * mm(cj, state_low)).astype(low), NT))
        both = mm(by_head, (laters[j] * kept_ref[j]).astype(low), NT)
        overlap.append(jnp.sum(both, axis=1, keepdims=True))
    stack = lambda a: jnp.concatenate(a, axis=0)
    ended = to_end * stack(xv)
    col_state = ended * step
    d_step = stack(d_steps_all) + ended
    d_ld = (
        stack(inside_all)
        + running(stack(row_state), True)
        + (running(col_state, False) - col_state)
        + whole * stack(overlap)
    )
    d_dt = (d_step - d_ld * ea) * jax.nn.sigmoid(v)
    head_grad_ref[0] += sum([eight(d_dt, j) for j in range(GROUP)])
    head_grad_ref[1] += sum([eight(d_ld * ld, j) for j in range(GROUP)])
    skip_grad_ref[...] += jnp.sum((dy * x).reshape(BLOCK // 8, 8, WIDE), axis=0)

    dx = stack(dxs) + skip_ref[...] * dy
    later_ref[0:BLOCK, 0:WIDE] = dx * slope[:, :WIDE]
    later_ref[0:BLOCK, WIDE:256] = jnp.zeros((BLOCK, 256 - WIDE), f32)
    later_ref[0:BLOCK, 256:384] = stack(dbs) * slope[:, 256:384]
    later_ref[0:BLOCK, 384:512] = stack(dcs) * slope[:, 384:512]
    d_conv_in = jnp.zeros((BLOCK, 512), f32)
    for k in range(CONV):
        moved = later_ref[pl.ds(CONV - 1 - k, BLOCK), :]
        d_conv_in = d_conv_in + conv_ref[k : k + 1, :] * moved
        conv_grad_ref[k] += jnp.sum((moved * conv_in).reshape(BLOCK // 8, 8, 512), axis=0)
        if k == CONV - 1:
            conv_grad_ref[CONV] += jnp.sum(moved.reshape(BLOCK // 8, 8, 512), axis=0)

    turned = []
    for j in range(GROUP):
        tall = [jnp.zeros((64, CHUNK), f32), eight(d_dt, j), jnp.zeros((56, CHUNK), f32)]
        turned.append(jnp.concatenate(tall, axis=0).T)
    d_proj_ref[:, 0:128] = dz[:, 0:128].astype(low)
    d_proj_ref[:, 128:256] = jnp.concatenate(
        [dz[:, 128:WIDE], stack(turned)[:, 64:128]], axis=1
    ).astype(low)
    d_proj_ref[:, 256:PAD] = d_conv_in.astype(low)

    row = count - 1 - step_id
    my_x, my_y = place_ref[0], place_ref[1]
    up = lax.rem(row - my_y + 4, 4)
    for j in range(GROUP):
        given = mm(d_proj_ref[CHUNK * j : CHUNK * (j + 1), :], w_ref[...], NT).astype(low)
        top_ref[up, j] = given[:64]
        bottom_ref[lax.rem(j - my_x + 4, 4), row] = given[64:]

    @pl.when(step_id == count - 1)
    def _():
        sums_ref[...] = jnp.zeros_like(sums_ref)
        for k in range(CONV + 1):
            sums_ref[k : k + 1, :] = jnp.sum(conv_grad_ref[k], axis=0, keepdims=True)
        sums_ref[5:6, 0:WIDE] = jnp.sum(skip_grad_ref[...], axis=0, keepdims=True)
        place = lax.broadcasted_iota(jnp.int32, (8, CHUNK), 1)
        bias = jnp.sum(head_grad_ref[0], axis=1, keepdims=True)
        rate = jnp.sum(head_grad_ref[1], axis=1, keepdims=True)
        sums_ref[8:16, 0:CHUNK] = jnp.where(place == 0, bias, jnp.where(place == 1, rate, 0.0))


def ssd_forward(both, w, w_out, rows, conv, heads, skip):
    length = both.shape[0]
    steps = length // BLOCK
    whole = lambda shape: pl.BlockSpec(shape, lambda i: (0,) * len(shape))
    here = lambda width: pl.BlockSpec((BLOCK, width), lambda i: (i, 0))
    return pl.pallas_call(
        forward_kernel,
        grid=(steps,),
        in_specs=[
            here(2 * D),
            whole((D, PAD)),
            whole((WIDE, D)),
            pl.BlockSpec((GROUP, 8, CHUNK), lambda i: (i, 0, 0)),
            whole((8, 512)),
            whole((2, 8 * GROUP, CHUNK)),
            whole((1, WIDE)),
        ],
        out_specs=[
            here(PAD),
            here(WIDE),
            here(WIDE),
            here(WIDE),
            pl.BlockSpec((GROUP, STATE, WIDE), lambda i: (i, 0, 0)),
            here(D),
            pl.BlockSpec((8, BLOCK), lambda i: (0, i)),
        ],
        out_shape=[
            jax.ShapeDtypeStruct((length, PAD), low),
            jax.ShapeDtypeStruct((length, WIDE), f32),
            jax.ShapeDtypeStruct((length, WIDE), low),
            jax.ShapeDtypeStruct((length, WIDE), f32),
            jax.ShapeDtypeStruct((length // CHUNK, STATE, WIDE), f32),
            jax.ShapeDtypeStruct((length, D), low),
            jax.ShapeDtypeStruct((8, length), f32),
        ],
        scratch_shapes=[pltpu.VMEM((BLOCK + 8, 512), f32), pltpu.VMEM((STATE, WIDE), f32)],
        compiler_params=pltpu.CompilerParams(
            dimension_semantics=("arbitrary",), vmem_limit_bytes=56 * 1024 * 1024
        ),
        name="ssd_forward",
    )(both, w, w_out, rows, conv, heads, skip)


def ssd_backward(place, both, w, proj, rows, conv, heads, skip, y, gated, u, kept):
    length = proj.shape[0]
    steps = length // BLOCK
    back = lambda i: steps - 1 - i
    whole = lambda shape: pl.BlockSpec(shape, lambda i: (0,) * len(shape))
    here = lambda width: pl.BlockSpec((BLOCK, width), lambda i: (back(i), 0))
    return pl.pallas_call(
        backward_kernel,
        grid=(steps,),
        in_specs=[
            pl.BlockSpec(memory_space=pltpu.SMEM),
            here(PAD),
            pl.BlockSpec((16, PAD), lambda i: (jnp.maximum(back(i) * (BLOCK // 16) - 1, 0), 0)),
            whole((D, PAD)),
            pl.BlockSpec((BLOCK, D), lambda i: (back(i), 1)),
            pl.BlockSpec((GROUP, 8, CHUNK), lambda i: (back(i), 0, 0)),
            whole((8, 512)),
            whole((2, 8 * GROUP, CHUNK)),
            whole((1, WIDE)),
            here(WIDE),
            here(WIDE),
            here(WIDE),
            pl.BlockSpec((GROUP, STATE, WIDE), lambda i: (back(i), 0, 0)),
        ],
        out_specs=[
            here(PAD),
            whole((4, 4, 64, D)),
            whole((4, 4, 64, D)),
            whole((WIDE, D)),
            whole((16, 512)),
        ],
        out_shape=[
            jax.ShapeDtypeStruct((length, PAD), low),
            jax.ShapeDtypeStruct((4, 4, 64, D), low),
            jax.ShapeDtypeStruct((4, 4, 64, D), low),
            jax.ShapeDtypeStruct((WIDE, D), f32),
            jax.ShapeDtypeStruct((16, 512), f32),
        ],
        scratch_shapes=[
            pltpu.VMEM((BLOCK + 8, 512), f32),
            pltpu.VMEM((BLOCK + 8, 512), f32),
            pltpu.VMEM((STATE, WIDE), f32),
            pltpu.VMEM((CONV + 1, 8, 512), f32),
            pltpu.VMEM((2, 8, CHUNK), f32),
            pltpu.VMEM((8, WIDE), f32),
        ],
        compiler_params=pltpu.CompilerParams(
            dimension_semantics=("arbitrary",), vmem_limit_bytes=56 * 1024 * 1024
        ),
        name="ssd_backward",
    )(place, proj, proj, w, both, rows, conv, heads, skip, y, gated, u, kept)


epsilon = 1e-05
BOTH = ("dp", "seq")


def columns_of(a, small):
    rows = a.shape[0]
    z = a[:, :INNER].reshape(rows, 16, WIDE)
    x = a[:, INNER : 2 * INNER].reshape(rows, 16, WIDE)
    bc = jnp.broadcast_to(a[:, None, 2 * INNER : 2 * INNER + 256], (rows, 16, 256))
    dt = a[:, 2 * INNER + 256 :].reshape(rows, 16, OWN)
    blank = lambda n: jnp.zeros((rows, 16, n), a.dtype)
    small = jnp.broadcast_to(small[:, None], (rows, 16, 22))
    return jnp.concatenate([z, dt, blank(61), x, small, blank(42), bc], axis=2).transpose(1, 0, 2)


def padded(a):
    return jnp.concatenate(
        [a[:, :WIDE], jnp.zeros((a.shape[0], 64), a.dtype), a[:, WIDE:]], axis=1
    )


def along_x(a, k):
    return lax.ppermute(a, "seq", [(s, (s // 4) * 4 + (s % 4 + k) % 4) for s in range(16)])


def along_y(a, k):
    return lax.ppermute(a, "seq", [(s, ((s // 4 + k) % 4) * 4 + s % 4) for s in range(16)])


def along_z(a, k):
    return lax.ppermute(a, "dp", [(d, ((d // 2 + k) % 4) * 2 + d % 2) for d in range(8)])


def other_core(a):
    return lax.ppermute(a, "dp", [(d, d ^ 1) for d in range(8)])


def put(buf, piece, *at):
    return lax.dynamic_update_slice(buf, piece, tuple(at) + (0,) * (buf.ndim - len(at)))


def take(a, i):
    return lax.dynamic_index_in_dim(a, i % a.shape[0], 0, False)


def added(a, b):
    return (a.astype(f32) + b.astype(f32)).astype(low)


def scattered_sum(top, bottom):
    me = lax.axis_index("seq")
    x, y = me % 4, me // 4
    total = lambda own, others: sum([o.astype(f32) for o in others], own.astype(f32))
    top = total(top[0], [along_y(top[k], k) for k in (2, 1, 3)]).astype(low)
    bottom = total(bottom[0], [along_x(bottom[k], k) for k in (2, 1, 3)]).astype(low)
    own_top = total(take(top, x), [along_x(take(top, x + k), k) for k in (2, 1, 3)])
    own_bottom = total(take(bottom, y), [along_y(take(bottom, y + k), k) for k in (2, 1, 3)])
    return jnp.concatenate([own_top, own_bottom], axis=0)


def gathered_z(a):
    d = lax.axis_index("dp")
    z, core = d // 2, d % 2
    h = a.shape[0] // 2
    first, last = a[:h], a[h:]
    up_first = along_z(first, 1)
    down_last = along_z(last, 3)
    up_last = along_z(last, 1)
    down_first = along_z(first, 3)
    far_first = along_z(up_first, 1)
    far_last = along_z(down_last, 3)
    mine = put(jnp.zeros((4, 2, h, a.shape[1]), a.dtype), a.reshape(1, 2, h, -1), z)
    for k, p, q in ((3, up_first, up_last), (1, down_first, down_last), (2, far_first, far_last)):
        mine = put(mine, p[None, None], (z + k) % 4, 0)
        mine = put(mine, q[None, None], (z + k) % 4, 1)
    mine = mine.reshape(4, 1, 2 * h, -1)
    other = other_core(mine)
    first = core == 0
    pair = (jnp.where(first, mine, other), jnp.where(first, other, mine))
    return jnp.concatenate(pair, axis=1).reshape(8, 2 * h, -1)


def seq_sum(a):
    a = a + along_x(a, 1) + along_x(a, 3) + along_x(a, 2)
    return a + along_y(a, 1) + along_y(a, 3) + along_y(a, 2)


def block_order(back):
    pairs = [(f, (f % 8) * 16 + f // 8) for f in range(128)]
    return [(b, a) for a, b in pairs] if back else pairs


def local(
    hidden,
    segments,
    pre_gain,
    w_in,
    conv_weight,
    conv_bias,
    dt_bias,
    a_log,
    d_skip,
    gate_gain,
    w_out,
    grad_out,
):
    me = lax.axis_index("seq")
    row = lax.axis_index("dp")
    tokens = hidden[0].astype(f32)
    r0 = lax.rsqrt(jnp.mean(tokens * tokens, axis=-1, keepdims=True) + epsilon)
    hn = (tokens * r0).astype(low)
    both = jnp.concatenate([hn, grad_out[0]], axis=1)
    both = lax.all_gather(both, "seq", axis=0, tiled=True)

    gain_in = pre_gain.astype(f32)[:, None]
    gain_out = gate_gain.astype(f32)[:, None]
    w_in_wide = w_in.astype(f32)
    w_out_wide = w_out.astype(f32)
    small = jnp.concatenate([conv_weight.reshape(-1), conv_bias, segments[0].astype(low)])
    small = jnp.pad(small, (0, 264 - small.shape[0])).reshape(12, 22)
    parts = columns_of((w_in_wide * gain_in).astype(low), small).reshape(16 * 12, PAD)
    parts = lax.all_to_all(parts, "seq", 0, 0, tiled=True)
    segment = parts[:, 448:470].reshape(16, 264)[:, 130:258].astype(f32).reshape(1, 2048)
    before = jnp.concatenate([jnp.full((1, 1), -1.0, f32), segment[:, :-1]], axis=1)
    blocks = lax.ppermute((w_out_wide * gain_out).astype(low), BOTH, block_order(False))
    weights = gathered_z(jnp.concatenate([parts, blocks.reshape(48, PAD)], axis=0))
    w_own = weights[:, :192].reshape(D, PAD)
    w_out_own = weights[:, 192:].reshape(WIDE, D)
    conv_all = weights[:, :192, 448:470].reshape(128, 264)[:, :130].astype(f32)
    conv_all = conv_all.reshape(128, 5, 26).transpose(1, 0, 2).reshape(5, CONV_CH)
    conv = jnp.concatenate(
        [lax.dynamic_slice_in_dim(conv_all, me * WIDE, WIDE, 1), conv_all[:, INNER:]], axis=1
    )
    conv = jnp.concatenate([padded(conv), jnp.zeros((3, 512), f32)], axis=0)
    own = lambda a: lax.dynamic_slice_in_dim(a, me * OWN, OWN, 0)
    tall = lambda a: jnp.broadcast_to(
        jnp.tile(jnp.pad(own(a), (0, 8 - OWN)), GROUP)[:, None], (8 * GROUP, CHUNK)
    )
    heads = jnp.stack([tall(dt_bias), tall(a_log)])
    skip = jnp.repeat(own(d_skip), 64)[None]
    by_chunk = lambda rows: jnp.concatenate(
        rows + [jnp.zeros((8 - len(rows), 2048), f32)], axis=0
    ).reshape(8, 16, CHUNK).transpose(1, 0, 2)

    proj, y, gated, u, kept, partial_out, sums = ssd_forward(
        both, w_own, w_out_own, by_chunk([segment, before]), conv, heads, skip
    )
    total = lax.psum_scatter(partial_out, "seq", scatter_dimension=0, tiled=True)
    sums = seq_sum(sums[:2].reshape(32, 128)).reshape(2, 2048)
    r = lax.rsqrt(sums[0:1] / INNER + epsilon)
    c = r * r * r * (sums[1:2] / INNER)

    place = jnp.stack([me % 4, me // 4])
    d_proj, top, bottom, grad_out_w, small = ssd_backward(
        place, both, w_own, proj, by_chunk([segment, before, r, c]), conv, heads, skip, y, gated, u, kept
    )
    v = scattered_sum(top, bottom)
    grad_in = lax.dot_general(
        both[:, :D], d_proj, (((0,), (0,)), ((), ())), preferred_element_type=f32
    )
    grads = jnp.concatenate(
        [grad_in.reshape(8, 192, PAD), grad_out_w.reshape(8, 48, PAD)], axis=1
    ).astype(low)
    grads, total = lax.optimization_barrier((grads, total))
    grads = lax.psum_scatter(grads.reshape(8 * 240, PAD), "dp", scatter_dimension=0, tiled=True)
    conv_flat = jnp.zeros((5, CONV_CH), f32)
    conv_flat = lax.dynamic_update_slice(conv_flat, small[:5, 256:], (0, INNER))
    conv_flat = lax.dynamic_update_slice(conv_flat, small[:5, :WIDE], (0, me * WIDE))
    conv_flat = conv_flat.reshape(5, 128, 26).transpose(1, 0, 2).reshape(128, 130)
    head_own = jnp.concatenate(
        [small[8:11, 0], small[8:11, 1], small[5, :WIDE].reshape(OWN, 64).sum(axis=1)]
    )
    small = jnp.concatenate([conv_flat, jnp.broadcast_to(head_own[None], (128, 9))], axis=1)
    small = lax.all_to_all(small, BOTH, 0, 0, tiled=True)
    conv_sum = jnp.sum(small[:, :130], axis=0).reshape(5, 26)
    head_sum = jnp.sum(small[:, 130:].reshape(8, 16, 3, OWN), axis=0)
    head_sum = head_sum.transpose(1, 0, 2).reshape(3, HEADS)
    g_parts = lax.all_to_all(grads[:192], "seq", 0, 0, tiled=True).reshape(16, 12, PAD)
    g_out = lax.ppermute(grads[192:].reshape(24, D), BOTH, block_order(True)).astype(f32)
    g_parts = g_parts.astype(f32).transpose(1, 0, 2)
    g_in = jnp.concatenate(
        [
            g_parts[:, :, :WIDE].reshape(12, INNER),
            g_parts[:, :, 256 : 256 + WIDE].reshape(12, INNER),
            jnp.sum(g_parts[:, :, 512:], axis=1),
            g_parts[:, :, WIDE : WIDE + OWN].reshape(12, HEADS),
        ],
        axis=1,
    )
    grad_w_in = gain_in * g_in
    grad_pre_gain = jnp.sum(w_in_wide * g_in, axis=1)
    grad_w_out = gain_out * g_out
    grad_gate_gain = jnp.sum(w_out_wide * g_out, axis=1)
    r_own = lax.dynamic_slice_in_dim(r[0], me * 128, 128, 0)
    block_out = (r_own[:, None] * total.astype(f32) + tokens).astype(low)
    mean = jnp.mean(v * tokens, axis=-1, keepdims=True)
    grad_hidden = (
        grad_out[0].astype(f32) + r0 * v - tokens * (r0 * r0 * r0 * mean)
    ).astype(low)
    return (
        block_out[None],
        grad_hidden[None],
        grad_pre_gain,
        grad_w_in,
        conv_sum[:CONV],
        conv_sum[CONV],
        head_sum[0],
        head_sum[1],
        head_sum[2],
        grad_gate_gain,
        grad_w_out,
    )


def solution(mesh):
    placed = (
        P("dp", "seq", None),
        P("dp", "seq"),
        P(BOTH),
        P(BOTH, None),
        P(None, BOTH),
        P(BOTH),
        P(),
        P(),
        P(),
        P(BOTH),
        P(BOTH, None),
        P("dp", "seq", None),
    )
    return jax.shard_map(
        local,
        mesh=mesh,
        in_specs=placed,
        out_specs=(
            P("dp", "seq", None),
            P("dp", "seq", None),
            P(BOTH),
            P(BOTH, None),
            P(None, BOTH),
            P(BOTH),
            P(),
            P(),
            P(),
            P(BOTH),
            P(BOTH, None),
        ),
        check_vma=False,
    )
```

time: 486 us -> 321 us (0.66)
  waiting for transfers between devices: 276 us -> 116 us
  matrix products: 41.1 us -> 8.24 us
  starting transfers between devices: 37.1 us -> 69.9 us
  blocking collectives: 13.7 us -> 0 us
  other arithmetic: 14.1 us -> 20.5 us
  Pallas kernels: 56.9 us -> 61.9 us
    reduce_scatter x1, waiting for transfers between devices: 83.1 us -> 8.89 us  [local(): lax.psum_scatter(partial_out, 'seq', scatter_dimension=0, tiled=True)]
    reduce_scatter x2 -> x1, waiting for transfers between devices: 59.1 us -> 0.02 us  [local(): lax.psum_scatter(grads.reshape(8 * 240, PAD), 'dp', scatter_dimension=0,...]
    all_gather x3 -> x1, waiting for transfers between devices: 96.1 us -> 44.6 us  [local(): both = lax.all_gather(both, 'seq', axis=0, tiled=True)]
    ppermute x0 -> x25, waiting for transfers between devices: none -> 44.9 us  [the longest x9 32.4 us: along_y(): lax.ppermute(a, 'seq', [(s, (s // 4 + k) % 4 * 4 + s % 4) for s in range(...]
    ppermute x0 -> x25, starting transfers between devices: none -> 42.7 us  [the longest x9 15.1 us: along_x(): lax.ppermute(a, 'seq', [(s, s // 4 * 4 + (s % 4 + k) % 4) for s in range(...]
    dot_general x6 -> x1, matrix products: 41.1 us -> 8.24 us  [local(): lax.dot_general(both[:, :D], d_proj, (((0,), (0,)), ((), ())), preferred_...]
    all_to_all x2 -> x1, waiting for transfers between devices: 18.4 us -> 0.01 us  [local(): small = lax.all_to_all(small, BOTH, 0, 0, tiled=True)]
    all_to_all x1 -> x0, blocking collectives: 13.7 us -> none  [local(): lax.all_to_all(jnp.broadcast_to(sums.reshape(1, 32, 128), (16, 32, 128)),...]
  transfers between devices with their start and end apart: 12 -> 33, of which waited for: 10 -> 19; matrix products, arithmetic and copies ran while one was open for 9% -> 15% of each run, Pallas kernels for 4% -> 13%
where the time goes in v2:
time: 321 us; the launch traced here: 320 us
  waiting for transfers between devices  116 us (36%)
  starting transfers between devices  69.9 us (22%)
  Pallas kernels  61.9 us (19%)
  local copies, waits for them, and re-layouts  28.9 us (9%)
  other arithmetic  20.5 us (6%)
  between operations  14.8 us (5%)
  matrix products  8.24 us (3%)
    all_gather x1, waiting for transfers between devices, local(): both = lax.all_gather(both, 'seq', axis=0, tiled=True)  44.6 us
    pallas_call x1, Pallas kernels, ssd_backward(): pl.pallas_call(backward_kernel, grid=(steps,), in_specs=[pl.BlockSpec(mem...  42.2 us
    ppermute x9, waiting for transfers between devices, along_y(): lax.ppermute(a, 'seq', [(s, (s // 4 + k) % 4 * 4 + s % 4) for s in range(...  32.4 us
    pallas_call x1, Pallas kernels, ssd_forward(): pl.pallas_call(forward_kernel, grid=(steps,), in_specs=[here(2 * D), whol...  19.7 us
    ppermute x9, starting transfers between devices, along_x(): lax.ppermute(a, 'seq', [(s, s // 4 * 4 + (s % 4 + k) % 4) for s in range(...  15.1 us
    ppermute x6, starting transfers between devices, along_z(): lax.ppermute(a, 'dp', [(d, (d // 2 + k) % 4 * 2 + d % 2) for d in range(8)])  14.3 us
    ppermute x9, starting transfers between devices, along_y(): lax.ppermute(a, 'seq', [(s, (s // 4 + k) % 4 * 4 + s % 4) for s in range(...  13.2 us
    all_to_all x1, starting transfers between devices, local(): lax.all_to_all(grads[:192], 'seq', 0, 0, tiled=True).reshape(16, 12, PAD)  10.1 us
  transfers between devices with their start and end apart: 33, of which 19 were waited for; matrix products, arithmetic and copies ran while one was open for 15% of the time, Pallas kernels for 13%

profile of v2, /device:TPU:0, one launch (start us, length us, event | category | flops | bytes accessed | tf_op | source)
XLA Modules:
  0.0 320.1 jit_solution(14969546885673398631)
XLA Ops:
  14.4 7.1 %all-to-all-start = ((bf16[16,12,768]{2,1,0:T(8,128)(2,1)}), bf16[16,12,768]{2,1,0:T(8,128)(2,1)S(1)}, u32[]{:S(2)}, u32[]{:S(2)}) async-start(bf16[16,12,768]{2,1,0:T(8,128)(2,1)} %bitcast.3), calls=%async_computation | async-start | bytes 786432 | tf_op jit(solution)/shard_map/all_to_all | solution.py:590
  22.4 9.8 %all-to-all-done = bf16[16,12,768]{2,1,0:T(8,128)(2,1)S(1)} async-done(((bf16[16,12,768]{2,1,0:T(8,128)(2,1)}), bf16[16,12,768]{2,1,0:T(8,128)(2,1)S(1)}, u32[]{:S(2)}, u32[]{:S(2)}) %all-to-all-start) | async-done | bytes 294944 | tf_op jit(solution)/shard_map/all_to_all | solution.py:590
  32.3 7.2 %collective-permute-start.4 = (bf16[120,768]{1,0:T(8,128)(2,1)S(1)}, bf16[120,768]{1,0:T(8,128)(2,1)S(1)}, u32[]{:S(2)}, u32[]{:S(2)}) collective-permute-start(bf16[120,768]{1,0:T(8,128)(2,1)S(1)} %slice.203), channel_id=1, source_target_pairs={{0,96},{16,112},{32,0},{48,16},{64,32},{80,48},{96,64},{112,80},{1... | collective-permute-start | bytes 552968 | tf_op jit(solution)/shard_map/ppermute | solution.py:499
  39.9 3.2 %collective-permute-start.3 = (bf16[120,768]{1,0:T(8,128)(2,1)S(1)}, bf16[120,768]{1,0:T(8,128)(2,1)S(1)}, u32[]{:S(2)}, u32[]{:S(2)}) collective-permute-start(bf16[120,768]{1,0:T(8,128)(2,1)S(1)} %slice.157), channel_id=1, source_target_pairs={{0,96},{16,112},{32,0},{48,16},{64,32},{80,48},{96,64},{112,80},{1... | collective-permute-start | bytes 552968 | tf_op jit(solution)/shard_map/ppermute | solution.py:499
  44.3 3.7 %collective-permute-start.6 = (bf16[120,768]{1,0:T(8,128)(2,1)S(1)}, bf16[120,768]{1,0:T(8,128)(2,1)S(1)}, u32[]{:S(2)}, u32[]{:S(2)}) collective-permute-start(bf16[120,768]{1,0:T(8,128)(2,1)S(1)} %collective-permute-done.4), channel_id=1, source_target_pairs={{0,96},{16,112},{32,0},{48,16},{64,32},{80,48},{96,64},{112,80},{1... | collective-permute-start | bytes 552968 | tf_op jit(solution)/shard_map/ppermute | solution.py:499
  48.0 3.3 %collective-permute-done.2 = bf16[120,768]{1,0:T(8,128)(2,1)S(1)} collective-permute-done((bf16[120,768]{1,0:T(8,128)(2,1)S(1)}, bf16[120,768]{1,0:T(8,128)(2,1)S(1)}, u32[]{:S(2)}, u32[]{:S(2)}) %collective-permute-start.2) | collective-permute-done | bytes 184352 | tf_op jit(solution)/shard_map/ppermute | solution.py:499
  51.4 3.3 %collective-permute-done.5 = bf16[120,768]{1,0:T(8,128)(2,1)S(1)} collective-permute-done((bf16[120,768]{1,0:T(8,128)(2,1)S(1)}, bf16[120,768]{1,0:T(8,128)(2,1)S(1)}, u32[]{:S(2)}, u32[]{:S(2)}) %collective-permute-start.5) | collective-permute-done | bytes 184352 | tf_op jit(solution)/shard_map/ppermute | solution.py:499
  66.6 44.6 %all-gather.2.cloned.1.call-done.both_ref.cot_ref = bf16[2048,3072]{1,0:T(8,128)(2,1)} async-done(((bf16[128,3072]{1,0:T(8,128)(2,1)}), bf16[2048,3072]{1,0:T(8,128)(2,1)}) %all-gather.2.cloned.1.call-update) | async-done | bytes 12582928 | tf_op jit(solution)/shard_map/all_gather | solution.py:581
  111.2 19.7 %ssd_forward.1 = (bf16[2048,768]{1,0:T(8,128)(2,1)}, f32[2048,192]{1,0:T(8,128)}, bf16[2048,192]{1,0:T(8,128)(2,1)}, f32[2048,192]{1,0:T(8,128)}, f32[16,128,192...) custom-call(bf16[2048,3072]{1,0:T(8,128)(2,1)} %all-gather.2.cloned.1.call-done.both_ref.cot_ref, ...), custom_call_target="tpu_custom_call" | custom-call | tf_op jit(solution)/shard_map/ssd_forward/pallas_call | solution.py:378
  131.8 3.0 collective-permute-start.10
  146.5 2.5 collective-permute-done.11
  149.7 42.2 %ssd_backward.1 = (bf16[2048,768]{1,0:T(8,128)(2,1)}, bf16[4,4,64,1536]{3,2,1,0:T(8,128)(2,1)}, bf16[4,4,64,1536]{3,2,1,0:T(8,128)(2,1)}, f32[192,1536]{1,0:T(8,128)}, f32[16,512]{1,0:T(8,128)}) custom-call(s32[2]{0:T(128)} %pad_add_fusion.place_ref, bf16[2048,768]{1,0:T(8,128)(2,1)} %get-tuple-element.26.proj_ref.before_ref, ...), custom_call_target="tpu_custom_call" | custom-call | tf_op jit(solution)/shard_map/ssd_backward/pallas_call | solution.py:422
  193.5 8.2 %fusion.2 = bf16[1536,768]{1,0:T(8,128)(2,1)S(1)} fusion(bf16[2048,768]{1,0:T(8,128)(2,1)} %get-tuple-element.31, bf16[2048,3072]{1,0:T(8,128)(2,1)} %all-gather.2.cloned.1.call-done.both_ref.cot_ref), kind=kOutput, calls=%fused_computation.2 | convolution fusion | flops 4833017856 | bytes 11796480 | tf_op jit(solution)/shard_map/dot_general | solution.py:626
  203.5 8.9 %reduce-scatter.3.cloned.1.call-done = bf16[128,1536]{1,0:T(8,128)(2,1)} async-done(((bf16[2048,1536]{1,0:T(8,128)(2,1)}), bf16[128,1536]{1,0:T(8,128)(2,1)}) %reduce-scatter.3.cloned.1.call-update) | async-done | bytes 393232 | tf_op jit(solution)/shard_map/reduce_scatter | solution.py:616
  215.3 8.6 %all-to-all-start.2 = ((f32[128,1,139]{2,1,0:T(1,128)}), f32[128,1,139]{2,1,0:T(1,128)}, u32[]{:S(2)}, u32[]{:S(2)}) async-start(f32[128,1,139]{2,1,0:T(1,128)} %copy.96), calls=%async_computation.4 | async-start | bytes 262144 | tf_op jit(solution)/shard_map/all_to_all | solution.py:642
  223.9 3.2 %slice_bitcast_fusion.5 = (bf16[4,64,1536]{2,1,0:T(8,128)(2,1)}, bf16[4,64,1536]{2,1,0:T(8,128)(2,1)}, bf16[4,64,1536]{2,1,0:T(8,128)(2,1)}) fusion(bf16[4,4,64,1536]{3,2,1,0:T(8,128)(2,1)} %get-tuple-element.35), kind=kLoop, calls=%fused_computation.36 | loop fusion | bytes 4718592 | tf_op jit(solution)/shard_map/squeeze | solution.py:522
  233.0 3.0 collective-permute-start.20
  241.7 7.7 %collective-permute-done.14 = bf16[4,64,1536]{2,1,0:T(8,128)(2,1)} collective-permute-done((bf16[4,64,1536]{2,1,0:T(8,128)(2,1)}, bf16[4,64,1536]{2,1,0:T(8,128)(2,1)}, u32[]{:S(2)}, u32[]{:S(2)}) %collective-permute-start.14) | collective-permute-done | bytes 786464 | tf_op jit(solution)/shard_map/ppermute | solution.py:495
  250.2 14.7 %collective-permute-done.16 = bf16[4,64,1536]{2,1,0:T(8,128)(2,1)} collective-permute-done((bf16[4,64,1536]{2,1,0:T(8,128)(2,1)}, bf16[4,64,1536]{2,1,0:T(8,128)(2,1)}, u32[]{:S(2)}, u32[]{:S(2)}) %collective-permute-start.16) | collective-permute-done | bytes 786464 | tf_op jit(solution)/shard_map/ppermute | solution.py:495
  267.2 3.1 collective-permute-start.17
  274.1 2.9 collective-permute-start.23
  279.9 3.7 %collective-permute-done.23 = bf16[64,1536]{1,0:T(8,128)(2,1)S(1)} collective-permute-done((bf16[64,1536]{1,0:T(8,128)(2,1)S(1)}, bf16[64,1536]{1,0:T(8,128)(2,1)S(1)}, u32[]{:S(2)}, u32[]{:S(2)}) %collective-permute-start.23) | collective-permute-done | bytes 196640 | tf_op jit(solution)/shard_map/ppermute | solution.py:495
  290.9 10.1 %all-to-all-start.1 = ((bf16[16,12,768]{2,1,0:T(8,128)(2,1)}), bf16[16,12,768]{2,1,0:T(8,128)(2,1)S(1)}, u32[]{:S(2)}, u32[]{:S(2)}) async-start(bf16[16,12,768]{2,1,0:T(8,128)(2,1)} %all_to_all.22), calls=%async_computation.3 | async-start | bytes 786432 | tf_op jit(solution)/shard_map/all_to_all | solution.py:646
  303.4 7.6 %all-to-all-done.1 = bf16[16,12,768]{2,1,0:T(8,128)(2,1)S(1)} async-done(((bf16[16,12,768]{2,1,0:T(8,128)(2,1)}), bf16[16,12,768]{2,1,0:T(8,128)(2,1)S(1)}, u32[]{:S(2)}, u32[]{:S(2)}) %all-to-all-start.1) | async-done | bytes 294944 | tf_op jit(solution)/shard_map/all_to_all | solution.py:646
  (232 shorter events, 74.0 us)
Async XLA Ops:
  7.2 104.0 %all-gather.2.cloned.1.call-start = ((), (), s32[]{:S(2)}) async-start(), calls=%async_computation.5 | async-start | bytes 13369344 | tf_op jit(solution)/shard_map/all_gather | solution.py:581
  14.4 17.8 %all-to-all-start = ((bf16[16,12,768]{2,1,0:T(8,128)(2,1)}), bf16[16,12,768]{2,1,0:T(8,128)(2,1)S(1)}, u32[]{:S(2)}, u32[]{:S(2)}) async-start(bf16[16,12,768]{2,1,0:T(8,128)(2,1)} %bitcast.3), calls=%async_computation | async-start | bytes 786432 | tf_op jit(solution)/shard_map/all_to_all | solution.py:590
  21.5 190.9 %reduce-scatter.3.cloned.1.call-start = ((), (), s32[]{:S(2)}) async-start(), calls=%async_computation.6 | async-start | bytes 6684672 | tf_op jit(solution)/shard_map/reduce_scatter | solution.py:616
  32.3 12.0 %collective-permute-start.4 = (bf16[120,768]{1,0:T(8,128)(2,1)S(1)}, bf16[120,768]{1,0:T(8,128)(2,1)S(1)}, u32[]{:S(2)}, u32[]{:S(2)}) collective-permute-start(bf16[120,768]{1,0:T(8,128)(2,1)S(1)} %slice.203), channel_id=1, source_target_pairs={{0,96},{16,112},{32,0},{48,16},{64,32},{80,48},{96,64},{112,80},{1... | collective-permute-start | bytes 552968 | tf_op jit(solution)/shard_map/ppermute | solution.py:499
  39.6 8.4 %collective-permute-start.1 = (bf16[120,768]{1,0:T(8,128)(2,1)S(1)}, bf16[120,768]{1,0:T(8,128)(2,1)S(1)}, u32[]{:S(2)}, u32[]{:S(2)}) collective-permute-start(bf16[120,768]{1,0:T(8,128)(2,1)S(1)} %slice.157), channel_id=1, source_target_pairs={{0,32},{16,48},{32,64},{48,80},{64,96},{80,112},{96,0},{112,16},{1... | collective-permute-start | bytes 552968 | tf_op jit(solution)/shard_map/ppermute | solution.py:499
  39.8 11.6 %collective-permute-start.2 = (bf16[120,768]{1,0:T(8,128)(2,1)S(1)}, bf16[120,768]{1,0:T(8,128)(2,1)S(1)}, u32[]{:S(2)}, u32[]{:S(2)}) collective-permute-start(bf16[120,768]{1,0:T(8,128)(2,1)S(1)} %slice.203), channel_id=1, source_target_pairs={{0,32},{16,48},{32,64},{48,80},{64,96},{80,112},{96,0},{112,16},{1... | collective-permute-start | bytes 552968 | tf_op jit(solution)/shard_map/ppermute | solution.py:499
  39.9 11.5 %collective-permute-start.3 = (bf16[120,768]{1,0:T(8,128)(2,1)S(1)}, bf16[120,768]{1,0:T(8,128)(2,1)S(1)}, u32[]{:S(2)}, u32[]{:S(2)}) collective-permute-start(bf16[120,768]{1,0:T(8,128)(2,1)S(1)} %slice.157), channel_id=1, source_target_pairs={{0,96},{16,112},{32,0},{48,16},{64,32},{80,48},{96,64},{112,80},{1... | collective-permute-start | bytes 552968 | tf_op jit(solution)/shard_map/ppermute | solution.py:499
  44.3 10.5 %collective-permute-start.6 = (bf16[120,768]{1,0:T(8,128)(2,1)S(1)}, bf16[120,768]{1,0:T(8,128)(2,1)S(1)}, u32[]{:S(2)}, u32[]{:S(2)}) collective-permute-start(bf16[120,768]{1,0:T(8,128)(2,1)S(1)} %collective-permute-done.4), channel_id=1, source_target_pairs={{0,96},{16,112},{32,0},{48,16},{64,32},{80,48},{96,64},{112,80},{1... | collective-permute-start | bytes 552968 | tf_op jit(solution)/shard_map/ppermute | solution.py:499
  130.9 156.5 %reduce-scatter.5.cloned.1.call-start = ((), (), s32[]{:S(2)}) async-start(), calls=%async_computation.7 | async-start | bytes 3317760 | tf_op jit(solution)/shard_map/reduce_scatter | solution.py:633
  215.3 21.8 %all-to-all-start.2 = ((f32[128,1,139]{2,1,0:T(1,128)}), f32[128,1,139]{2,1,0:T(1,128)}, u32[]{:S(2)}, u32[]{:S(2)}) async-start(f32[128,1,139]{2,1,0:T(1,128)} %copy.96), calls=%async_computation.4 | async-start | bytes 262144 | tf_op jit(solution)/shard_map/all_to_all | solution.py:642
  227.1 22.3 %collective-permute-start.14 = (bf16[4,64,1536]{2,1,0:T(8,128)(2,1)}, bf16[4,64,1536]{2,1,0:T(8,128)(2,1)}, u32[]{:S(2)}, u32[]{:S(2)}) collective-permute-start(bf16[4,64,1536]{2,1,0:T(8,128)(2,1)} %get-tuple-element.41), channel_id=1, source_target_pairs={{0,8},{1,9},{2,10},{3,11},{4,12},{5,13},{6,14},{7,15},{8,0},{9,1},... | collective-permute-start | bytes 2359304 | tf_op jit(solution)/shard_map/ppermute | solution.py:495
  229.5 35.4 %collective-permute-start.16 = (bf16[4,64,1536]{2,1,0:T(8,128)(2,1)}, bf16[4,64,1536]{2,1,0:T(8,128)(2,1)}, u32[]{:S(2)}, u32[]{:S(2)}) collective-permute-start(bf16[4,64,1536]{2,1,0:T(8,128)(2,1)} %get-tuple-element.42), channel_id=1, source_target_pairs={{0,12},{1,13},{2,14},{3,15},{4,0},{5,1},{6,2},{7,3},{8,4},{9,5},{1... | collective-permute-start | bytes 2359304 | tf_op jit(solution)/shard_map/ppermute | solution.py:495
  230.6 34.2 %collective-permute-start.15 = (bf16[4,64,1536]{2,1,0:T(8,128)(2,1)}, bf16[4,64,1536]{2,1,0:T(8,128)(2,1)}, u32[]{:S(2)}, u32[]{:S(2)}) collective-permute-start(bf16[4,64,1536]{2,1,0:T(8,128)(2,1)} %get-tuple-element.43), channel_id=1, source_target_pairs={{0,4},{1,5},{2,6},{3,7},{4,8},{5,9},{6,10},{7,11},{8,12},{9,13},{1... | collective-permute-start | bytes 2359304 | tf_op jit(solution)/shard_map/ppermute | solution.py:495
  233.0 38.4 %collective-permute-start.20 = (bf16[4,64,1536]{2,1,0:T(8,128)(2,1)}, bf16[4,64,1536]{2,1,0:T(8,128)(2,1)}, u32[]{:S(2)}, u32[]{:S(2)}) collective-permute-start(bf16[4,64,1536]{2,1,0:T(8,128)(2,1)} %get-tuple-element.44), channel_id=1, source_target_pairs={{0,2},{1,3},{2,0},{3,1},{4,6},{5,7},{6,4},{7,5},{8,10},{9,11},{10,... | collective-permute-start | bytes 2359304 | tf_op jit(solution)/shard_map/ppermute | solution.py:491
  235.9 36.3 %collective-permute-start.22 = (bf16[4,64,1536]{2,1,0:T(8,128)(2,1)}, bf16[4,64,1536]{2,1,0:T(8,128)(2,1)}, u32[]{:S(2)}, u32[]{:S(2)}) collective-permute-start(bf16[4,64,1536]{2,1,0:T(8,128)(2,1)} %get-tuple-element.45), channel_id=1, source_target_pairs={{0,3},{1,0},{2,1},{3,2},{4,7},{5,4},{6,5},{7,6},{8,11},{9,8},{10,9... | collective-permute-start | bytes 2359304 | tf_op jit(solution)/shard_map/ppermute | solution.py:491
  249.4 22.9 %collective-permute-start.21 = (bf16[4,64,1536]{2,1,0:T(8,128)(2,1)}, bf16[4,64,1536]{2,1,0:T(8,128)(2,1)S(1)}, u32[]{:S(2)}, u32[]{:S(2)}) collective-permute-start(bf16[4,64,1536]{2,1,0:T(8,128)(2,1)} %get-tuple-element.46), channel_id=1, source_target_pairs={{0,1},{1,2},{2,3},{3,0},{4,5},{5,6},{6,7},{7,4},{8,9},{9,10},{10,1... | collective-permute-start | bytes 2359304 | tf_op jit(solution)/shard_map/ppermute | solution.py:491
  267.2 11.1 %collective-permute-start.17 = (bf16[64,1536]{1,0:T(8,128)(2,1)S(1)}, bf16[64,1536]{1,0:T(8,128)(2,1)S(1)}, u32[]{:S(2)}, u32[]{:S(2)}) collective-permute-start(bf16[64,1536]{1,0:T(8,128)(2,1)S(1)} %get-tuple-element.51), channel_id=1, source_target_pairs={{0,2},{1,3},{2,0},{3,1},{4,6},{5,7},{6,4},{7,5},{8,10},{9,11},{10,... | collective-permute-start | bytes 589832 | tf_op jit(solution)/shard_map/ppermute | solution.py:491
  270.2 9.5 %collective-permute-start.19 = (bf16[64,1536]{1,0:T(8,128)(2,1)S(1)}, bf16[64,1536]{1,0:T(8,128)(2,1)S(1)}, u32[]{:S(2)}, u32[]{:S(2)}) collective-permute-start(bf16[64,1536]{1,0:T(8,128)(2,1)S(1)} %get-tuple-element.52), channel_id=1, source_target_pairs={{0,3},{1,0},{2,1},{3,2},{4,7},{5,4},{6,5},{7,6},{8,11},{9,8},{10,9... | collective-permute-start | bytes 589832 | tf_op jit(solution)/shard_map/ppermute | solution.py:491
  271.4 8.4 %collective-permute-start.18 = (bf16[64,1536]{1,0:T(8,128)(2,1)S(1)}, bf16[64,1536]{1,0:T(8,128)(2,1)S(1)}, u32[]{:S(2)}, u32[]{:S(2)}) collective-permute-start(bf16[64,1536]{1,0:T(8,128)(2,1)S(1)} %get-tuple-element.53), channel_id=1, source_target_pairs={{0,1},{1,2},{2,3},{3,0},{4,5},{5,6},{6,7},{7,4},{8,9},{9,10},{10,1... | collective-permute-start | bytes 589832 | tf_op jit(solution)/shard_map/ppermute | solution.py:491
  274.1 9.4 %collective-permute-start.23 = (bf16[64,1536]{1,0:T(8,128)(2,1)S(1)}, bf16[64,1536]{1,0:T(8,128)(2,1)S(1)}, u32[]{:S(2)}, u32[]{:S(2)}) collective-permute-start(bf16[64,1536]{1,0:T(8,128)(2,1)S(1)} %get-tuple-element.54), channel_id=1, source_target_pairs={{0,8},{1,9},{2,10},{3,11},{4,12},{5,13},{6,14},{7,15},{8,0},{9,1},... | collective-permute-start | bytes 589832 | tf_op jit(solution)/shard_map/ppermute | solution.py:495
  277.1 8.8 %collective-permute-start.25 = (bf16[64,1536]{1,0:T(8,128)(2,1)S(1)}, bf16[64,1536]{1,0:T(8,128)(2,1)S(1)}, u32[]{:S(2)}, u32[]{:S(2)}) collective-permute-start(bf16[64,1536]{1,0:T(8,128)(2,1)S(1)} %get-tuple-element.55), channel_id=1, source_target_pairs={{0,12},{1,13},{2,14},{3,15},{4,0},{5,1},{6,2},{7,3},{8,4},{9,5},{1... | collective-permute-start | bytes 589832 | tf_op jit(solution)/shard_map/ppermute | solution.py:495
  278.3 8.0 %collective-permute-start.24 = (bf16[64,1536]{1,0:T(8,128)(2,1)S(1)}, bf16[64,1536]{1,0:T(8,128)(2,1)S(1)}, u32[]{:S(2)}, u32[]{:S(2)}) collective-permute-start(bf16[64,1536]{1,0:T(8,128)(2,1)S(1)} %get-tuple-element.56), channel_id=1, source_target_pairs={{0,4},{1,5},{2,6},{3,7},{4,8},{5,9},{6,10},{7,11},{8,12},{9,13},{1... | collective-permute-start | bytes 589832 | tf_op jit(solution)/shard_map/ppermute | solution.py:495
  288.4 13.6 %collective-permute-start.26 = (bf16[24,1536]{1,0:T(8,128)(2,1)S(1)}, bf16[24,1536]{1,0:T(8,128)(2,1)S(1)}, u32[]{:S(2)}, u32[]{:S(2)}) collective-permute-start(bf16[24,1536]{1,0:T(8,128)(2,1)S(1)} %reshape.325), channel_id=1, source_target_pairs={{0,0},{16,1},{32,2},{48,3},{64,4},{80,5},{96,6},{112,7},{1,8},{17,... | collective-permute-start | bytes 221192 | tf_op jit(solution)/shard_map/ppermute | solution.py:647
  290.9 20.1 %all-to-all-start.1 = ((bf16[16,12,768]{2,1,0:T(8,128)(2,1)}), bf16[16,12,768]{2,1,0:T(8,128)(2,1)S(1)}, u32[]{:S(2)}, u32[]{:S(2)}) async-start(bf16[16,12,768]{2,1,0:T(8,128)(2,1)} %all_to_all.22), calls=%async_computation.3 | async-start | bytes 786432 | tf_op jit(solution)/shard_map/all_to_all | solution.py:646
  (26 other events, 163.6 us)
Sparse Core Ops, SparseCore 0:
  12.2 98.8 all-gather.1
  131.0 81.3 reduce-scatter.2
  214.8 36.0 reduce-scatter.4

commit v3 on v2

--- a/solution.py
+++ b/solution.py
@@ -182,7 +182,7 @@
     proj_ref,
     before_ref,
     w_ref,
-    cot_ref,
+    both_ref,
     rows_ref,
     conv_ref,
     head_ref,
@@ -191,17 +191,25 @@
     gated_ref,
     u_ref,
     kept_ref,
-    d_proj_ref,
-    top_ref,
-    bottom_ref,
-    out_grad_ref,
-    sums_ref,
+    top_0,
+    top_1,
+    top_2,
+    top_3,
+    bottom_0,
+    bottom_1,
+    bottom_2,
+    bottom_3,
+    grads_ref,
     ext_ref,
     later_ref,
     state_ref,
     conv_grad_ref,
     head_grad_ref,
     skip_grad_ref,
+    d_proj_ref,
+    given_ref,
+    total_ref,
+    sums_ref,
 ):
     step_id = pl.program_id(0)
     count = pl.num_programs(0)
@@ -213,7 +221,7 @@
         conv_grad_ref[...] = jnp.zeros_like(conv_grad_ref)
         head_grad_ref[...] = jnp.zeros_like(head_grad_ref)
         skip_grad_ref[...] = jnp.zeros_like(skip_grad_ref)
-        out_grad_ref[...] = jnp.zeros_like(out_grad_ref)
+        total_ref[...] = jnp.zeros_like(total_ref)
 
     @pl.when(step_id > 0)
     def _():
@@ -245,7 +253,10 @@
     dz = d_gated * y * (z_sig * (1.0 + z * (1.0 - z_sig)))
     dy_low = dy.astype(low)
     normed = (gated_ref[...].astype(f32) * r_col).astype(low)
-    out_grad_ref[...] += mm(normed, cot_ref[...], TN)
+    out_grad = mm(normed, both_ref[:, D : 2 * D], TN)
+    for d in range(8):
+        total_ref[d, 192:216] += out_grad[24 * d : 24 * d + 24, 0:PAD]
+        total_ref[d, 216:240] += out_grad[24 * d : 24 * d + 24, PAD:D]
 
     t = lax.broadcasted_iota(jnp.int32, (CHUNK, CHUNK), 0)
     s = lax.broadcasted_iota(jnp.int32, (CHUNK, CHUNK), 1)
@@ -350,24 +361,43 @@
     ).astype(low)
     d_proj_ref[:, 256:PAD] = d_conv_in.astype(low)
 
+    in_grad = mm(both_ref[:, 0:D], d_proj_ref[...], TN)
+    for d in range(8):
+        total_ref[d, 0:192] += in_grad[192 * d : 192 * d + 192]
+
+    given_ref[...] = mm(d_proj_ref[...], w_ref[...], NT).astype(low)
     row = count - 1 - step_id
-    my_x, my_y = place_ref[0], place_ref[1]
-    up = lax.rem(row - my_y + 4, 4)
-    for j in range(GROUP):
-        given = mm(d_proj_ref[CHUNK * j : CHUNK * (j + 1), :], w_ref[...], NT).astype(low)
-        top_ref[up, j] = given[:64]
-        bottom_ref[lax.rem(j - my_x + 4, 4), row] = given[64:]
+    up = lax.rem(row - place_ref[1] + 4, 4)
+    for k, ref in enumerate((top_0, top_1, top_2, top_3)):
+
+        @pl.when(up == k)
+        def _():
+            for j in range(GROUP):
+                ref[j] = given_ref[CHUNK * j : CHUNK * j + 64, :]
+
+    for k, ref in enumerate((bottom_0, bottom_1, bottom_2, bottom_3)):
+        for j in range(GROUP):
+
+            @pl.when(lax.rem(j - place_ref[0] + 4, 4) == k)
+            def _():
+                ref[row] = given_ref[CHUNK * j + 64 : CHUNK * (j + 1), :]
 
     @pl.when(step_id == count - 1)
     def _():
-        sums_ref[...] = jnp.zeros_like(sums_ref)
-        for k in range(CONV + 1):
-            sums_ref[k : k + 1, :] = jnp.sum(conv_grad_ref[k], axis=0, keepdims=True)
-        sums_ref[5:6, 0:WIDE] = jnp.sum(skip_grad_ref[...], axis=0, keepdims=True)
-        place = lax.broadcasted_iota(jnp.int32, (8, CHUNK), 1)
+        place = lax.broadcasted_iota(jnp.int32, (8, 256), 1)
         bias = jnp.sum(head_grad_ref[0], axis=1, keepdims=True)
         rate = jnp.sum(head_grad_ref[1], axis=1, keepdims=True)
-        sums_ref[8:16, 0:CHUNK] = jnp.where(place == 0, bias, jnp.where(place == 1, rate, 0.0))
+        sums_ref[:, 512:PAD] = jnp.where(place == 0, bias, jnp.where(place == 1, rate, 0.0))
+        for k in range(CONV + 1):
+            sums_ref[k : k + 1, 0:512] = jnp.sum(conv_grad_ref[k], axis=0, keepdims=True)
+        sums_ref[5:8, 0:512] = jnp.zeros((3, 512), f32)
+        sums_ref[5:6, 0:WIDE] = jnp.sum(skip_grad_ref[...], axis=0, keepdims=True)
+        sums = sums_ref[...]
+        high = sums.astype(low).astype(f32)
+        tail = jnp.concatenate([high, sums - high], axis=0).astype(low)
+        for d in range(8):
+            grads_ref[d, 0:240] = total_ref[d].astype(low)
+            grads_ref[d, 240:256] = tail
 
 
 def ssd_forward(both, w, w_out, rows, conv, heads, skip):
@@ -427,7 +457,7 @@
             here(PAD),
             pl.BlockSpec((16, PAD), lambda i: (jnp.maximum(back(i) * (BLOCK // 16) - 1, 0), 0)),
             whole((D, PAD)),
-            pl.BlockSpec((BLOCK, D), lambda i: (back(i), 1)),
+            here(2 * D),
             pl.BlockSpec((GROUP, 8, CHUNK), lambda i: (back(i), 0, 0)),
             whole((8, 512)),
             whole((2, 8 * GROUP, CHUNK)),
@@ -438,18 +468,12 @@
             pl.BlockSpec((GROUP, STATE, WIDE), lambda i: (back(i), 0, 0)),
         ],
         out_specs=[
-            here(PAD),
-            whole((4, 4, 64, D)),
-            whole((4, 4, 64, D)),
-            whole((WIDE, D)),
-            whole((16, 512)),
+            *[whole((4, 64, D)) for _ in range(8)],
+            whole((8, 256, PAD)),
         ],
         out_shape=[
-            jax.ShapeDtypeStruct((length, PAD), low),
-            jax.ShapeDtypeStruct((4, 4, 64, D), low),
-            jax.ShapeDtypeStruct((4, 4, 64, D), low),
-            jax.ShapeDtypeStruct((WIDE, D), f32),
-            jax.ShapeDtypeStruct((16, 512), f32),
+            *[jax.ShapeDtypeStruct((4, 64, D), low) for _ in range(8)],
+            jax.ShapeDtypeStruct((8, 256, PAD), low),
         ],
         scratch_shapes=[
             pltpu.VMEM((BLOCK + 8, 512), f32),
@@ -458,6 +482,10 @@
             pltpu.VMEM((CONV + 1, 8, 512), f32),
             pltpu.VMEM((2, 8, CHUNK), f32),
             pltpu.VMEM((8, WIDE), f32),
+            pltpu.VMEM((BLOCK, PAD), low),
+            pltpu.VMEM((BLOCK, D), low),
+            pltpu.VMEM((8, 240, PAD), f32),
+            pltpu.VMEM((8, PAD), f32),
         ],
         compiler_params=pltpu.CompilerParams(
             dimension_semantics=("arbitrary",), vmem_limit_bytes=56 * 1024 * 1024
@@ -515,15 +543,30 @@
     return (a.astype(f32) + b.astype(f32)).astype(low)
 
 
+def ring_sum(block, along, wait):
+    h = block[2].shape[0] // 2
+    from_up, from_down = wait((along(block[2][:h], 1), along(block[2][h:], 3)))
+    up = jnp.concatenate([added(block[1][:h], from_up), block[1][h:]], axis=0)
+    down = jnp.concatenate([block[3][:h], added(block[3][h:], from_down)], axis=0)
+    up, down = along(up, 1), along(down, 3)
+    return block[0].astype(f32) + up.astype(f32) + down.astype(f32)
+
+
 def scattered_sum(top, bottom):
     me = lax.axis_index("seq")
     x, y = me % 4, me // 4
-    total = lambda own, others: sum([o.astype(f32) for o in others], own.astype(f32))
-    top = total(top[0], [along_y(top[k], k) for k in (2, 1, 3)]).astype(low)
-    bottom = total(bottom[0], [along_x(bottom[k], k) for k in (2, 1, 3)]).astype(low)
+    total = lambda own, sent: sum([s.astype(f32) for s in sent], own.astype(f32))
+    came = []
+
+    def wait(pieces):
+        came.extend(pieces)
+        return pieces
+
+    top = ring_sum(top, along_y, wait).astype(low)
+    bottom = ring_sum(bottom, along_x, wait).astype(low)
     own_top = total(take(top, x), [along_x(take(top, x + k), k) for k in (2, 1, 3)])
     own_bottom = total(take(bottom, y), [along_y(take(bottom, y + k), k) for k in (2, 1, 3)])
-    return jnp.concatenate([own_top, own_bottom], axis=0)
+    return jnp.concatenate([own_top, own_bottom], axis=0), came
 
 
 def gathered_z(a):
@@ -619,32 +662,37 @@
     c = r * r * r * (sums[1:2] / INNER)
 
     place = jnp.stack([me % 4, me // 4])
-    d_proj, top, bottom, grad_out_w, small = ssd_backward(
+    *pieces, grads = ssd_backward(
         place, both, w_own, proj, by_chunk([segment, before, r, c]), conv, heads, skip, y, gated, u, kept
     )
-    v = scattered_sum(top, bottom)
-    grad_in = lax.dot_general(
-        both[:, :D], d_proj, (((0,), (0,)), ((), ())), preferred_element_type=f32
-    )
-    grads = jnp.concatenate(
-        [grad_in.reshape(8, 192, PAD), grad_out_w.reshape(8, 48, PAD)], axis=1
-    ).astype(low)
-    grads, total = lax.optimization_barrier((grads, total))
-    grads = lax.psum_scatter(grads.reshape(8 * 240, PAD), "dp", scatter_dimension=0, tiled=True)
-    conv_flat = jnp.zeros((5, CONV_CH), f32)
-    conv_flat = lax.dynamic_update_slice(conv_flat, small[:5, 256:], (0, INNER))
-    conv_flat = lax.dynamic_update_slice(conv_flat, small[:5, :WIDE], (0, me * WIDE))
-    conv_flat = conv_flat.reshape(5, 128, 26).transpose(1, 0, 2).reshape(128, 130)
-    head_own = jnp.concatenate(
-        [small[8:11, 0], small[8:11, 1], small[5, :WIDE].reshape(OWN, 64).sum(axis=1)]
-    )
-    small = jnp.concatenate([conv_flat, jnp.broadcast_to(head_own[None], (128, 9))], axis=1)
-    small = lax.all_to_all(small, BOTH, 0, 0, tiled=True)
-    conv_sum = jnp.sum(small[:, :130], axis=0).reshape(5, 26)
-    head_sum = jnp.sum(small[:, 130:].reshape(8, 16, 3, OWN), axis=0)
-    head_sum = head_sum.transpose(1, 0, 2).reshape(3, HEADS)
-    g_parts = lax.all_to_all(grads[:192], "seq", 0, 0, tiled=True).reshape(16, 12, PAD)
-    g_out = lax.ppermute(grads[192:].reshape(24, D), BOTH, block_order(True)).astype(f32)
+    v, came = scattered_sum(pieces[:4], pieces[4:])
+    grads, total, came = lax.optimization_barrier((grads, total, came))
+    grads = lax.psum_scatter(
+        grads.reshape(8 * 256, PAD), "dp", scatter_dimension=0, tiled=True
+    ).astype(f32)
+    small = (grads[240:248] + grads[248:256]).astype(low)
+    grads = grads[:240].astype(low)
+    g_parts = jnp.concatenate(
+        [grads[:192].reshape(16, 12, PAD), jnp.broadcast_to(small[None], (16, 8, PAD))], axis=1
+    )
+    g_parts = lax.all_to_all(g_parts, "seq", 0, 0)
+    small = g_parts[:, 12:].astype(f32)
+    g_parts = g_parts[:, :12]
+    g_out = lax.ppermute(grads[192:], BOTH, block_order(True)).astype(f32)
+    g_out = jnp.concatenate([g_out[:24], g_out[24:]], axis=1)
+    conv_sum = jnp.concatenate(
+        [
+            small[:, : CONV + 1, :WIDE].transpose(1, 0, 2).reshape(CONV + 1, INNER),
+            jnp.sum(small[:, : CONV + 1, 256:512], axis=0),
+        ],
+        axis=1,
+    )
+    conv_sum = lax.dynamic_slice_in_dim(conv_sum, 26 * (16 * row + me), 26, 1)
+    head_sum = (
+        small[:, :OWN, 512].reshape(HEADS),
+        small[:, :OWN, 513].reshape(HEADS),
+        small[:, 5, :WIDE].reshape(HEADS, 64).sum(axis=1),
+    )
     g_parts = g_parts.astype(f32).transpose(1, 0, 2)
     g_in = jnp.concatenate(
         [

time: 321 us -> 298 us (0.928)
  starting transfers between devices: 69.9 us -> 57.8 us
  local copies, waits for them, and re-layouts: 28.9 us -> 20 us
  matrix products: 8.24 us -> 0 us
  waiting for transfers between devices: 116 us -> 121 us
    ppermute x9 -> x10, waiting for transfers between devices: 4.76 us -> 25.8 us  [along_x(): lax.ppermute(a, 'seq', [(s, s // 4 * 4 + (s % 4 + k) % 4) for s in range(...]
    ppermute x9 -> x10, waiting for transfers between devices: 32.4 us -> 19.5 us  [along_y(): lax.ppermute(a, 'seq', [(s, (s // 4 + k) % 4 * 4 + s % 4) for s in range(...]
    all_to_all x2 -> x1, starting transfers between devices: 18.6 us -> 8.88 us  [local(): g_parts = lax.all_to_all(g_parts, 'seq', 0, 0)]
    dot_general x1 -> x0, matrix products: 8.24 us -> none  [local(): lax.dot_general(both[:, :D], d_proj, (((0,), (0,)), ((), ())), preferred_...]
    reduce_scatter x1, waiting for transfers between devices: 8.89 us -> 0.77 us  [local(): lax.psum_scatter(partial_out, 'seq', scatter_dimension=0, tiled=True)]
    squeeze x5 -> x1, local copies, waits for them, and re-layouts: 6.47 us -> 0.52 us  [local(): conv_sum[CONV]]
    ppermute x9 -> x10, starting transfers between devices: 15.1 us -> 13 us  [along_x(): lax.ppermute(a, 'seq', [(s, s // 4 * 4 + (s % 4 + k) % 4) for s in range(...]
    all_to_all x2 -> x1, waiting for transfers between devices: 7.64 us -> 9.6 us  [local(): g_parts = lax.all_to_all(g_parts, 'seq', 0, 0)]
  transfers between devices with their start and end apart: 33 -> 34, of which waited for: 19 -> 23; matrix products, arithmetic and copies ran while one was open for 15% -> 9% of each run, Pallas kernels for 13% -> 15%
where the time goes in v3:
time: 298 us; the launch traced here: 297 us
  waiting for transfers between devices  121 us (41%)
  Pallas kernels  64.7 us (22%)
  starting transfers between devices  57.8 us (19%)
  local copies, waits for them, and re-layouts  20 us (7%)
  other arithmetic  19.3 us (6%)
  between operations  15 us (5%)
    all_gather x1, waiting for transfers between devices, local(): both = lax.all_gather(both, 'seq', axis=0, tiled=True)  47.4 us
    pallas_call x1, Pallas kernels, ssd_backward(): pl.pallas_call(backward_kernel, grid=(steps,), in_specs=[pl.BlockSpec(mem...  44.8 us
    ppermute x10, waiting for transfers between devices, along_x(): lax.ppermute(a, 'seq', [(s, s // 4 * 4 + (s % 4 + k) % 4) for s in range(...  25.8 us
    pallas_call x1, Pallas kernels, ssd_forward(): pl.pallas_call(forward_kernel, grid=(steps,), in_specs=[here(2 * D), whol...  19.8 us
    ppermute x10, waiting for transfers between devices, along_y(): lax.ppermute(a, 'seq', [(s, (s // 4 + k) % 4 * 4 + s % 4) for s in range(...  19.5 us
    ppermute x6, starting transfers between devices, along_z(): lax.ppermute(a, 'dp', [(d, (d // 2 + k) % 4 * 2 + d % 2) for d in range(8)])  14.3 us
    ppermute x10, starting transfers between devices, along_y(): lax.ppermute(a, 'seq', [(s, (s // 4 + k) % 4 * 4 + s % 4) for s in range(...  13 us
    ppermute x10, starting transfers between devices, along_x(): lax.ppermute(a, 'seq', [(s, s // 4 * 4 + (s % 4 + k) % 4) for s in range(...  13 us
  transfers between devices with their start and end apart: 34, of which 23 were waited for; matrix products, arithmetic and copies ran while one was open for 9% of the time, Pallas kernels for 15%

profile of v3, /device:TPU:0, one launch (start us, length us, event | category | flops | bytes accessed | tf_op | source)
XLA Modules:
  0.0 297.5 jit_solution(8515983060422360990)
XLA Ops:
  14.4 7.1 %all-to-all-start = ((bf16[16,12,768]{2,1,0:T(8,128)(2,1)}), bf16[16,12,768]{2,1,0:T(8,128)(2,1)S(1)}, u32[]{:S(2)}, u32[]{:S(2)}) async-start(bf16[16,12,768]{2,1,0:T(8,128)(2,1)} %bitcast.3), calls=%async_computation | async-start | bytes 786432 | tf_op jit(solution)/shard_map/all_to_all | solution.py:633
  22.4 9.8 %all-to-all-done = bf16[16,12,768]{2,1,0:T(8,128)(2,1)S(1)} async-done(((bf16[16,12,768]{2,1,0:T(8,128)(2,1)}), bf16[16,12,768]{2,1,0:T(8,128)(2,1)S(1)}, u32[]{:S(2)}, u32[]{:S(2)}) %all-to-all-start) | async-done | bytes 294944 | tf_op jit(solution)/shard_map/all_to_all | solution.py:633
  32.3 7.2 %collective-permute-start.4 = (bf16[120,768]{1,0:T(8,128)(2,1)S(1)}, bf16[120,768]{1,0:T(8,128)(2,1)S(1)}, u32[]{:S(2)}, u32[]{:S(2)}) collective-permute-start(bf16[120,768]{1,0:T(8,128)(2,1)S(1)} %slice.207), channel_id=1, source_target_pairs={{0,96},{16,112},{32,0},{48,16},{64,32},{80,48},{96,64},{112,80},{1... | collective-permute-start | bytes 552968 | tf_op jit(solution)/shard_map/ppermute | solution.py:527
  39.9 3.2 %collective-permute-start.3 = (bf16[120,768]{1,0:T(8,128)(2,1)S(1)}, bf16[120,768]{1,0:T(8,128)(2,1)S(1)}, u32[]{:S(2)}, u32[]{:S(2)}) collective-permute-start(bf16[120,768]{1,0:T(8,128)(2,1)S(1)} %slice.158), channel_id=1, source_target_pairs={{0,96},{16,112},{32,0},{48,16},{64,32},{80,48},{96,64},{112,80},{1... | collective-permute-start | bytes 552968 | tf_op jit(solution)/shard_map/ppermute | solution.py:527
  44.3 3.7 %collective-permute-start.6 = (bf16[120,768]{1,0:T(8,128)(2,1)S(1)}, bf16[120,768]{1,0:T(8,128)(2,1)S(1)}, u32[]{:S(2)}, u32[]{:S(2)}) collective-permute-start(bf16[120,768]{1,0:T(8,128)(2,1)S(1)} %collective-permute-done.4), channel_id=1, source_target_pairs={{0,96},{16,112},{32,0},{48,16},{64,32},{80,48},{96,64},{112,80},{1... | collective-permute-start | bytes 552968 | tf_op jit(solution)/shard_map/ppermute | solution.py:527
  48.0 3.3 %collective-permute-done.2 = bf16[120,768]{1,0:T(8,128)(2,1)S(1)} collective-permute-done((bf16[120,768]{1,0:T(8,128)(2,1)S(1)}, bf16[120,768]{1,0:T(8,128)(2,1)S(1)}, u32[]{:S(2)}, u32[]{:S(2)}) %collective-permute-start.2) | collective-permute-done | bytes 184352 | tf_op jit(solution)/shard_map/ppermute | solution.py:527
  51.4 3.3 %collective-permute-done.5 = bf16[120,768]{1,0:T(8,128)(2,1)S(1)} collective-permute-done((bf16[120,768]{1,0:T(8,128)(2,1)S(1)}, bf16[120,768]{1,0:T(8,128)(2,1)S(1)}, u32[]{:S(2)}, u32[]{:S(2)}) %collective-permute-start.5) | collective-permute-done | bytes 184352 | tf_op jit(solution)/shard_map/ppermute | solution.py:527
  63.7 47.4 %all-gather.2.cloned.1.call-done.both_ref = bf16[2048,3072]{1,0:T(8,128)(2,1)} async-done(((bf16[128,3072]{1,0:T(8,128)(2,1)}), bf16[2048,3072]{1,0:T(8,128)(2,1)}) %all-gather.2.cloned.1.call-update) | async-done | bytes 12582928 | tf_op jit(solution)/shard_map/all_gather | solution.py:624
  111.1 19.8 %ssd_forward.1 = (bf16[2048,768]{1,0:T(8,128)(2,1)}, f32[2048,192]{1,0:T(8,128)}, bf16[2048,192]{1,0:T(8,128)(2,1)}, f32[2048,192]{1,0:T(8,128)}, f32[16,128,192...) custom-call(bf16[2048,3072]{1,0:T(8,128)(2,1)} %all-gather.2.cloned.1.call-done.both_ref, ...), custom_call_target="tpu_custom_call" | custom-call | tf_op jit(solution)/shard_map/ssd_forward/pallas_call | solution.py:408
  131.9 3.0 collective-permute-start.10
  138.6 2.4 collective-permute-done.8
  146.5 2.5 collective-permute-done.11
  149.8 44.8 %ssd_backward.1 = (bf16[4,64,1536]{2,1,0:T(8,128)(2,1)}, bf16[4,64,1536]{2,1,0:T(8,128)(2,1)}, bf16[4,64,1536]{2,1,0:T(8,128)(2,1)}, bf16[4,64,1536]{2,1,0:T(8,1...) custom-call(s32[2]{0:T(128)} %pad_add_fusion.place_ref, ...), custom_call_target="tpu_custom_call" | custom-call | tf_op jit(solution)/shard_map/ssd_backward/pallas_call | solution.py:452
  200.1 7.1 %collective-permute-done.15 = bf16[2,64,1536]{2,1,0:T(8,128)(2,1)} collective-permute-done((bf16[2,64,1536]{2,1,0:T(8,128)(2,1)S(1)}, bf16[2,64,1536]{2,1,0:T(8,128)(2,1)}, u32[]{:S(2)}, u32[]{:S(2)}) %collective-permute-start.15) | collective-permute-done | bytes 393248 | tf_op jit(solution)/shard_map/ppermute | solution.py:523
  208.6 2.5 collective-permute-done.17
  225.1 2.5 collective-permute-start.19
  227.6 9.7 %collective-permute-done.23 = bf16[4,64,1536]{2,1,0:T(8,128)(2,1)S(1)} collective-permute-done((bf16[4,64,1536]{2,1,0:T(8,128)(2,1)S(1)}, bf16[4,64,1536]{2,1,0:T(8,128)(2,1)S(1)}, u32[]{:S(2)}, u32[]{:S(2)}) %collective-permute-start.23) | collective-permute-done | bytes 786464 | tf_op jit(solution)/shard_map/ppermute | solution.py:519
  239.7 2.2 collective-permute-start.27
  241.9 3.2 %collective-permute-done.18 = bf16[4,64,1536]{2,1,0:T(8,128)(2,1)S(1)} collective-permute-done((bf16[4,64,1536]{2,1,0:T(8,128)(2,1)S(1)}, bf16[4,64,1536]{2,1,0:T(8,128)(2,1)S(1)}, u32[]{:S(2)}, u32[]{:S(2)}) %collective-permute-start.18) | collective-permute-done | bytes 786464 | tf_op jit(solution)/shard_map/ppermute | solution.py:523
  245.0 4.2 %collective-permute-done.19 = bf16[4,64,1536]{2,1,0:T(8,128)(2,1)S(1)} collective-permute-done((bf16[4,64,1536]{2,1,0:T(8,128)(2,1)S(1)}, bf16[4,64,1536]{2,1,0:T(8,128)(2,1)S(1)}, u32[]{:S(2)}, u32[]{:S(2)}) %collective-permute-start.19) | collective-permute-done | bytes 786464 | tf_op jit(solution)/shard_map/ppermute | solution.py:523
  249.8 2.2 collective-permute-start.22
  252.1 4.8 %collective-permute-done.20 = bf16[64,1536]{1,0:T(8,128)(2,1)S(1)} collective-permute-done((bf16[64,1536]{1,0:T(8,128)(2,1)S(1)}, bf16[64,1536]{1,0:T(8,128)(2,1)S(1)}, u32[]{:S(2)}, u32[]{:S(2)}) %collective-permute-start.20) | collective-permute-done | bytes 196640 | tf_op jit(solution)/shard_map/ppermute | solution.py:519
  263.9 8.9 %all-to-all-start.1 = ((bf16[16,20,768]{2,1,0:T(8,128)(2,1)}), bf16[16,20,768]{2,1,0:T(8,128)(2,1)S(1)}, u32[]{:S(2)}, u32[]{:S(2)}) async-start(bf16[16,20,768]{2,1,0:T(8,128)(2,1)} %pad_maximum_fusion.6), calls=%async_computation.3 | async-start | bytes 1179648 | tf_op jit(solution)/shard_map/all_to_all | solution.py:678
  275.3 9.6 %all-to-all-done.1 = bf16[16,20,768]{2,1,0:T(8,128)(2,1)S(1)} async-done(((bf16[16,20,768]{2,1,0:T(8,128)(2,1)}), bf16[16,20,768]{2,1,0:T(8,128)(2,1)S(1)}, u32[]{:S(2)}, u32[]{:S(2)}) %all-to-all-start.1) | async-done | bytes 491552 | tf_op jit(solution)/shard_map/all_to_all | solution.py:678
  (251 shorter events, 68.0 us)
Async XLA Ops:
  7.2 104.0 %all-gather.2.cloned.1.call-start = ((), (), s32[]{:S(2)}) async-start(), calls=%async_computation.4 | async-start | bytes 13369344 | tf_op jit(solution)/shard_map/all_gather | solution.py:624
  14.4 17.8 %all-to-all-start = ((bf16[16,12,768]{2,1,0:T(8,128)(2,1)}), bf16[16,12,768]{2,1,0:T(8,128)(2,1)S(1)}, u32[]{:S(2)}, u32[]{:S(2)}) async-start(bf16[16,12,768]{2,1,0:T(8,128)(2,1)} %bitcast.3), calls=%async_computation | async-start | bytes 786432 | tf_op jit(solution)/shard_map/all_to_all | solution.py:633
  21.5 192.5 %reduce-scatter.3.cloned.1.call-start = ((), (), s32[]{:S(2)}) async-start(), calls=%async_computation.5 | async-start | bytes 6684672 | tf_op jit(solution)/shard_map/reduce_scatter | solution.py:659
  32.3 12.0 %collective-permute-start.4 = (bf16[120,768]{1,0:T(8,128)(2,1)S(1)}, bf16[120,768]{1,0:T(8,128)(2,1)S(1)}, u32[]{:S(2)}, u32[]{:S(2)}) collective-permute-start(bf16[120,768]{1,0:T(8,128)(2,1)S(1)} %slice.207), channel_id=1, source_target_pairs={{0,96},{16,112},{32,0},{48,16},{64,32},{80,48},{96,64},{112,80},{1... | collective-permute-start | bytes 552968 | tf_op jit(solution)/shard_map/ppermute | solution.py:527
  39.6 8.4 %collective-permute-start.1 = (bf16[120,768]{1,0:T(8,128)(2,1)S(1)}, bf16[120,768]{1,0:T(8,128)(2,1)S(1)}, u32[]{:S(2)}, u32[]{:S(2)}) collective-permute-start(bf16[120,768]{1,0:T(8,128)(2,1)S(1)} %slice.158), channel_id=1, source_target_pairs={{0,32},{16,48},{32,64},{48,80},{64,96},{80,112},{96,0},{112,16},{1... | collective-permute-start | bytes 552968 | tf_op jit(solution)/shard_map/ppermute | solution.py:527
  39.8 11.6 %collective-permute-start.2 = (bf16[120,768]{1,0:T(8,128)(2,1)S(1)}, bf16[120,768]{1,0:T(8,128)(2,1)S(1)}, u32[]{:S(2)}, u32[]{:S(2)}) collective-permute-start(bf16[120,768]{1,0:T(8,128)(2,1)S(1)} %slice.207), channel_id=1, source_target_pairs={{0,32},{16,48},{32,64},{48,80},{64,96},{80,112},{96,0},{112,16},{1... | collective-permute-start | bytes 552968 | tf_op jit(solution)/shard_map/ppermute | solution.py:527
  39.9 11.5 %collective-permute-start.3 = (bf16[120,768]{1,0:T(8,128)(2,1)S(1)}, bf16[120,768]{1,0:T(8,128)(2,1)S(1)}, u32[]{:S(2)}, u32[]{:S(2)}) collective-permute-start(bf16[120,768]{1,0:T(8,128)(2,1)S(1)} %slice.158), channel_id=1, source_target_pairs={{0,96},{16,112},{32,0},{48,16},{64,32},{80,48},{96,64},{112,80},{1... | collective-permute-start | bytes 552968 | tf_op jit(solution)/shard_map/ppermute | solution.py:527
  44.3 10.5 %collective-permute-start.6 = (bf16[120,768]{1,0:T(8,128)(2,1)S(1)}, bf16[120,768]{1,0:T(8,128)(2,1)S(1)}, u32[]{:S(2)}, u32[]{:S(2)}) collective-permute-start(bf16[120,768]{1,0:T(8,128)(2,1)S(1)} %collective-permute-done.4), channel_id=1, source_target_pairs={{0,96},{16,112},{32,0},{48,16},{64,32},{80,48},{96,64},{112,80},{1... | collective-permute-start | bytes 552968 | tf_op jit(solution)/shard_map/ppermute | solution.py:527
  131.0 129.2 %reduce-scatter.5.cloned.1.call-start = ((), (), s32[]{:S(2)}) async-start(), calls=%async_computation.6 | async-start | bytes 3538944 | tf_op jit(solution)/shard_map/reduce_scatter | solution.py:670
  195.9 11.3 %collective-permute-start.15 = (bf16[2,64,1536]{2,1,0:T(8,128)(2,1)S(1)}, bf16[2,64,1536]{2,1,0:T(8,128)(2,1)}, u32[]{:S(2)}, u32[]{:S(2)}) collective-permute-start(bf16[2,64,1536]{2,1,0:T(8,128)(2,1)S(1)} %get-tuple-element.61), channel_id=1, source_target_pairs={{0,12},{1,13},{2,14},{3,15},{4,0},{5,1},{6,2},{7,3},{8,4},{9,5},{1... | collective-permute-start | bytes 1179656 | tf_op jit(solution)/shard_map/ppermute | solution.py:523
  195.9 12.6 %collective-permute-start.14 = (bf16[2,64,1536]{2,1,0:T(8,128)(2,1)S(1)}, bf16[2,64,1536]{2,1,0:T(8,128)(2,1)}, u32[]{:S(2)}, u32[]{:S(2)}) collective-permute-start(bf16[2,64,1536]{2,1,0:T(8,128)(2,1)S(1)} %get-tuple-element.62), channel_id=1, source_target_pairs={{0,4},{1,5},{2,6},{3,7},{4,8},{5,9},{6,10},{7,11},{8,12},{9,13},{1... | collective-permute-start | bytes 1179656 | tf_op jit(solution)/shard_map/ppermute | solution.py:523
  198.0 13.1 %collective-permute-start.17 = (bf16[2,64,1536]{2,1,0:T(8,128)(2,1)S(1)}, bf16[2,64,1536]{2,1,0:T(8,128)(2,1)}, u32[]{:S(2)}, u32[]{:S(2)}) collective-permute-start(bf16[2,64,1536]{2,1,0:T(8,128)(2,1)S(1)} %get-tuple-element.59), channel_id=1, source_target_pairs={{0,3},{1,0},{2,1},{3,2},{4,7},{5,4},{6,5},{7,6},{8,11},{9,8},{10,9... | collective-permute-start | bytes 1179656 | tf_op jit(solution)/shard_map/ppermute | solution.py:519
  198.1 15.1 %collective-permute-start.16 = (bf16[2,64,1536]{2,1,0:T(8,128)(2,1)S(1)}, bf16[2,64,1536]{2,1,0:T(8,128)(2,1)}, u32[]{:S(2)}, u32[]{:S(2)}) collective-permute-start(bf16[2,64,1536]{2,1,0:T(8,128)(2,1)S(1)} %get-tuple-element.60), channel_id=1, source_target_pairs={{0,1},{1,2},{2,3},{3,0},{4,5},{5,6},{6,7},{7,4},{8,9},{9,10},{10,1... | collective-permute-start | bytes 1179656 | tf_op jit(solution)/shard_map/ppermute | solution.py:519
  217.1 20.2 %collective-permute-start.23 = (bf16[4,64,1536]{2,1,0:T(8,128)(2,1)S(1)}, bf16[4,64,1536]{2,1,0:T(8,128)(2,1)S(1)}, u32[]{:S(2)}, u32[]{:S(2)}) collective-permute-start(bf16[4,64,1536]{2,1,0:T(8,128)(2,1)S(1)} %pad_maximum_fusion.4), channel_id=1, source_target_pairs={{0,1},{1,2},{2,3},{3,0},{4,5},{5,6},{6,7},{7,4},{8,9},{9,10},{10,1... | collective-permute-start | bytes 2359304 | tf_op jit(solution)/shard_map/ppermute | solution.py:519
  219.7 18.1 %collective-permute-start.24 = (bf16[4,64,1536]{2,1,0:T(8,128)(2,1)S(1)}, bf16[4,64,1536]{2,1,0:T(8,128)(2,1)S(1)}, u32[]{:S(2)}, u32[]{:S(2)}) collective-permute-start(bf16[4,64,1536]{2,1,0:T(8,128)(2,1)S(1)} %pad_maximum_fusion.5), channel_id=1, source_target_pairs={{0,3},{1,0},{2,1},{3,2},{4,7},{5,4},{6,5},{7,6},{8,11},{9,8},{10,9... | collective-permute-start | bytes 2359304 | tf_op jit(solution)/shard_map/ppermute | solution.py:519
  223.0 22.0 %collective-permute-start.18 = (bf16[4,64,1536]{2,1,0:T(8,128)(2,1)S(1)}, bf16[4,64,1536]{2,1,0:T(8,128)(2,1)S(1)}, u32[]{:S(2)}, u32[]{:S(2)}) collective-permute-start(bf16[4,64,1536]{2,1,0:T(8,128)(2,1)S(1)} %pad_maximum_fusion.2), channel_id=1, source_target_pairs={{0,4},{1,5},{2,6},{3,7},{4,8},{5,9},{6,10},{7,11},{8,12},{9,13},{1... | collective-permute-start | bytes 2359304 | tf_op jit(solution)/shard_map/ppermute | solution.py:523
  225.1 24.2 %collective-permute-start.19 = (bf16[4,64,1536]{2,1,0:T(8,128)(2,1)S(1)}, bf16[4,64,1536]{2,1,0:T(8,128)(2,1)S(1)}, u32[]{:S(2)}, u32[]{:S(2)}) collective-permute-start(bf16[4,64,1536]{2,1,0:T(8,128)(2,1)S(1)} %pad_maximum_fusion.3), channel_id=1, source_target_pairs={{0,12},{1,13},{2,14},{3,15},{4,0},{5,1},{6,2},{7,3},{8,4},{9,5},{1... | collective-permute-start | bytes 2359304 | tf_op jit(solution)/shard_map/ppermute | solution.py:523
  238.1 13.8 %collective-permute-start.25 = (bf16[64,1536]{1,0:T(8,128)(2,1)S(1)}, bf16[64,1536]{1,0:T(8,128)(2,1)S(1)}, u32[]{:S(2)}, u32[]{:S(2)}) collective-permute-start(bf16[64,1536]{1,0:T(8,128)(2,1)S(1)} %get-tuple-element.56), channel_id=1, source_target_pairs={{0,8},{1,9},{2,10},{3,11},{4,12},{5,13},{6,14},{7,15},{8,0},{9,1},... | collective-permute-start | bytes 589832 | tf_op jit(solution)/shard_map/ppermute | solution.py:523
  239.7 12.3 %collective-permute-start.27 = (bf16[64,1536]{1,0:T(8,128)(2,1)S(1)}, bf16[64,1536]{1,0:T(8,128)(2,1)S(1)}, u32[]{:S(2)}, u32[]{:S(2)}) collective-permute-start(bf16[64,1536]{1,0:T(8,128)(2,1)S(1)} %get-tuple-element.57), channel_id=1, source_target_pairs={{0,12},{1,13},{2,14},{3,15},{4,0},{5,1},{6,2},{7,3},{8,4},{9,5},{1... | collective-permute-start | bytes 589832 | tf_op jit(solution)/shard_map/ppermute | solution.py:523
  241.9 10.1 %collective-permute-start.26 = (bf16[64,1536]{1,0:T(8,128)(2,1)S(1)}, bf16[64,1536]{1,0:T(8,128)(2,1)S(1)}, u32[]{:S(2)}, u32[]{:S(2)}) collective-permute-start(bf16[64,1536]{1,0:T(8,128)(2,1)S(1)} %get-tuple-element.58), channel_id=1, source_target_pairs={{0,4},{1,5},{2,6},{3,7},{4,8},{5,9},{6,10},{7,11},{8,12},{9,13},{1... | collective-permute-start | bytes 589832 | tf_op jit(solution)/shard_map/ppermute | solution.py:523
  249.7 7.3 %collective-permute-start.20 = (bf16[64,1536]{1,0:T(8,128)(2,1)S(1)}, bf16[64,1536]{1,0:T(8,128)(2,1)S(1)}, u32[]{:S(2)}, u32[]{:S(2)}) collective-permute-start(bf16[64,1536]{1,0:T(8,128)(2,1)S(1)} %get-tuple-element.53), channel_id=1, source_target_pairs={{0,2},{1,3},{2,0},{3,1},{4,6},{5,7},{6,4},{7,5},{8,10},{9,11},{10,... | collective-permute-start | bytes 589832 | tf_op jit(solution)/shard_map/ppermute | solution.py:519
  249.8 7.2 %collective-permute-start.22 = (bf16[64,1536]{1,0:T(8,128)(2,1)S(1)}, bf16[64,1536]{1,0:T(8,128)(2,1)S(1)}, u32[]{:S(2)}, u32[]{:S(2)}) collective-permute-start(bf16[64,1536]{1,0:T(8,128)(2,1)S(1)} %get-tuple-element.54), channel_id=1, source_target_pairs={{0,3},{1,0},{2,1},{3,2},{4,7},{5,4},{6,5},{7,6},{8,11},{9,8},{10,9... | collective-permute-start | bytes 589832 | tf_op jit(solution)/shard_map/ppermute | solution.py:519
  261.1 12.7 %collective-permute-start.28 = (bf16[48,768]{1,0:T(8,128)(2,1)S(1)}, bf16[48,768]{1,0:T(8,128)(2,1)S(1)}, u32[]{:S(2)}, u32[]{:S(2)}) collective-permute-start(bf16[48,768]{1,0:T(8,128)(2,1)S(1)} %slice.232), channel_id=1, source_target_pairs={{0,0},{16,1},{32,2},{48,3},{64,4},{80,5},{96,6},{112,7},{1,8},{17,... | collective-permute-start | bytes 221192 | tf_op jit(solution)/shard_map/ppermute | solution.py:681
  263.9 20.9 %all-to-all-start.1 = ((bf16[16,20,768]{2,1,0:T(8,128)(2,1)}), bf16[16,20,768]{2,1,0:T(8,128)(2,1)S(1)}, u32[]{:S(2)}, u32[]{:S(2)}) async-start(bf16[16,20,768]{2,1,0:T(8,128)(2,1)} %pad_maximum_fusion.6), calls=%async_computation.3 | async-start | bytes 1179648 | tf_op jit(solution)/shard_map/all_to_all | solution.py:678
  (37 other events, 220.5 us)
Sparse Core Ops, SparseCore 0:
  12.2 98.8 all-gather.1
  131.1 82.8 reduce-scatter.2
  216.4 35.5 reduce-scatter.4

commit v4 on v3

--- a/solution.py
+++ b/solution.py
@@ -42,18 +42,42 @@
     )
 
 
-def running(a, back):
+def in_parts(a, count):
+    parts = []
+    for _ in range(count):
+        parts.append(a.astype(low))
+        a = a - parts[-1].astype(f32)
+    return jnp.concatenate(parts, axis=0)
+
+
+def summed_parts(a, count):
+    n = a.shape[0] // count
+    return sum([a[n * i : n * (i + 1)] for i in range(count)])
+
+
+def running(a):
+    s = lax.broadcasted_iota(jnp.int32, (CHUNK, CHUNK), 0)
+    t = lax.broadcasted_iota(jnp.int32, (CHUNK, CHUNK), 1)
+    return summed_parts(mm(in_parts(a, 3), (s <= t).astype(low)), 3)
+
+
+def running_by_steps(a):
     lane = lax.broadcasted_iota(jnp.int32, a.shape, 1)
     step = 1
     while step < CHUNK:
-        if back:
-            a = a + jnp.where(lane < CHUNK - step, pltpu.roll(a, CHUNK - step, 1), 0.0)
-        else:
-            a = a + jnp.where(lane >= step, pltpu.roll(a, step, 1), 0.0)
+        a = a + jnp.where(lane >= step, pltpu.roll(a, step, 1), 0.0)
         step *= 2
     return a
 
 
+def reaching(after, before):
+    s = lax.broadcasted_iota(jnp.int32, (2 * CHUNK, CHUNK), 0)
+    t = lax.broadcasted_iota(jnp.int32, (2 * CHUNK, CHUNK), 1)
+    ones = ((s < CHUNK) & (s >= t)) | ((s >= CHUNK) & (s - CHUNK < t))
+    both = jnp.concatenate([after, before], axis=1)
+    return summed_parts(mm(in_parts(both, 2), ones.astype(low)), 2)
+
+
 def part(a, j):
     return a[CHUNK * j : CHUNK * (j + 1)]
 
@@ -62,7 +86,7 @@
     return a[8 * j : 8 * (j + 1)]
 
 
-def block_terms(zdt, rows_ref, head_ref):
+def block_terms(zdt, rows_ref, head_ref, running):
     raw = jnp.concatenate([part(zdt, j)[:, 128:256].T[64:72] for j in range(GROUP)], axis=0)
     wide = lambda row: jnp.concatenate(
         [jnp.broadcast_to(rows_ref[j, row : row + 1, :], (8, CHUNK)) for j in range(GROUP)], axis=0
@@ -71,7 +95,7 @@
     ea = jnp.exp(head_ref[1])
     step = jnp.maximum(v, 0.0) + jnp.log1p(jnp.exp(-jnp.abs(v)))
     ld = -step * ea
-    cum = running(ld, False)
+    cum = running(ld)
     total = cum[:, CHUNK - 1 : CHUNK]
     seg = wide(0)
     before = wide(1)[:, 0:1]
@@ -110,7 +134,10 @@
     head_ref,
     skip_ref,
     proj_ref,
-    y_ref,
+    act_ref,
+    slope_ref,
+    z_act_ref,
+    y_slope_ref,
     gated_ref,
     u_ref,
     kept_ref,
@@ -135,27 +162,32 @@
     zdt = proj_ref[:, 0:256].astype(f32)
     ext_ref[8 : BLOCK + 8, :] = proj_ref[:, 256:PAD].astype(f32)
     pre = convolved(ext_ref, conv_ref)
-    act = pre * jax.nn.sigmoid(pre)
+    sig = jax.nn.sigmoid(pre)
+    act = pre * sig
+    act_ref[...] = act.astype(low)
+    slope_ref[...] = (sig + act * (1.0 - sig)).astype(low)
     x = act[:, :WIDE]
     x_low = x.astype(low)
     b_low = act[:, 256:384].astype(low)
     c_low = act[:, 384:512].astype(low)
-    v, ea, step, ld, cum, to_end, whole, cols = block_terms(zdt, rows_ref, head_ref)
-    inner, local, entries, wholes = [], [], [], []
-    for j in range(GROUP):
+    v, ea, step, ld, cum, to_end, whole, cols = block_terms(zdt, rows_ref, head_ref, running_by_steps)
+    chunks = range(GROUP)
+    scores_all = [mm(part(c_low, j), part(b_low, j), NT) for j in chunks]
+    leavings = [per_head([c[:, 16 + h : 17 + h] for h in range(OWN)]) for c in cols]
+    entries = [per_head([c[:, 8 + h : 9 + h] for h in range(OWN)]) for c in cols]
+    wholes = [per_head([whole[8 * j + h : 8 * j + h + 1] for h in range(OWN)]) for j in chunks]
+    local = [mm(part(b_low, j), (leavings[j] * part(x, j)).astype(low), TN) for j in chunks]
+    mixing_all = []
+    for j in chunks:
         col = cols[j]
         bar = barred(col, rows_ref[j, 0:1, :])
-        scores = mm(part(c_low, j), part(b_low, j), NT)
         mixing = []
         for h in range(OWN):
             i = 8 * j + h
             decay = jnp.exp(col[:, h : h + 1] - cum[i : i + 1] + bar)
-            mixing.append((scores * decay * step[i : i + 1]).astype(low))
-        inner.append(mm(jnp.concatenate(mixing, axis=1), stacked(part(x_low, j))))
-        leaving = per_head([col[:, 16 + h : 17 + h] for h in range(OWN)])
-        local.append(mm(part(b_low, j), (leaving * part(x, j)).astype(low), TN))
-        entries.append(per_head([col[:, 8 + h : 9 + h] for h in range(OWN)]))
-        wholes.append(per_head([whole[8 * j + h : 8 * j + h + 1] for h in range(OWN)]))
+            mixing.append((scores_all[j] * decay * step[i : i + 1]).astype(low))
+        mixing_all.append(jnp.concatenate(mixing, axis=1))
+    inner = [mm(mixing_all[j], stacked(part(x_low, j))) for j in chunks]
     state = state_ref[...]
     ys = []
     for j in range(GROUP):
@@ -165,11 +197,16 @@
     state_ref[...] = state
     y = jnp.concatenate(ys, axis=0) + skip_ref[...] * x
     z = zdt[:, :WIDE]
-    gated = y * z * jax.nn.sigmoid(z)
+    z_sig = jax.nn.sigmoid(z)
+    z_act = z * z_sig
+    gated = y * z_act
     gated_low = gated.astype(low)
-    y_ref[...] = y
+    z_act_ref[...] = z_act.astype(low)
+    y_slope_ref[...] = (y * (z_sig + z_act * (1.0 - z_sig))).astype(low)
     gated_ref[...] = gated_low
-    total_ref[...] = mm(gated_low, out_ref[...]).astype(low)
+    given = mm(gated_low, out_ref[...]).astype(low)
+    for j in range(GROUP):
+        total_ref[j, 0] = part(given, j)
     ones = jnp.ones((8, WIDE), low)
     squares = mm(ones, (gated * gated).astype(low), NT)
     products = mm(ones, (gated * u_ref[...]).astype(low), NT)
@@ -180,14 +217,16 @@
 def backward_kernel(
     place_ref,
     proj_ref,
-    before_ref,
     w_ref,
     both_ref,
     rows_ref,
     conv_ref,
     head_ref,
     skip_ref,
-    y_ref,
+    act_ref,
+    slope_ref,
+    z_act_ref,
+    y_slope_ref,
     gated_ref,
     u_ref,
     kept_ref,
@@ -200,7 +239,6 @@
     bottom_2,
     bottom_3,
     grads_ref,
-    ext_ref,
     later_ref,
     state_ref,
     conv_grad_ref,
@@ -227,32 +265,22 @@
     def _():
         later_ref[BLOCK : BLOCK + 8, :] = later_ref[0:8, :]
 
-    ahead = before_ref[8:16, 256:PAD].astype(f32)
-    ext_ref[0:8, :] = jnp.where(step_id == count - 1, 0.0, ahead)
     conv_in = proj_ref[:, 256:PAD].astype(f32)
-    ext_ref[8 : BLOCK + 8, :] = conv_in
     zdt = proj_ref[:, 0:256].astype(f32)
-    pre = convolved(ext_ref, conv_ref)
-    sig = jax.nn.sigmoid(pre)
-    act = pre * sig
-    slope = sig * (1.0 + pre * (1.0 - sig))
-    x = act[:, :WIDE]
-    x_low = x.astype(low)
-    b_low = act[:, 256:384].astype(low)
-    c_low = act[:, 384:512].astype(low)
-    v, ea, step, ld, cum, to_end, whole, cols = block_terms(zdt, rows_ref, head_ref)
-
-    z = zdt[:, :WIDE]
-    z_sig = jax.nn.sigmoid(z)
-    z_act = z * z_sig
-    y = y_ref[...]
+    x_low = act_ref[:, :WIDE]
+    x = x_low.astype(f32)
+    b_low = act_ref[:, 256:384]
+    c_low = act_ref[:, 384:512]
+    v, ea, step, ld, cum, to_end, whole, cols = block_terms(zdt, rows_ref, head_ref, running)
+
     r_col = jnp.concatenate([c[:, 26:27] for c in cols], axis=0)
     c_col = jnp.concatenate([c[:, 27:28] for c in cols], axis=0)
-    d_gated = r_col * u_ref[...] - c_col * (y * z_act)
-    dy = d_gated * z_act
-    dz = d_gated * y * (z_sig * (1.0 + z * (1.0 - z_sig)))
+    gated = gated_ref[...].astype(f32)
+    d_gated = r_col * u_ref[...] - c_col * gated
+    dy = d_gated * z_act_ref[...].astype(f32)
+    dz = d_gated * y_slope_ref[...].astype(f32)
     dy_low = dy.astype(low)
-    normed = (gated_ref[...].astype(f32) * r_col).astype(low)
+    normed = (gated * r_col).astype(low)
     out_grad = mm(normed, both_ref[:, D : 2 * D], TN)
     for d in range(8):
         total_ref[d, 192:216] += out_grad[24 * d : 24 * d + 24, 0:PAD]
@@ -266,13 +294,19 @@
     lane = lax.broadcasted_iota(jnp.int32, (8, WIDE), 1)
     by_head = ((lane >= 64 * row_head) & (lane < 64 * row_head + 64)).astype(low)
 
-    dx_in, d_scores_all, d_steps_all, inside_all = [], [], [], []
-    entries, leavings, wholes, to_state, dy_entries = [], [], [], [], []
-    for j in range(GROUP):
+    chunks = range(GROUP)
+    d_scores_all, d_steps_all, inside_all, mixing_all, flow_all = [], [], [], [], []
+    entries = [per_head([c[:, 8 + h : 9 + h] for h in range(OWN)]) for c in cols]
+    leavings = [per_head([c[:, 16 + h : 17 + h] for h in range(OWN)]) for c in cols]
+    wholes = [per_head([whole[8 * j + h : 8 * j + h + 1] for h in range(OWN)]) for j in chunks]
+    scores_all = [mm(part(c_low, j), part(b_low, j), NT) for j in chunks]
+    d_mixing_all = [mm(part(dy_low, j), stacked(part(x_low, j)), NT) for j in chunks]
+    dy_entries = [entries[j] * part(dy, j) for j in chunks]
+    to_state = [mm(part(c_low, j), dy_entries[j].astype(low), TN) for j in chunks]
+    for j in chunks:
         col = cols[j]
         bar = barred(col, rows_ref[j, 0:1, :])
-        scores = mm(part(c_low, j), part(b_low, j), NT)
-        d_mixing = mm(part(dy_low, j), stacked(part(x_low, j)), NT)
+        scores, d_mixing = scores_all[j], d_mixing_all[j]
         d_scores = jnp.zeros((CHUNK, CHUNK), f32)
         mixings, flows, d_steps = [], [], []
         for h in range(OWN):
@@ -285,21 +319,17 @@
             d_scores = d_scores + d_mix * stepped
             flows.append((d_mix * mixing).astype(low))
             d_steps.append(jnp.sum(d_mix * scores * decay, axis=0, keepdims=True))
-        reach = mm(jnp.concatenate(flows, axis=0), earlier)
-        inside = [
-            jnp.sum(jnp.where(t >= s, part(reach, h), 0.0), axis=0, keepdims=True)
-            for h in range(OWN)
-        ]
         d_scores_all.append(d_scores.astype(low))
         d_steps_all += d_steps + [blank]
-        inside_all += inside + [blank]
-        dx_in.append(mm(jnp.concatenate(mixings, axis=0), stacked(part(dy_low, j)), TN))
-        entry = per_head([col[:, 8 + h : 9 + h] for h in range(OWN)])
-        dy_entry = entry * part(dy, j)
-        dy_entries.append(dy_entry)
-        to_state.append(mm(part(c_low, j), dy_entry.astype(low), TN))
-        leavings.append(per_head([col[:, 16 + h : 17 + h] for h in range(OWN)]))
-        wholes.append(per_head([whole[8 * j + h : 8 * j + h + 1] for h in range(OWN)]))
+        mixing_all.append(jnp.concatenate(mixings, axis=0))
+        flow_all.append(jnp.concatenate(flows, axis=0))
+    reach_all = [mm(flow_all[j], earlier) for j in chunks]
+    dx_in = [mm(mixing_all[j], stacked(part(dy_low, j)), TN) for j in chunks]
+    for j in chunks:
+        inside_all += [
+            jnp.sum(jnp.where(t >= s, part(reach_all[j], h), 0.0), axis=0, keepdims=True)
+            for h in range(OWN)
+        ] + [blank]
 
     laters = [None] * GROUP
     later = state_ref[...]
@@ -308,29 +338,35 @@
         later = wholes[j] * later + to_state[j]
     state_ref[...] = later
 
-    xv, row_state, overlap, dxs, dbs, dcs = [], [], [], [], [], []
-    for j in range(GROUP):
-        bj, cj, xj = part(b_low, j), part(c_low, j), part(x, j)
-        state_low = kept_ref[j].astype(low)
-        later_low = laters[j].astype(low)
-        from_later = mm(bj, later_low)
-        dxs.append(dx_in[j] + leavings[j] * from_later)
-        x_leaving = (leavings[j] * xj).astype(low)
-        d_scores = d_scores_all[j]
-        dcs.append(mm(d_scores, bj) + mm(dy_entries[j].astype(low), state_low, NT))
-        dbs.append(mm(d_scores, cj, TN) + mm(x_leaving, later_low, NT))
-        xv.append(mm(by_head, (xj * from_later).astype(low), NT))
-        row_state.append(mm(by_head, (dy_entries[j] * mm(cj, state_low)).astype(low), NT))
-        both = mm(by_head, (laters[j] * kept_ref[j]).astype(low), NT)
-        overlap.append(jnp.sum(both, axis=1, keepdims=True))
+    bs = [part(b_low, j) for j in chunks]
+    cs = [part(c_low, j) for j in chunks]
+    states = [kept_ref[j] for j in chunks]
+    state_lows = [a.astype(low) for a in states]
+    later_lows = [a.astype(low) for a in laters]
+    from_laters = [mm(bs[j], later_lows[j]) for j in chunks]
+    from_states = [mm(cs[j], state_lows[j]) for j in chunks]
+    dc_in = [mm(d_scores_all[j], bs[j]) for j in chunks]
+    db_in = [mm(d_scores_all[j], cs[j], TN) for j in chunks]
+    dc_out = [mm(dy_entries[j].astype(low), state_lows[j], NT) for j in chunks]
+    db_out = [
+        mm((leavings[j] * part(x, j)).astype(low), later_lows[j], NT) for j in chunks
+    ]
+    xv = [mm(by_head, (part(x, j) * from_laters[j]).astype(low), NT) for j in chunks]
+    row_state = [mm(by_head, (dy_entries[j] * from_states[j]).astype(low), NT) for j in chunks]
+    overlap = [
+        jnp.sum(mm(by_head, (laters[j] * states[j]).astype(low), NT), axis=1, keepdims=True)
+        for j in chunks
+    ]
+    dxs = [dx_in[j] + leavings[j] * from_laters[j] for j in chunks]
+    dcs = [dc_in[j] + dc_out[j] for j in chunks]
+    dbs = [db_in[j] + db_out[j] for j in chunks]
     stack = lambda a: jnp.concatenate(a, axis=0)
     ended = to_end * stack(xv)
     col_state = ended * step
     d_step = stack(d_steps_all) + ended
     d_ld = (
         stack(inside_all)
-        + running(stack(row_state), True)
-        + (running(col_state, False) - col_state)
+        + reaching(stack(row_state), col_state)
         + whole * stack(overlap)
     )
     d_dt = (d_step - d_ld * ea) * jax.nn.sigmoid(v)
@@ -339,10 +375,10 @@
     skip_grad_ref[...] += jnp.sum((dy * x).reshape(BLOCK // 8, 8, WIDE), axis=0)
 
     dx = stack(dxs) + skip_ref[...] * dy
-    later_ref[0:BLOCK, 0:WIDE] = dx * slope[:, :WIDE]
+    later_ref[0:BLOCK, 0:WIDE] = dx * slope_ref[:, :WIDE].astype(f32)
     later_ref[0:BLOCK, WIDE:256] = jnp.zeros((BLOCK, 256 - WIDE), f32)
-    later_ref[0:BLOCK, 256:384] = stack(dbs) * slope[:, 256:384]
-    later_ref[0:BLOCK, 384:512] = stack(dcs) * slope[:, 384:512]
+    later_ref[0:BLOCK, 256:384] = stack(dbs) * slope_ref[:, 256:384].astype(f32)
+    later_ref[0:BLOCK, 384:512] = stack(dcs) * slope_ref[:, 384:512].astype(f32)
     d_conv_in = jnp.zeros((BLOCK, 512), f32)
     for k in range(CONV):
         moved = later_ref[pl.ds(CONV - 1 - k, BLOCK), :]
@@ -364,8 +400,8 @@
     in_grad = mm(both_ref[:, 0:D], d_proj_ref[...], TN)
     for d in range(8):
         total_ref[d, 0:192] += in_grad[192 * d : 192 * d + 192]
-
     given_ref[...] = mm(d_proj_ref[...], w_ref[...], NT).astype(low)
+
     row = count - 1 - step_id
     up = lax.rem(row - place_ref[1] + 4, 4)
     for k, ref in enumerate((top_0, top_1, top_2, top_3)):
@@ -384,20 +420,25 @@
 
     @pl.when(step_id == count - 1)
     def _():
-        place = lax.broadcasted_iota(jnp.int32, (8, 256), 1)
+        lane = lax.broadcasted_iota(jnp.int32, (8, 256), 1)
+        head = lax.broadcasted_iota(jnp.int32, (8, 256), 0)
         bias = jnp.sum(head_grad_ref[0], axis=1, keepdims=True)
         rate = jnp.sum(head_grad_ref[1], axis=1, keepdims=True)
-        sums_ref[:, 512:PAD] = jnp.where(place == 0, bias, jnp.where(place == 1, rate, 0.0))
-        for k in range(CONV + 1):
-            sums_ref[k : k + 1, 0:512] = jnp.sum(conv_grad_ref[k], axis=0, keepdims=True)
-        sums_ref[5:8, 0:512] = jnp.zeros((3, 512), f32)
-        sums_ref[5:6, 0:WIDE] = jnp.sum(skip_grad_ref[...], axis=0, keepdims=True)
-        sums = sums_ref[...]
-        high = sums.astype(low).astype(f32)
-        tail = jnp.concatenate([high, sums - high], axis=0).astype(low)
+        heads = jnp.where((lane == head) & (head < OWN), bias, 0.0)
+        heads = heads + jnp.where((lane == head + OWN) & (head < OWN), rate, 0.0)
+        taps = [jnp.sum(conv_grad_ref[k], axis=0, keepdims=True) for k in range(CONV + 1)]
+        skips = jnp.sum(skip_grad_ref[...], axis=0, keepdims=True)
+        for k in range(CONV):
+            sums_ref[k : k + 1, 0:512] = taps[k]
+        sums_ref[0:1, 512:PAD] = taps[CONV][:, 0:256]
+        sums_ref[1:2, 512:PAD] = taps[CONV][:, 256:512]
+        sums_ref[2:3, 512 : 512 + WIDE] = skips
+        sums_ref[2:3, 512 + WIDE : PAD] = jnp.zeros((1, 256 - WIDE), f32)
+        sums_ref[3:4, 512:PAD] = jnp.sum(heads, axis=0, keepdims=True)
+        high = sums_ref[0:4, :].astype(low).astype(f32)
+        tail = jnp.concatenate([high, sums_ref[0:4, :] - high], axis=0)
         for d in range(8):
-            grads_ref[d, 0:240] = total_ref[d].astype(low)
-            grads_ref[d, 240:256] = tail
+            grads_ref[d] = jnp.concatenate([total_ref[d], tail], axis=0).astype(low)
 
 
 def ssd_forward(both, w, w_out, rows, conv, heads, skip):
@@ -419,20 +460,26 @@
         ],
         out_specs=[
             here(PAD),
+            here(512),
+            here(512),
+            here(WIDE),
             here(WIDE),
             here(WIDE),
             here(WIDE),
             pl.BlockSpec((GROUP, STATE, WIDE), lambda i: (i, 0, 0)),
-            here(D),
+            pl.BlockSpec((GROUP, 1, CHUNK, D), lambda i: (0, i, 0, 0)),
             pl.BlockSpec((8, BLOCK), lambda i: (0, i)),
         ],
         out_shape=[
             jax.ShapeDtypeStruct((length, PAD), low),
-            jax.ShapeDtypeStruct((length, WIDE), f32),
+            jax.ShapeDtypeStruct((length, 512), low),
+            jax.ShapeDtypeStruct((length, 512), low),
+            jax.ShapeDtypeStruct((length, WIDE), low),
+            jax.ShapeDtypeStruct((length, WIDE), low),
             jax.ShapeDtypeStruct((length, WIDE), low),
             jax.ShapeDtypeStruct((length, WIDE), f32),
             jax.ShapeDtypeStruct((length // CHUNK, STATE, WIDE), f32),
-            jax.ShapeDtypeStruct((length, D), low),
+            jax.ShapeDtypeStruct((GROUP, steps, CHUNK, D), low),
             jax.ShapeDtypeStruct((8, length), f32),
         ],
         scratch_shapes=[pltpu.VMEM((BLOCK + 8, 512), f32), pltpu.VMEM((STATE, WIDE), f32)],
@@ -443,7 +490,7 @@
     )(both, w, w_out, rows, conv, heads, skip)
 
 
-def ssd_backward(place, both, w, proj, rows, conv, heads, skip, y, gated, u, kept):
+def ssd_backward(place, both, w, proj, rows, conv, heads, skip, *saved):
     length = proj.shape[0]
     steps = length // BLOCK
     back = lambda i: steps - 1 - i
@@ -455,13 +502,15 @@
         in_specs=[
             pl.BlockSpec(memory_space=pltpu.SMEM),
             here(PAD),
-            pl.BlockSpec((16, PAD), lambda i: (jnp.maximum(back(i) * (BLOCK // 16) - 1, 0), 0)),
             whole((D, PAD)),
             here(2 * D),
             pl.BlockSpec((GROUP, 8, CHUNK), lambda i: (back(i), 0, 0)),
             whole((8, 512)),
             whole((2, 8 * GROUP, CHUNK)),
             whole((1, WIDE)),
+            here(512),
+            here(512),
+            here(WIDE),
             here(WIDE),
             here(WIDE),
             here(WIDE),
@@ -469,14 +518,13 @@
         ],
         out_specs=[
             *[whole((4, 64, D)) for _ in range(8)],
-            whole((8, 256, PAD)),
+            whole((8, 248, PAD)),
         ],
         out_shape=[
             *[jax.ShapeDtypeStruct((4, 64, D), low) for _ in range(8)],
-            jax.ShapeDtypeStruct((8, 256, PAD), low),
+            jax.ShapeDtypeStruct((8, 248, PAD), low),
         ],
         scratch_shapes=[
-            pltpu.VMEM((BLOCK + 8, 512), f32),
             pltpu.VMEM((BLOCK + 8, 512), f32),
             pltpu.VMEM((STATE, WIDE), f32),
             pltpu.VMEM((CONV + 1, 8, 512), f32),
@@ -491,11 +539,13 @@
             dimension_semantics=("arbitrary",), vmem_limit_bytes=56 * 1024 * 1024
         ),
         name="ssd_backward",
-    )(place, proj, proj, w, both, rows, conv, heads, skip, y, gated, u, kept)
+    )(place, proj, w, both, rows, conv, heads, skip, *saved)
 
 
 epsilon = 1e-05
 BOTH = ("dp", "seq")
+X_GROUPS = [[4 * y + x for x in range(4)] for y in range(4)]
+Y_GROUPS = [[4 * y + x for y in range(4)] for x in range(4)]
 
 
 def columns_of(a, small):
@@ -653,45 +703,53 @@
         rows + [jnp.zeros((8 - len(rows), 2048), f32)], axis=0
     ).reshape(8, 16, CHUNK).transpose(1, 0, 2)
 
-    proj, y, gated, u, kept, partial_out, sums = ssd_forward(
+    proj, *saved, partial_out, sums = ssd_forward(
         both, w_own, w_out_own, by_chunk([segment, before]), conv, heads, skip
     )
-    total = lax.psum_scatter(partial_out, "seq", scatter_dimension=0, tiled=True)
+    total = lax.psum_scatter(
+        partial_out.reshape(2048, D), "seq", scatter_dimension=0, tiled=True, axis_index_groups=X_GROUPS
+    )
     sums = seq_sum(sums[:2].reshape(32, 128)).reshape(2, 2048)
     r = lax.rsqrt(sums[0:1] / INNER + epsilon)
     c = r * r * r * (sums[1:2] / INNER)
 
     place = jnp.stack([me % 4, me // 4])
     *pieces, grads = ssd_backward(
-        place, both, w_own, proj, by_chunk([segment, before, r, c]), conv, heads, skip, y, gated, u, kept
+        place, both, w_own, proj, by_chunk([segment, before, r, c]), conv, heads, skip, *saved
     )
     v, came = scattered_sum(pieces[:4], pieces[4:])
-    grads, total, came = lax.optimization_barrier((grads, total, came))
-    grads = lax.psum_scatter(
-        grads.reshape(8 * 256, PAD), "dp", scatter_dimension=0, tiled=True
-    ).astype(f32)
-    small = (grads[240:248] + grads[248:256]).astype(low)
-    grads = grads[:240].astype(low)
+    grads, total = lax.optimization_barrier((grads, total))
+    grads = lax.psum_scatter(grads.reshape(8 * 248, PAD), "dp", scatter_dimension=0, tiled=True)
+    grads, total = lax.optimization_barrier((grads, total))
+    total = lax.psum_scatter(
+        total, "seq", scatter_dimension=0, tiled=True, axis_index_groups=Y_GROUPS
+    )
+    small = (grads[240:244].astype(f32) + grads[244:248].astype(f32)).astype(low)
     g_parts = jnp.concatenate(
-        [grads[:192].reshape(16, 12, PAD), jnp.broadcast_to(small[None], (16, 8, PAD))], axis=1
+        [grads[:192].reshape(16, 12, PAD), jnp.broadcast_to(small[None], (16, 4, PAD))], axis=1
     )
     g_parts = lax.all_to_all(g_parts, "seq", 0, 0)
+    g_out = lax.ppermute(grads[192:240], BOTH, block_order(True)).astype(f32)
+    g_out = jnp.concatenate([g_out[:24], g_out[24:]], axis=1)
     small = g_parts[:, 12:].astype(f32)
     g_parts = g_parts[:, :12]
-    g_out = lax.ppermute(grads[192:], BOTH, block_order(True)).astype(f32)
-    g_out = jnp.concatenate([g_out[:24], g_out[24:]], axis=1)
     conv_sum = jnp.concatenate(
         [
-            small[:, : CONV + 1, :WIDE].transpose(1, 0, 2).reshape(CONV + 1, INNER),
-            jnp.sum(small[:, : CONV + 1, 256:512], axis=0),
+            small[:, :, :WIDE].transpose(1, 0, 2).reshape(CONV, INNER),
+            jnp.sum(small[:, :, 256:512], axis=0),
         ],
         axis=1,
     )
-    conv_sum = lax.dynamic_slice_in_dim(conv_sum, 26 * (16 * row + me), 26, 1)
+    bias_sum = jnp.concatenate(
+        [small[:, 0, 512 : 512 + WIDE].reshape(INNER), jnp.sum(small[:, 1, 512:], axis=0)]
+    )
+    at = 26 * (16 * row + me)
+    conv_sum = lax.dynamic_slice_in_dim(conv_sum, at, 26, 1)
+    bias_sum = lax.dynamic_slice_in_dim(bias_sum, at, 26, 0)
     head_sum = (
-        small[:, :OWN, 512].reshape(HEADS),
-        small[:, :OWN, 513].reshape(HEADS),
-        small[:, 5, :WIDE].reshape(HEADS, 64).sum(axis=1),
+        small[:, 3, 512 : 512 + OWN].reshape(HEADS),
+        small[:, 3, 512 + OWN : 512 + 2 * OWN].reshape(HEADS),
+        small[:, 2, 512 : 512 + WIDE].reshape(HEADS, 64).sum(axis=1),
     )
     g_parts = g_parts.astype(f32).transpose(1, 0, 2)
     g_in = jnp.concatenate(
@@ -718,8 +776,8 @@
         grad_hidden[None],
         grad_pre_gain,
         grad_w_in,
-        conv_sum[:CONV],
-        conv_sum[CONV],
+        conv_sum,
+        bias_sum,
         head_sum[0],
         head_sum[1],
         head_sum[2],

time: 298 us -> 289 us (0.970)
  waiting for transfers between devices: 121 us -> 113 us
  Pallas kernels: 64.7 us -> 59.8 us
  starting transfers between devices: 57.8 us -> 62.2 us
    ppermute x10, waiting for transfers between devices: 19.5 us -> 3.53 us  [along_y(): lax.ppermute(a, 'seq', [(s, (s // 4 + k) % 4 * 4 + s % 4) for s in range(...]
    ppermute x10, waiting for transfers between devices: 25.8 us -> 33.9 us  [along_x(): lax.ppermute(a, 'seq', [(s, s // 4 * 4 + (s % 4 + k) % 4) for s in range(...]
    pallas_call x1, Pallas kernels: 44.8 us -> 38.8 us  [ssd_backward(): pl.pallas_call(backward_kernel, grid=(steps,), in_specs=[pl.BlockSpec(mem...]
    ppermute x10, starting transfers between devices: 13 us -> 17 us  [along_x(): lax.ppermute(a, 'seq', [(s, s // 4 * 4 + (s % 4 + k) % 4) for s in range(...]
    convert_element_type x4, other arithmetic: 4.36 us -> 0.37 us  [added(): return (a.astype(f32) + b.astype(f32)).astype(low)]
    reduce_scatter x2 -> x3, waiting for transfers between devices: 0.79 us -> 3.97 us  [the longest x1 3.95 us: local(): lax.psum_scatter(partial_out.reshape(2048, D), 'seq', scatter_dimension=0...]
  transfers between devices with their start and end apart: 34 -> 35, of which waited for: 23 -> 19; matrix products, arithmetic and copies ran while one was open for 9% -> 10% of each run, Pallas kernels for 15% -> 13%
where the time goes in v4:
time: 289 us; the launch traced here: 288 us
  waiting for transfers between devices  113 us (39%)
  starting transfers between devices  62.2 us (22%)
  Pallas kernels  59.8 us (21%)
  local copies, waits for them, and re-layouts  19.8 us (7%)
  other arithmetic  18.1 us (6%)
  between operations  14.8 us (5%)
    all_gather x1, waiting for transfers between devices, local(): both = lax.all_gather(both, 'seq', axis=0, tiled=True)  44.5 us
    pallas_call x1, Pallas kernels, ssd_backward(): pl.pallas_call(backward_kernel, grid=(steps,), in_specs=[pl.BlockSpec(mem...  38.8 us
    ppermute x10, waiting for transfers between devices, along_x(): lax.ppermute(a, 'seq', [(s, s // 4 * 4 + (s % 4 + k) % 4) for s in range(...  33.9 us
    pallas_call x1, Pallas kernels, ssd_forward(): pl.pallas_call(forward_kernel, grid=(steps,), in_specs=[here(2 * D), whol...  20.9 us
    ppermute x10, starting transfers between devices, along_x(): lax.ppermute(a, 'seq', [(s, s // 4 * 4 + (s % 4 + k) % 4) for s in range(...  17 us
    ppermute x6, starting transfers between devices, along_z(): lax.ppermute(a, 'dp', [(d, (d // 2 + k) % 4 * 2 + d % 2) for d in range(8)])  14.3 us
    ppermute x10, starting transfers between devices, along_y(): lax.ppermute(a, 'seq', [(s, (s // 4 + k) % 4 * 4 + s % 4) for s in range(...  13.3 us
    all_to_all x1, waiting for transfers between devices, local(): parts = lax.all_to_all(parts, 'seq', 0, 0, tiled=True)  9.77 us
  transfers between devices with their start and end apart: 35, of which 19 were waited for; matrix products, arithmetic and copies ran while one was open for 10% of the time, Pallas kernels for 13%

profile of v4, /device:TPU:0, one launch (start us, length us, event | category | flops | bytes accessed | tf_op | source)
XLA Modules:
  0.0 287.8 jit_solution(8322471946853758911)
XLA Ops:
  14.4 7.1 %all-to-all-start = ((bf16[16,12,768]{2,1,0:T(8,128)(2,1)}), bf16[16,12,768]{2,1,0:T(8,128)(2,1)S(1)}, u32[]{:S(2)}, u32[]{:S(2)}) async-start(bf16[16,12,768]{2,1,0:T(8,128)(2,1)} %bitcast.3), calls=%async_computation | async-start | bytes 786432 | tf_op jit(solution)/shard_map/all_to_all | solution.py:683
  22.4 9.8 %all-to-all-done = bf16[16,12,768]{2,1,0:T(8,128)(2,1)S(1)} async-done(((bf16[16,12,768]{2,1,0:T(8,128)(2,1)}), bf16[16,12,768]{2,1,0:T(8,128)(2,1)S(1)}, u32[]{:S(2)}, u32[]{:S(2)}) %all-to-all-start) | async-done | bytes 294944 | tf_op jit(solution)/shard_map/all_to_all | solution.py:683
  32.3 7.2 %collective-permute-start.4 = (bf16[120,768]{1,0:T(8,128)(2,1)S(1)}, bf16[120,768]{1,0:T(8,128)(2,1)S(1)}, u32[]{:S(2)}, u32[]{:S(2)}) collective-permute-start(bf16[120,768]{1,0:T(8,128)(2,1)S(1)} %slice.203), channel_id=1, source_target_pairs={{0,96},{16,112},{32,0},{48,16},{64,32},{80,48},{96,64},{112,80},{1... | collective-permute-start | bytes 552968 | tf_op jit(solution)/shard_map/ppermute | solution.py:577
  39.9 3.2 %collective-permute-start.3 = (bf16[120,768]{1,0:T(8,128)(2,1)S(1)}, bf16[120,768]{1,0:T(8,128)(2,1)S(1)}, u32[]{:S(2)}, u32[]{:S(2)}) collective-permute-start(bf16[120,768]{1,0:T(8,128)(2,1)S(1)} %slice.154), channel_id=1, source_target_pairs={{0,96},{16,112},{32,0},{48,16},{64,32},{80,48},{96,64},{112,80},{1... | collective-permute-start | bytes 552968 | tf_op jit(solution)/shard_map/ppermute | solution.py:577
  44.3 3.7 %collective-permute-start.6 = (bf16[120,768]{1,0:T(8,128)(2,1)S(1)}, bf16[120,768]{1,0:T(8,128)(2,1)S(1)}, u32[]{:S(2)}, u32[]{:S(2)}) collective-permute-start(bf16[120,768]{1,0:T(8,128)(2,1)S(1)} %collective-permute-done.4), channel_id=1, source_target_pairs={{0,96},{16,112},{32,0},{48,16},{64,32},{80,48},{96,64},{112,80},{1... | collective-permute-start | bytes 552968 | tf_op jit(solution)/shard_map/ppermute | solution.py:577
  48.0 3.3 %collective-permute-done.2 = bf16[120,768]{1,0:T(8,128)(2,1)S(1)} collective-permute-done((bf16[120,768]{1,0:T(8,128)(2,1)S(1)}, bf16[120,768]{1,0:T(8,128)(2,1)S(1)}, u32[]{:S(2)}, u32[]{:S(2)}) %collective-permute-start.2) | collective-permute-done | bytes 184352 | tf_op jit(solution)/shard_map/ppermute | solution.py:577
  51.5 3.3 %collective-permute-done.5 = bf16[120,768]{1,0:T(8,128)(2,1)S(1)} collective-permute-done((bf16[120,768]{1,0:T(8,128)(2,1)S(1)}, bf16[120,768]{1,0:T(8,128)(2,1)S(1)}, u32[]{:S(2)}, u32[]{:S(2)}) %collective-permute-start.5) | collective-permute-done | bytes 184352 | tf_op jit(solution)/shard_map/ppermute | solution.py:577
  66.7 44.5 %all-gather.2.cloned.1.call-done.both_ref = bf16[2048,3072]{1,0:T(8,128)(2,1)} async-done(((bf16[128,3072]{1,0:T(8,128)(2,1)}), bf16[2048,3072]{1,0:T(8,128)(2,1)}) %all-gather.2.cloned.1.call-update) | async-done | bytes 12582928 | tf_op jit(solution)/shard_map/all_gather | solution.py:674
  111.2 20.9 %ssd_forward.1 = (bf16[2048,768]{1,0:T(8,128)(2,1)}, bf16[2048,512]{1,0:T(8,128)(2,1)}, bf16[2048,512]{1,0:T(8,128)(2,1)}, bf16[2048,192]{1,0:T(8,128)(2,1)}, bf...) custom-call(bf16[2048,3072]{1,0:T(8,128)(2,1)} %all-gather.2.cloned., ...), custom_call_target="tpu_custom_call" | custom-call | tf_op jit(solution)/shard_map/ssd_forward/pallas_call | solution.py:449
  133.1 3.0 %collective-permute-start.10 = (f32[32,128]{1,0:T(8,128)S(1)}, f32[32,128]{1,0:T(8,128)S(1)}, u32[]{:S(2)}, u32[]{:S(2)}) collective-permute-start(f32[32,128]{1,0:T(8,128)S(1)} %reshape.275), channel_id=1, source_target_pairs={{0,2},{1,3},{2,0},{3,1},{4,6},{5,7},{6,4},{7,5},{8,10},{9,11},{10,... | collective-permute-start | bytes 49160 | tf_op jit(solution)/shard_map/ppermute | solution.py:569
  139.8 2.4 collective-permute-done.8
  147.7 2.4 collective-permute-done.11
  150.9 38.8 %ssd_backward.1 = (bf16[4,64,1536]{2,1,0:T(8,128)(2,1)}, bf16[4,64,1536]{2,1,0:T(8,128)(2,1)}, bf16[4,64,1536]{2,1,0:T(8,128)(2,1)}, bf16[4,64,1536]{2,1,0:T(8,1...) custom-call(s32[2]{0:T(128)} %pad_add_fusion.place_ref, ...), custom_call_target="tpu_custom_call" | custom-call | tf_op jit(solution)/shard_map/ssd_backward/pallas_call | solution.py:499
  192.0 4.0 %reduce-scatter.4.cloned.1.call-done = bf16[512,1536]{1,0:T(8,128)(2,1)} async-done(((bf16[2048,1536]{1,0:T(8,128)(2,1)}), bf16[512,1536]{1,0:T(8,128)(2,1)}) %reduce-scatter.4.cloned.1.call-update) | async-done | bytes 1572880 | tf_op jit(solution)/shard_map/reduce_scatter | solution.py:709
  202.6 5.5 %collective-permute-done.23 = bf16[2,64,1536]{2,1,0:T(8,128)(2,1)S(1)} collective-permute-done((bf16[2,64,1536]{2,1,0:T(8,128)(2,1)S(1)}, bf16[2,64,1536]{2,1,0:T(8,128)(2,1)S(1)}, u32[]{:S(2)}, u32[]{:S(2)}) %collective-permute-start.23) | collective-permute-done | bytes 393248 | tf_op jit(solution)/shard_map/ppermute | solution.py:569
  208.3 2.1 collective-permute-start.24
  210.4 2.3 collective-permute-done.21
  215.8 11.1 %collective-permute-done.24 = bf16[4,64,1536]{2,1,0:T(8,128)(2,1)S(1)} collective-permute-done((bf16[4,64,1536]{2,1,0:T(8,128)(2,1)S(1)}, bf16[4,64,1536]{2,1,0:T(8,128)(2,1)S(1)}, u32[]{:S(2)}, u32[]{:S(2)}) %collective-permute-start.24) | collective-permute-done | bytes 786464 | tf_op jit(solution)/shard_map/ppermute | solution.py:569
  226.9 5.0 %collective-permute-done.22 = bf16[4,64,1536]{2,1,0:T(8,128)(2,1)S(1)} collective-permute-done((bf16[4,64,1536]{2,1,0:T(8,128)(2,1)S(1)}, bf16[4,64,1536]{2,1,0:T(8,128)(2,1)S(1)}, u32[]{:S(2)}, u32[]{:S(2)}) %collective-permute-start.22) | collective-permute-done | bytes 786464 | tf_op jit(solution)/shard_map/ppermute | solution.py:569
  236.5 3.4 %collective-permute-start.18 = (bf16[64,1536]{1,0:T(8,128)(2,1)S(1)}, bf16[64,1536]{1,0:T(8,128)(2,1)S(1)}, u32[]{:S(2)}, u32[]{:S(2)}) collective-permute-start(bf16[64,1536]{1,0:T(8,128)(2,1)S(1)} %get-tuple-element.65), channel_id=1, source_target_pairs={{0,2},{1,3},{2,0},{3,1},{4,6},{5,7},{6,4},{7,5},{8,10},{9,11},{10,... | collective-permute-start | bytes 589832 | tf_op jit(solution)/shard_map/ppermute | solution.py:569
  239.8 3.5 %collective-permute-start.20 = (bf16[64,1536]{1,0:T(8,128)(2,1)S(1)}, bf16[64,1536]{1,0:T(8,128)(2,1)S(1)}, u32[]{:S(2)}, u32[]{:S(2)}) collective-permute-start(bf16[64,1536]{1,0:T(8,128)(2,1)S(1)} %get-tuple-element.66), channel_id=1, source_target_pairs={{0,3},{1,0},{2,1},{3,2},{4,7},{5,4},{6,5},{7,6},{8,11},{9,8},{10,9... | collective-permute-start | bytes 589832 | tf_op jit(solution)/shard_map/ppermute | solution.py:569
  244.3 5.6 %collective-permute-done.20 = bf16[64,1536]{1,0:T(8,128)(2,1)S(1)} collective-permute-done((bf16[64,1536]{1,0:T(8,128)(2,1)S(1)}, bf16[64,1536]{1,0:T(8,128)(2,1)S(1)}, u32[]{:S(2)}, u32[]{:S(2)}) %collective-permute-start.20) | collective-permute-done | bytes 196640 | tf_op jit(solution)/shard_map/ppermute | solution.py:569
  252.0 8.9 %all-to-all-start.1 = ((bf16[16,16,768]{2,1,0:T(8,128)(2,1)}), bf16[16,16,768]{2,1,0:T(8,128)(2,1)S(1)}, u32[]{:S(2)}, u32[]{:S(2)}) async-start(bf16[16,16,768]{2,1,0:T(8,128)(2,1)} %pad_maximum_fusion.7), calls=%async_computation.4 | async-start | bytes 786432 | tf_op jit(solution)/shard_map/all_to_all | solution.py:731
  262.3 9.7 %all-to-all-done.1 = bf16[16,16,768]{2,1,0:T(8,128)(2,1)S(1)} async-done(((bf16[16,16,768]{2,1,0:T(8,128)(2,1)}), bf16[16,16,768]{2,1,0:T(8,128)(2,1)S(1)}, u32[]{:S(2)}, u32[]{:S(2)}) %all-to-all-start.1) | async-done | bytes 393248 | tf_op jit(solution)/shard_map/all_to_all | solution.py:731
  (251 shorter events, 62.2 us)
Async XLA Ops:
  7.2 104.0 %all-gather.2.cloned.1.call-start = ((), (), s32[]{:S(2)}) async-start(), calls=%async_computation.5 | async-start | bytes 13369344 | tf_op jit(solution)/shard_map/all_gather | solution.py:674
  14.4 17.8 %all-to-all-start = ((bf16[16,12,768]{2,1,0:T(8,128)(2,1)}), bf16[16,12,768]{2,1,0:T(8,128)(2,1)S(1)}, u32[]{:S(2)}, u32[]{:S(2)}) async-start(bf16[16,12,768]{2,1,0:T(8,128)(2,1)} %bitcast.3), calls=%async_computation | async-start | bytes 786432 | tf_op jit(solution)/shard_map/all_to_all | solution.py:683
  21.5 174.4 %reduce-scatter.4.cloned.1.call-start = ((), (), s32[]{:S(2)}) async-start(), calls=%async_computation.6 | async-start | bytes 7864320 | tf_op jit(solution)/shard_map/reduce_scatter | solution.py:709
  32.3 12.0 %collective-permute-start.4 = (bf16[120,768]{1,0:T(8,128)(2,1)S(1)}, bf16[120,768]{1,0:T(8,128)(2,1)S(1)}, u32[]{:S(2)}, u32[]{:S(2)}) collective-permute-start(bf16[120,768]{1,0:T(8,128)(2,1)S(1)} %slice.203), channel_id=1, source_target_pairs={{0,96},{16,112},{32,0},{48,16},{64,32},{80,48},{96,64},{112,80},{1... | collective-permute-start | bytes 552968 | tf_op jit(solution)/shard_map/ppermute | solution.py:577
  39.6 8.4 %collective-permute-start.1 = (bf16[120,768]{1,0:T(8,128)(2,1)S(1)}, bf16[120,768]{1,0:T(8,128)(2,1)S(1)}, u32[]{:S(2)}, u32[]{:S(2)}) collective-permute-start(bf16[120,768]{1,0:T(8,128)(2,1)S(1)} %slice.154), channel_id=1, source_target_pairs={{0,32},{16,48},{32,64},{48,80},{64,96},{80,112},{96,0},{112,16},{1... | collective-permute-start | bytes 552968 | tf_op jit(solution)/shard_map/ppermute | solution.py:577
  39.8 11.6 %collective-permute-start.2 = (bf16[120,768]{1,0:T(8,128)(2,1)S(1)}, bf16[120,768]{1,0:T(8,128)(2,1)S(1)}, u32[]{:S(2)}, u32[]{:S(2)}) collective-permute-start(bf16[120,768]{1,0:T(8,128)(2,1)S(1)} %slice.203), channel_id=1, source_target_pairs={{0,32},{16,48},{32,64},{48,80},{64,96},{80,112},{96,0},{112,16},{1... | collective-permute-start | bytes 552968 | tf_op jit(solution)/shard_map/ppermute | solution.py:577
  39.9 11.5 %collective-permute-start.3 = (bf16[120,768]{1,0:T(8,128)(2,1)S(1)}, bf16[120,768]{1,0:T(8,128)(2,1)S(1)}, u32[]{:S(2)}, u32[]{:S(2)}) collective-permute-start(bf16[120,768]{1,0:T(8,128)(2,1)S(1)} %slice.154), channel_id=1, source_target_pairs={{0,96},{16,112},{32,0},{48,16},{64,32},{80,48},{96,64},{112,80},{1... | collective-permute-start | bytes 552968 | tf_op jit(solution)/shard_map/ppermute | solution.py:577
  44.3 10.5 %collective-permute-start.6 = (bf16[120,768]{1,0:T(8,128)(2,1)S(1)}, bf16[120,768]{1,0:T(8,128)(2,1)S(1)}, u32[]{:S(2)}, u32[]{:S(2)}) collective-permute-start(bf16[120,768]{1,0:T(8,128)(2,1)S(1)} %collective-permute-done.4), channel_id=1, source_target_pairs={{0,96},{16,112},{32,0},{48,16},{64,32},{80,48},{96,64},{112,80},{1... | collective-permute-start | bytes 552968 | tf_op jit(solution)/shard_map/ppermute | solution.py:577
  132.2 112.1 %reduce-scatter.6.cloned.1.call-start = ((), (), s32[]{:S(2)}) async-start(), calls=%async_computation.7 | async-start | bytes 3428352 | tf_op jit(solution)/shard_map/reduce_scatter | solution.py:722
  196.0 82.3 %reduce-scatter.8.cloned.1.call-start = ((), (), s32[]{:S(2)}) async-start(), calls=%async_computation.8 | async-start | bytes 1966080 | tf_op jit(solution)/shard_map/reduce_scatter | solution.py:724
  197.1 11.0 %collective-permute-start.23 = (bf16[2,64,1536]{2,1,0:T(8,128)(2,1)S(1)}, bf16[2,64,1536]{2,1,0:T(8,128)(2,1)S(1)}, u32[]{:S(2)}, u32[]{:S(2)}) collective-permute-start(bf16[2,64,1536]{2,1,0:T(8,128)(2,1)S(1)} %get-tuple-element.74), channel_id=1, source_target_pairs={{0,3},{1,0},{2,1},{3,2},{4,7},{5,4},{6,5},{7,6},{8,11},{9,8},{10,9... | collective-permute-start | bytes 1179656 | tf_op jit(solution)/shard_map/ppermute | solution.py:569
  198.1 16.9 %collective-permute-start.14 = (bf16[2,64,1536]{2,1,0:T(8,128)(2,1)S(1)}, bf16[2,64,1536]{2,1,0:T(8,128)(2,1)S(1)}, u32[]{:S(2)}, u32[]{:S(2)}) collective-permute-start(bf16[2,64,1536]{2,1,0:T(8,128)(2,1)S(1)} %get-tuple-element.68), channel_id=1, source_target_pairs={{0,4},{1,5},{2,6},{3,7},{4,8},{5,9},{6,10},{7,11},{8,12},{9,13},{1... | collective-permute-start | bytes 1179656 | tf_op jit(solution)/shard_map/ppermute | solution.py:573
  199.7 13.3 %collective-permute-start.16 = (bf16[2,64,1536]{2,1,0:T(8,128)(2,1)S(1)}, bf16[2,64,1536]{2,1,0:T(8,128)(2,1)S(1)}, u32[]{:S(2)}, u32[]{:S(2)}) collective-permute-start(bf16[2,64,1536]{2,1,0:T(8,128)(2,1)S(1)} %get-tuple-element.69), channel_id=1, source_target_pairs={{0,12},{1,13},{2,14},{3,15},{4,0},{5,1},{6,2},{7,3},{8,4},{9,5},{1... | collective-permute-start | bytes 1179656 | tf_op jit(solution)/shard_map/ppermute | solution.py:573
  201.4 11.3 %collective-permute-start.21 = (bf16[2,64,1536]{2,1,0:T(8,128)(2,1)S(1)}, bf16[2,64,1536]{2,1,0:T(8,128)(2,1)S(1)}, u32[]{:S(2)}, u32[]{:S(2)}) collective-permute-start(bf16[2,64,1536]{2,1,0:T(8,128)(2,1)S(1)} %get-tuple-element.73), channel_id=1, source_target_pairs={{0,1},{1,2},{2,3},{3,0},{4,5},{5,6},{6,7},{7,4},{8,9},{9,10},{10,1... | collective-permute-start | bytes 1179656 | tf_op jit(solution)/shard_map/ppermute | solution.py:569
  208.3 18.6 %collective-permute-start.24 = (bf16[4,64,1536]{2,1,0:T(8,128)(2,1)S(1)}, bf16[4,64,1536]{2,1,0:T(8,128)(2,1)S(1)}, u32[]{:S(2)}, u32[]{:S(2)}) collective-permute-start(bf16[4,64,1536]{2,1,0:T(8,128)(2,1)S(1)} %pad_maximum_fusion.5), channel_id=1, source_target_pairs={{0,3},{1,0},{2,1},{3,2},{4,7},{5,4},{6,5},{7,6},{8,11},{9,8},{10,9... | collective-permute-start | bytes 2359304 | tf_op jit(solution)/shard_map/ppermute | solution.py:569
  212.9 19.0 %collective-permute-start.22 = (bf16[4,64,1536]{2,1,0:T(8,128)(2,1)S(1)}, bf16[4,64,1536]{2,1,0:T(8,128)(2,1)S(1)}, u32[]{:S(2)}, u32[]{:S(2)}) collective-permute-start(bf16[4,64,1536]{2,1,0:T(8,128)(2,1)S(1)} %pad_maximum_fusion.4), channel_id=1, source_target_pairs={{0,1},{1,2},{2,3},{3,0},{4,5},{5,6},{6,7},{7,4},{8,9},{9,10},{10,1... | collective-permute-start | bytes 2359304 | tf_op jit(solution)/shard_map/ppermute | solution.py:569
  213.2 22.9 %collective-permute-start.17 = (bf16[4,64,1536]{2,1,0:T(8,128)(2,1)S(1)}, bf16[4,64,1536]{2,1,0:T(8,128)(2,1)S(1)}, u32[]{:S(2)}, u32[]{:S(2)}) collective-permute-start(bf16[4,64,1536]{2,1,0:T(8,128)(2,1)S(1)} %pad_maximum_fusion.3), channel_id=1, source_target_pairs={{0,12},{1,13},{2,14},{3,15},{4,0},{5,1},{6,2},{7,3},{8,4},{9,5},{1... | collective-permute-start | bytes 2359304 | tf_op jit(solution)/shard_map/ppermute | solution.py:573
  215.2 20.8 %collective-permute-start.15 = (bf16[4,64,1536]{2,1,0:T(8,128)(2,1)S(1)}, bf16[4,64,1536]{2,1,0:T(8,128)(2,1)S(1)}, u32[]{:S(2)}, u32[]{:S(2)}) collective-permute-start(bf16[4,64,1536]{2,1,0:T(8,128)(2,1)S(1)} %pad_maximum_fusion.2), channel_id=1, source_target_pairs={{0,4},{1,5},{2,6},{3,7},{4,8},{5,9},{6,10},{7,11},{8,12},{9,13},{1... | collective-permute-start | bytes 2359304 | tf_op jit(solution)/shard_map/ppermute | solution.py:573
  232.3 11.1 %collective-permute-start.25 = (bf16[64,1536]{1,0:T(8,128)(2,1)S(1)}, bf16[64,1536]{1,0:T(8,128)(2,1)S(1)}, u32[]{:S(2)}, u32[]{:S(2)}) collective-permute-start(bf16[64,1536]{1,0:T(8,128)(2,1)S(1)} %get-tuple-element.70), channel_id=1, source_target_pairs={{0,8},{1,9},{2,10},{3,11},{4,12},{5,13},{6,14},{7,15},{8,0},{9,1},... | collective-permute-start | bytes 589832 | tf_op jit(solution)/shard_map/ppermute | solution.py:573
  234.1 10.1 %collective-permute-start.27 = (bf16[64,1536]{1,0:T(8,128)(2,1)S(1)}, bf16[64,1536]{1,0:T(8,128)(2,1)S(1)}, u32[]{:S(2)}, u32[]{:S(2)}) collective-permute-start(bf16[64,1536]{1,0:T(8,128)(2,1)S(1)} %get-tuple-element.71), channel_id=1, source_target_pairs={{0,12},{1,13},{2,14},{3,15},{4,0},{5,1},{6,2},{7,3},{8,4},{9,5},{1... | collective-permute-start | bytes 589832 | tf_op jit(solution)/shard_map/ppermute | solution.py:573
  235.2 9.0 %collective-permute-start.26 = (bf16[64,1536]{1,0:T(8,128)(2,1)S(1)}, bf16[64,1536]{1,0:T(8,128)(2,1)S(1)}, u32[]{:S(2)}, u32[]{:S(2)}) collective-permute-start(bf16[64,1536]{1,0:T(8,128)(2,1)S(1)} %get-tuple-element.72), channel_id=1, source_target_pairs={{0,4},{1,5},{2,6},{3,7},{4,8},{5,9},{6,10},{7,11},{8,12},{9,13},{1... | collective-permute-start | bytes 589832 | tf_op jit(solution)/shard_map/ppermute | solution.py:573
  239.8 10.1 %collective-permute-start.20 = (bf16[64,1536]{1,0:T(8,128)(2,1)S(1)}, bf16[64,1536]{1,0:T(8,128)(2,1)S(1)}, u32[]{:S(2)}, u32[]{:S(2)}) collective-permute-start(bf16[64,1536]{1,0:T(8,128)(2,1)S(1)} %get-tuple-element.66), channel_id=1, source_target_pairs={{0,3},{1,0},{2,1},{3,2},{4,7},{5,4},{6,5},{7,6},{8,11},{9,8},{10,9... | collective-permute-start | bytes 589832 | tf_op jit(solution)/shard_map/ppermute | solution.py:569
  250.4 10.6 %collective-permute-start.28 = (bf16[48,768]{1,0:T(8,128)(2,1)S(1)}, bf16[48,768]{1,0:T(8,128)(2,1)S(1)}, u32[]{:S(2)}, u32[]{:S(2)}) collective-permute-start(bf16[48,768]{1,0:T(8,128)(2,1)S(1)} %slice.195), channel_id=1, source_target_pairs={{0,0},{16,1},{32,2},{48,3},{64,4},{80,5},{96,6},{112,7},{1,8},{17,... | collective-permute-start | bytes 221192 | tf_op jit(solution)/shard_map/ppermute | solution.py:732
  252.0 20.0 %all-to-all-start.1 = ((bf16[16,16,768]{2,1,0:T(8,128)(2,1)}), bf16[16,16,768]{2,1,0:T(8,128)(2,1)S(1)}, u32[]{:S(2)}, u32[]{:S(2)}) async-start(bf16[16,16,768]{2,1,0:T(8,128)(2,1)} %pad_maximum_fusion.7), calls=%async_computation.4 | async-start | bytes 786432 | tf_op jit(solution)/shard_map/all_to_all | solution.py:731
  (37 other events, 209.8 us)
Sparse Core Ops, SparseCore 0:
  12.3 98.8 all-gather.1
  132.3 63.6 reduce-scatter.3
  198.4 35.9 reduce-scatter.5
  244.4 30.0 reduce-scatter.7

commit v5 on v4

--- a/solution.py
+++ b/solution.py
@@ -10,6 +10,7 @@
 STATE = 128
 CONV = 4
 HEADS = 48
+HEADDIM = 64
 CONV_CH = 3328
 CHUNK = 128
 GROUP = 4
@@ -239,6 +240,7 @@
     bottom_2,
     bottom_3,
     grads_ref,
+    others_ref,
     later_ref,
     state_ref,
     conv_grad_ref,
@@ -424,21 +426,37 @@
         head = lax.broadcasted_iota(jnp.int32, (8, 256), 0)
         bias = jnp.sum(head_grad_ref[0], axis=1, keepdims=True)
         rate = jnp.sum(head_grad_ref[1], axis=1, keepdims=True)
-        heads = jnp.where((lane == head) & (head < OWN), bias, 0.0)
-        heads = heads + jnp.where((lane == head + OWN) & (head < OWN), rate, 0.0)
+        own = lax.broadcasted_iota(jnp.int32, (8, WIDE), 0) * HEADDIM
+        of_head = lax.broadcasted_iota(jnp.int32, (8, WIDE), 1) - own
+        skips = jnp.sum(skip_grad_ref[...], axis=0, keepdims=True)
+        skips = jnp.where((of_head >= 0) & (of_head < HEADDIM), skips, 0.0)
+        skips = jnp.sum(skips, axis=1, keepdims=True)
+        heads = jnp.zeros((8, 256), f32)
+        for q, value in enumerate((bias, rate, skips)):
+            at = 9 * place_ref[2] + OWN * q + head
+            high = value.astype(low).astype(f32)
+            rest = (value - high).astype(low).astype(f32)
+            heads = heads + jnp.where((lane == at) & (head < OWN), high, 0.0)
+            heads = heads + jnp.where((lane == at + 72) & (head < OWN), rest, 0.0)
         taps = [jnp.sum(conv_grad_ref[k], axis=0, keepdims=True) for k in range(CONV + 1)]
-        skips = jnp.sum(skip_grad_ref[...], axis=0, keepdims=True)
         for k in range(CONV):
             sums_ref[k : k + 1, 0:512] = taps[k]
         sums_ref[0:1, 512:PAD] = taps[CONV][:, 0:256]
         sums_ref[1:2, 512:PAD] = taps[CONV][:, 256:512]
-        sums_ref[2:3, 512 : 512 + WIDE] = skips
-        sums_ref[2:3, 512 + WIDE : PAD] = jnp.zeros((1, 256 - WIDE), f32)
+        sums_ref[2:3, 512:PAD] = jnp.zeros((1, 256), f32)
         sums_ref[3:4, 512:PAD] = jnp.sum(heads, axis=0, keepdims=True)
         high = sums_ref[0:4, :].astype(low).astype(f32)
         tail = jnp.concatenate([high, sums_ref[0:4, :] - high], axis=0)
         for d in range(8):
-            grads_ref[d] = jnp.concatenate([total_ref[d], tail], axis=0).astype(low)
+            own = jnp.concatenate([total_ref[d], tail], axis=0).astype(low)
+
+            @pl.when(lax.rem(place_ref[2], 2) == d % 2)
+            def _():
+                grads_ref[d // 2] = own
+
+            @pl.when(lax.rem(place_ref[2], 2) != d % 2)
+            def _():
+                others_ref[d // 2] = own
 
 
 def ssd_forward(both, w, w_out, rows, conv, heads, skip):
@@ -518,11 +536,13 @@
         ],
         out_specs=[
             *[whole((4, 64, D)) for _ in range(8)],
-            whole((8, 248, PAD)),
+            whole((4, 248, PAD)),
+            whole((4, 248, PAD)),
         ],
         out_shape=[
             *[jax.ShapeDtypeStruct((4, 64, D), low) for _ in range(8)],
-            jax.ShapeDtypeStruct((8, 248, PAD), low),
+            jax.ShapeDtypeStruct((4, 248, PAD), low),
+            jax.ShapeDtypeStruct((4, 248, PAD), low),
         ],
         scratch_shapes=[
             pltpu.VMEM((BLOCK + 8, 512), f32),
@@ -545,6 +565,7 @@
 epsilon = 1e-05
 BOTH = ("dp", "seq")
 X_GROUPS = [[4 * y + x for x in range(4)] for y in range(4)]
+Z_GROUPS = [[2 * z + core for z in range(4)] for core in range(2)]
 Y_GROUPS = [[4 * y + x for y in range(4)] for x in range(4)]
 
 
@@ -713,13 +734,16 @@
     r = lax.rsqrt(sums[0:1] / INNER + epsilon)
     c = r * r * r * (sums[1:2] / INNER)
 
-    place = jnp.stack([me % 4, me // 4])
-    *pieces, grads = ssd_backward(
+    place = jnp.stack([me % 4, me // 4, row])
+    *pieces, grads, others = ssd_backward(
         place, both, w_own, proj, by_chunk([segment, before, r, c]), conv, heads, skip, *saved
     )
     v, came = scattered_sum(pieces[:4], pieces[4:])
+    grads = added(grads, other_core(others)).reshape(4 * 248, PAD)
     grads, total = lax.optimization_barrier((grads, total))
-    grads = lax.psum_scatter(grads.reshape(8 * 248, PAD), "dp", scatter_dimension=0, tiled=True)
+    grads = lax.psum_scatter(
+        grads, "dp", scatter_dimension=0, tiled=True, axis_index_groups=Z_GROUPS
+    )
     grads, total = lax.optimization_barrier((grads, total))
     total = lax.psum_scatter(
         total, "seq", scatter_dimension=0, tiled=True, axis_index_groups=Y_GROUPS
@@ -746,11 +770,8 @@
     at = 26 * (16 * row + me)
     conv_sum = lax.dynamic_slice_in_dim(conv_sum, at, 26, 1)
     bias_sum = lax.dynamic_slice_in_dim(bias_sum, at, 26, 0)
-    head_sum = (
-        small[:, 3, 512 : 512 + OWN].reshape(HEADS),
-        small[:, 3, 512 + OWN : 512 + 2 * OWN].reshape(HEADS),
-        small[:, 2, 512 : 512 + WIDE].reshape(HEADS, 64).sum(axis=1),
-    )
+    head_sum = small[:, 3, 512:656].reshape(16, 16, 3, OWN).sum(axis=1)
+    head_sum = head_sum.transpose(1, 0, 2).reshape(3, HEADS)
     g_parts = g_parts.astype(f32).transpose(1, 0, 2)
     g_in = jnp.concatenate(
         [

time: 289 us -> 283 us (0.979)
  waiting for transfers between devices: 113 us -> 105 us
    ppermute x10, waiting for transfers between devices: 33.9 us -> 27.1 us  [along_x(): lax.ppermute(a, 'seq', [(s, s // 4 * 4 + (s % 4 + k) % 4) for s in range(...]
    reduce_scatter x1, waiting for transfers between devices: 3.95 us -> 0.01 us  [local(): lax.psum_scatter(partial_out.reshape(2048, D), 'seq', scatter_dimension=0...]
  transfers between devices with their start and end apart: 35 -> 36, of which waited for: 19 -> 20; matrix products, arithmetic and copies ran while one was open for 10% -> 12% of each run, Pallas kernels for 13% -> 14%
where the time goes in v5:
time: 283 us; the launch traced here: 282 us
  waiting for transfers between devices  105 us (37%)
  starting transfers between devices  59.9 us (21%)
  Pallas kernels  59.9 us (21%)
  local copies, waits for them, and re-layouts  22 us (8%)
  other arithmetic  20.5 us (7%)
  between operations  14.9 us (5%)
    all_gather x1, waiting for transfers between devices, local(): both = lax.all_gather(both, 'seq', axis=0, tiled=True)  44.5 us
    pallas_call x1, Pallas kernels, ssd_backward(): pl.pallas_call(backward_kernel, grid=(steps,), in_specs=[pl.BlockSpec(mem...  38.9 us
    ppermute x10, waiting for transfers between devices, along_x(): lax.ppermute(a, 'seq', [(s, s // 4 * 4 + (s % 4 + k) % 4) for s in range(...  27.1 us
    pallas_call x1, Pallas kernels, ssd_forward(): pl.pallas_call(forward_kernel, grid=(steps,), in_specs=[here(2 * D), whol...  20.9 us
    ppermute x10, starting transfers between devices, along_x(): lax.ppermute(a, 'seq', [(s, s // 4 * 4 + (s % 4 + k) % 4) for s in range(...  14.3 us
    ppermute x6, starting transfers between devices, along_z(): lax.ppermute(a, 'dp', [(d, (d // 2 + k) % 4 * 2 + d % 2) for d in range(8)])  14.3 us
    ppermute x10, starting transfers between devices, along_y(): lax.ppermute(a, 'seq', [(s, (s // 4 + k) % 4 * 4 + s % 4) for s in range(...  13.4 us
    all_to_all x1, waiting for transfers between devices, local(): parts = lax.all_to_all(parts, 'seq', 0, 0, tiled=True)  9.77 us
  transfers between devices with their start and end apart: 36, of which 20 were waited for; matrix products, arithmetic and copies ran while one was open for 12% of the time, Pallas kernels for 14%

profile of v5, /device:TPU:0, one launch (start us, length us, event | category | flops | bytes accessed | tf_op | source)
XLA Modules:
  0.0 281.9 jit_solution(610530351933773541)
XLA Ops:
  14.4 7.1 %all-to-all-start = ((bf16[16,12,768]{2,1,0:T(8,128)(2,1)}), bf16[16,12,768]{2,1,0:T(8,128)(2,1)S(1)}, u32[]{:S(2)}, u32[]{:S(2)}) async-start(bf16[16,12,768]{2,1,0:T(8,128)(2,1)} %bitcast.3), calls=%async_computation | async-start | bytes 786432 | tf_op jit(solution)/shard_map/all_to_all | solution.py:704
  22.4 9.8 %all-to-all-done = bf16[16,12,768]{2,1,0:T(8,128)(2,1)S(1)} async-done(((bf16[16,12,768]{2,1,0:T(8,128)(2,1)}), bf16[16,12,768]{2,1,0:T(8,128)(2,1)S(1)}, u32[]{:S(2)}, u32[]{:S(2)}) %all-to-all-start) | async-done | bytes 294944 | tf_op jit(solution)/shard_map/all_to_all | solution.py:704
  32.3 7.2 %collective-permute-start.4 = (bf16[120,768]{1,0:T(8,128)(2,1)S(1)}, bf16[120,768]{1,0:T(8,128)(2,1)S(1)}, u32[]{:S(2)}, u32[]{:S(2)}) collective-permute-start(bf16[120,768]{1,0:T(8,128)(2,1)S(1)} %slice.210), channel_id=1, source_target_pairs={{0,96},{16,112},{32,0},{48,16},{64,32},{80,48},{96,64},{112,80},{1... | collective-permute-start | bytes 552968 | tf_op jit(solution)/shard_map/ppermute | solution.py:598
  39.8 3.2 %collective-permute-start.3 = (bf16[120,768]{1,0:T(8,128)(2,1)S(1)}, bf16[120,768]{1,0:T(8,128)(2,1)S(1)}, u32[]{:S(2)}, u32[]{:S(2)}) collective-permute-start(bf16[120,768]{1,0:T(8,128)(2,1)S(1)} %slice.160), channel_id=1, source_target_pairs={{0,96},{16,112},{32,0},{48,16},{64,32},{80,48},{96,64},{112,80},{1... | collective-permute-start | bytes 552968 | tf_op jit(solution)/shard_map/ppermute | solution.py:598
  44.3 3.7 %collective-permute-start.6 = (bf16[120,768]{1,0:T(8,128)(2,1)S(1)}, bf16[120,768]{1,0:T(8,128)(2,1)S(1)}, u32[]{:S(2)}, u32[]{:S(2)}) collective-permute-start(bf16[120,768]{1,0:T(8,128)(2,1)S(1)} %collective-permute-done.4), channel_id=1, source_target_pairs={{0,96},{16,112},{32,0},{48,16},{64,32},{80,48},{96,64},{112,80},{1... | collective-permute-start | bytes 552968 | tf_op jit(solution)/shard_map/ppermute | solution.py:598
  48.0 3.3 %collective-permute-done.2 = bf16[120,768]{1,0:T(8,128)(2,1)S(1)} collective-permute-done((bf16[120,768]{1,0:T(8,128)(2,1)S(1)}, bf16[120,768]{1,0:T(8,128)(2,1)S(1)}, u32[]{:S(2)}, u32[]{:S(2)}) %collective-permute-start.2) | collective-permute-done | bytes 184352 | tf_op jit(solution)/shard_map/ppermute | solution.py:598
  51.4 3.3 %collective-permute-done.5 = bf16[120,768]{1,0:T(8,128)(2,1)S(1)} collective-permute-done((bf16[120,768]{1,0:T(8,128)(2,1)S(1)}, bf16[120,768]{1,0:T(8,128)(2,1)S(1)}, u32[]{:S(2)}, u32[]{:S(2)}) %collective-permute-start.5) | collective-permute-done | bytes 184352 | tf_op jit(solution)/shard_map/ppermute | solution.py:598
  66.6 44.5 %all-gather.2.cloned.1.call-done.both_ref = bf16[2048,3072]{1,0:T(8,128)(2,1)} async-done(((bf16[128,3072]{1,0:T(8,128)(2,1)}), bf16[2048,3072]{1,0:T(8,128)(2,1)}) %all-gather.2.cloned.1.call-update) | async-done | bytes 12582928 | tf_op jit(solution)/shard_map/all_gather | solution.py:695
  111.1 20.9 %ssd_forward.1 = (bf16[2048,768]{1,0:T(8,128)(2,1)}, bf16[2048,512]{1,0:T(8,128)(2,1)}, bf16[2048,512]{1,0:T(8,128)(2,1)}, bf16[2048,192]{1,0:T(8,128)(2,1)}, bf...) custom-call(bf16[2048,3072]{1,0:T(8,128)(2,1)} %all-gather.2.cloned., ...), custom_call_target="tpu_custom_call" | custom-call | tf_op jit(solution)/shard_map/ssd_forward/pallas_call | solution.py:467
  133.0 3.0 %collective-permute-start.10 = (f32[32,128]{1,0:T(8,128)S(1)}, f32[32,128]{1,0:T(8,128)S(1)}, u32[]{:S(2)}, u32[]{:S(2)}) collective-permute-start(f32[32,128]{1,0:T(8,128)S(1)} %reshape.282), channel_id=1, source_target_pairs={{0,2},{1,3},{2,0},{3,1},{4,6},{5,7},{6,4},{7,5},{8,10},{9,11},{10,... | collective-permute-start | bytes 49160 | tf_op jit(solution)/shard_map/ppermute | solution.py:590
  139.8 2.4 collective-permute-done.8
  147.7 2.4 collective-permute-done.11
  150.8 38.9 %ssd_backward.1 = (bf16[4,64,1536]{2,1,0:T(8,128)(2,1)}, bf16[4,64,1536]{2,1,0:T(8,128)(2,1)}, bf16[4,64,1536]{2,1,0:T(8,128)(2,1)}, bf16[4,64,1536]{2,1,0:T(8,1...) custom-call(s32[3]{0:T(128)} %pad_add_fusion.place_ref, ...), custom_call_target="tpu_custom_call" | custom-call | tf_op jit(solution)/shard_map/ssd_backward/pallas_call | solution.py:517
  193.9 3.2 %collective-permute-start.17 = (bf16[2,64,1536]{2,1,0:T(8,128)(2,1)S(1)}, bf16[2,64,1536]{2,1,0:T(8,128)(2,1)S(1)}, u32[]{:S(2)}, u32[]{:S(2)}) collective-permute-start(bf16[2,64,1536]{2,1,0:T(8,128)(2,1)S(1)} %get-tuple-element.67), channel_id=1, source_target_pairs={{0,12},{1,13},{2,14},{3,15},{4,0},{5,1},{6,2},{7,3},{8,4},{9,5},{1... | collective-permute-start | bytes 1179656 | tf_op jit(solution)/shard_map/ppermute | solution.py:594
  198.3 3.1 %collective-permute-done.24 = bf16[2,64,1536]{2,1,0:T(8,128)(2,1)S(1)} collective-permute-done((bf16[2,64,1536]{2,1,0:T(8,128)(2,1)S(1)}, bf16[2,64,1536]{2,1,0:T(8,128)(2,1)S(1)}, u32[]{:S(2)}, u32[]{:S(2)}) %collective-permute-start.24) | collective-permute-done | bytes 393248 | tf_op jit(solution)/shard_map/ppermute | solution.py:590
  203.2 3.3 %collective-permute-done.22 = bf16[2,64,1536]{2,1,0:T(8,128)(2,1)S(1)} collective-permute-done((bf16[2,64,1536]{2,1,0:T(8,128)(2,1)S(1)}, bf16[2,64,1536]{2,1,0:T(8,128)(2,1)S(1)}, u32[]{:S(2)}, u32[]{:S(2)}) %collective-permute-start.22) | collective-permute-done | bytes 393248 | tf_op jit(solution)/shard_map/ppermute | solution.py:590
  212.1 7.4 %collective-permute-done.25 = bf16[4,64,1536]{2,1,0:T(8,128)(2,1)} collective-permute-done((bf16[4,64,1536]{2,1,0:T(8,128)(2,1)S(1)}, bf16[4,64,1536]{2,1,0:T(8,128)(2,1)}, u32[]{:S(2)}, u32[]{:S(2)}) %collective-permute-start.25) | collective-permute-done | bytes 786464 | tf_op jit(solution)/shard_map/ppermute | solution.py:590
  219.6 3.6 %collective-permute-done.23 = bf16[4,64,1536]{2,1,0:T(8,128)(2,1)} collective-permute-done((bf16[4,64,1536]{2,1,0:T(8,128)(2,1)S(1)}, bf16[4,64,1536]{2,1,0:T(8,128)(2,1)}, u32[]{:S(2)}, u32[]{:S(2)}) %collective-permute-start.23) | collective-permute-done | bytes 786464 | tf_op jit(solution)/shard_map/ppermute | solution.py:590
  225.0 3.1 %collective-permute-start.26 = (bf16[64,1536]{1,0:T(8,128)(2,1)S(1)}, bf16[64,1536]{1,0:T(8,128)(2,1)S(1)}, u32[]{:S(2)}, u32[]{:S(2)}) collective-permute-start(bf16[64,1536]{1,0:T(8,128)(2,1)S(1)} %get-tuple-element.68), channel_id=1, source_target_pairs={{0,8},{1,9},{2,10},{3,11},{4,12},{5,13},{6,14},{7,15},{8,0},{9,1},... | collective-permute-start | bytes 589832 | tf_op jit(solution)/shard_map/ppermute | solution.py:594
  230.1 2.4 collective-permute-done.16
  232.8 3.1 %collective-permute-start.19 = (bf16[64,1536]{1,0:T(8,128)(2,1)S(1)}, bf16[64,1536]{1,0:T(8,128)(2,1)S(1)}, u32[]{:S(2)}, u32[]{:S(2)}) collective-permute-start(bf16[64,1536]{1,0:T(8,128)(2,1)S(1)} %get-tuple-element.63), channel_id=1, source_target_pairs={{0,2},{1,3},{2,0},{3,1},{4,6},{5,7},{6,4},{7,5},{8,10},{9,11},{10,... | collective-permute-start | bytes 589832 | tf_op jit(solution)/shard_map/ppermute | solution.py:590
  240.1 3.3 %collective-permute-done.21 = bf16[64,1536]{1,0:T(8,128)(2,1)S(1)} collective-permute-done((bf16[64,1536]{1,0:T(8,128)(2,1)S(1)}, bf16[64,1536]{1,0:T(8,128)(2,1)S(1)}, u32[]{:S(2)}, u32[]{:S(2)}) %collective-permute-start.21) | collective-permute-done | bytes 196640 | tf_op jit(solution)/shard_map/ppermute | solution.py:590
  245.5 9.2 %all-to-all-start.1 = ((bf16[16,16,768]{2,1,0:T(8,128)(2,1)}), bf16[16,16,768]{2,1,0:T(8,128)(2,1)S(1)}, u32[]{:S(2)}, u32[]{:S(2)}) async-start(bf16[16,16,768]{2,1,0:T(8,128)(2,1)} %pad_maximum_fusion.7), calls=%async_computation.4 | async-start | bytes 786432 | tf_op jit(solution)/shard_map/all_to_all | solution.py:755
  256.2 9.7 %all-to-all-done.1 = bf16[16,16,768]{2,1,0:T(8,128)(2,1)S(1)} async-done(((bf16[16,16,768]{2,1,0:T(8,128)(2,1)}), bf16[16,16,768]{2,1,0:T(8,128)(2,1)S(1)}, u32[]{:S(2)}, u32[]{:S(2)}) %all-to-all-start.1) | async-done | bytes 393248 | tf_op jit(solution)/shard_map/all_to_all | solution.py:755
  (260 shorter events, 65.6 us)
Async XLA Ops:
  7.2 104.0 %all-gather.2.cloned.1.call-start = ((), (), s32[]{:S(2)}) async-start(), calls=%async_computation.5 | async-start | bytes 13369344 | tf_op jit(solution)/shard_map/all_gather | solution.py:695
  14.4 17.8 %all-to-all-start = ((bf16[16,12,768]{2,1,0:T(8,128)(2,1)}), bf16[16,12,768]{2,1,0:T(8,128)(2,1)S(1)}, u32[]{:S(2)}, u32[]{:S(2)}) async-start(bf16[16,12,768]{2,1,0:T(8,128)(2,1)} %bitcast.3), calls=%async_computation | async-start | bytes 786432 | tf_op jit(solution)/shard_map/all_to_all | solution.py:704
  21.5 188.1 %reduce-scatter.4.cloned.1.call-start = ((), (), s32[]{:S(2)}) async-start(), calls=%async_computation.6 | async-start | bytes 7864320 | tf_op jit(solution)/shard_map/reduce_scatter | solution.py:730
  32.3 12.0 %collective-permute-start.4 = (bf16[120,768]{1,0:T(8,128)(2,1)S(1)}, bf16[120,768]{1,0:T(8,128)(2,1)S(1)}, u32[]{:S(2)}, u32[]{:S(2)}) collective-permute-start(bf16[120,768]{1,0:T(8,128)(2,1)S(1)} %slice.210), channel_id=1, source_target_pairs={{0,96},{16,112},{32,0},{48,16},{64,32},{80,48},{96,64},{112,80},{1... | collective-permute-start | bytes 552968 | tf_op jit(solution)/shard_map/ppermute | solution.py:598
  39.6 8.4 %collective-permute-start.1 = (bf16[120,768]{1,0:T(8,128)(2,1)S(1)}, bf16[120,768]{1,0:T(8,128)(2,1)S(1)}, u32[]{:S(2)}, u32[]{:S(2)}) collective-permute-start(bf16[120,768]{1,0:T(8,128)(2,1)S(1)} %slice.160), channel_id=1, source_target_pairs={{0,32},{16,48},{32,64},{48,80},{64,96},{80,112},{96,0},{112,16},{1... | collective-permute-start | bytes 552968 | tf_op jit(solution)/shard_map/ppermute | solution.py:598
  39.8 11.6 %collective-permute-start.2 = (bf16[120,768]{1,0:T(8,128)(2,1)S(1)}, bf16[120,768]{1,0:T(8,128)(2,1)S(1)}, u32[]{:S(2)}, u32[]{:S(2)}) collective-permute-start(bf16[120,768]{1,0:T(8,128)(2,1)S(1)} %slice.210), channel_id=1, source_target_pairs={{0,32},{16,48},{32,64},{48,80},{64,96},{80,112},{96,0},{112,16},{1... | collective-permute-start | bytes 552968 | tf_op jit(solution)/shard_map/ppermute | solution.py:598
  39.8 11.5 %collective-permute-start.3 = (bf16[120,768]{1,0:T(8,128)(2,1)S(1)}, bf16[120,768]{1,0:T(8,128)(2,1)S(1)}, u32[]{:S(2)}, u32[]{:S(2)}) collective-permute-start(bf16[120,768]{1,0:T(8,128)(2,1)S(1)} %slice.160), channel_id=1, source_target_pairs={{0,96},{16,112},{32,0},{48,16},{64,32},{80,48},{96,64},{112,80},{1... | collective-permute-start | bytes 552968 | tf_op jit(solution)/shard_map/ppermute | solution.py:598
  44.3 10.5 %collective-permute-start.6 = (bf16[120,768]{1,0:T(8,128)(2,1)S(1)}, bf16[120,768]{1,0:T(8,128)(2,1)S(1)}, u32[]{:S(2)}, u32[]{:S(2)}) collective-permute-start(bf16[120,768]{1,0:T(8,128)(2,1)S(1)} %collective-permute-done.4), channel_id=1, source_target_pairs={{0,96},{16,112},{32,0},{48,16},{64,32},{80,48},{96,64},{112,80},{1... | collective-permute-start | bytes 552968 | tf_op jit(solution)/shard_map/ppermute | solution.py:598
  132.1 106.0 %reduce-scatter.6.cloned.1.call-start = ((), (), s32[]{:S(2)}) async-start(), calls=%async_computation.7 | async-start | bytes 1904640 | tf_op jit(solution)/shard_map/reduce_scatter | solution.py:744
  192.2 9.3 %collective-permute-start.24 = (bf16[2,64,1536]{2,1,0:T(8,128)(2,1)S(1)}, bf16[2,64,1536]{2,1,0:T(8,128)(2,1)S(1)}, u32[]{:S(2)}, u32[]{:S(2)}) collective-permute-start(bf16[2,64,1536]{2,1,0:T(8,128)(2,1)S(1)} %get-tuple-element.72), channel_id=1, source_target_pairs={{0,3},{1,0},{2,1},{3,2},{4,7},{5,4},{6,5},{7,6},{8,11},{9,8},{10,9... | collective-permute-start | bytes 1179656 | tf_op jit(solution)/shard_map/ppermute | solution.py:590
  193.9 15.9 %collective-permute-start.15 = (bf16[2,64,1536]{2,1,0:T(8,128)(2,1)}, bf16[2,64,1536]{2,1,0:T(8,128)(2,1)S(1)}, u32[]{:S(2)}, u32[]{:S(2)}) collective-permute-start(bf16[2,64,1536]{2,1,0:T(8,128)(2,1)} %get-tuple-element.66), channel_id=1, source_target_pairs={{0,4},{1,5},{2,6},{3,7},{4,8},{5,9},{6,10},{7,11},{8,12},{9,13},{1... | collective-permute-start | bytes 1179656 | tf_op jit(solution)/shard_map/ppermute | solution.py:594
  193.9 13.8 %collective-permute-start.17 = (bf16[2,64,1536]{2,1,0:T(8,128)(2,1)S(1)}, bf16[2,64,1536]{2,1,0:T(8,128)(2,1)S(1)}, u32[]{:S(2)}, u32[]{:S(2)}) collective-permute-start(bf16[2,64,1536]{2,1,0:T(8,128)(2,1)S(1)} %get-tuple-element.67), channel_id=1, source_target_pairs={{0,12},{1,13},{2,14},{3,15},{4,0},{5,1},{6,2},{7,3},{8,4},{9,5},{1... | collective-permute-start | bytes 1179656 | tf_op jit(solution)/shard_map/ppermute | solution.py:594
  197.2 9.3 %collective-permute-start.22 = (bf16[2,64,1536]{2,1,0:T(8,128)(2,1)S(1)}, bf16[2,64,1536]{2,1,0:T(8,128)(2,1)S(1)}, u32[]{:S(2)}, u32[]{:S(2)}) collective-permute-start(bf16[2,64,1536]{2,1,0:T(8,128)(2,1)S(1)} %get-tuple-element.71), channel_id=1, source_target_pairs={{0,1},{1,2},{2,3},{3,0},{4,5},{5,6},{6,7},{7,4},{8,9},{9,10},{10,1... | collective-permute-start | bytes 1179656 | tf_op jit(solution)/shard_map/ppermute | solution.py:590
  198.3 9.5 %collective-permute-start.14 = (bf16[4,248,768]{2,1,0:T(8,128)(2,1)S(1)}, bf16[4,248,768]{2,1,0:T(8,128)(2,1)S(1)}, u32[]{:S(2)}, u32[]{:S(2)}) collective-permute-start(bf16[4,248,768]{2,1,0:T(8,128)(2,1)S(1)} %copy-done.17), channel_id=1, source_target_pairs={{0,16},{16,0},{32,48},{48,32},{64,80},{80,64},{96,112},{112,96},{1... | collective-permute-start | bytes 4571144 | tf_op jit(solution)/shard_map/ppermute | solution.py:602
  201.6 17.9 %collective-permute-start.25 = (bf16[4,64,1536]{2,1,0:T(8,128)(2,1)S(1)}, bf16[4,64,1536]{2,1,0:T(8,128)(2,1)}, u32[]{:S(2)}, u32[]{:S(2)}) collective-permute-start(bf16[4,64,1536]{2,1,0:T(8,128)(2,1)S(1)} %pad_maximum_fusion.5), channel_id=1, source_target_pairs={{0,3},{1,0},{2,1},{3,2},{4,7},{5,4},{6,5},{7,6},{8,11},{9,8},{10,9... | collective-permute-start | bytes 2359304 | tf_op jit(solution)/shard_map/ppermute | solution.py:590
  206.7 16.4 %collective-permute-start.23 = (bf16[4,64,1536]{2,1,0:T(8,128)(2,1)S(1)}, bf16[4,64,1536]{2,1,0:T(8,128)(2,1)}, u32[]{:S(2)}, u32[]{:S(2)}) collective-permute-start(bf16[4,64,1536]{2,1,0:T(8,128)(2,1)S(1)} %pad_maximum_fusion.4), channel_id=1, source_target_pairs={{0,1},{1,2},{2,3},{3,0},{4,5},{5,6},{6,7},{7,4},{8,9},{9,10},{10,1... | collective-permute-start | bytes 2359304 | tf_op jit(solution)/shard_map/ppermute | solution.py:590
  209.6 62.7 %reduce-scatter.8.cloned.1.call-start = ((), (), s32[]{:S(2)}) async-start(), calls=%async_computation.8 | async-start | bytes 1966080 | tf_op jit(solution)/shard_map/reduce_scatter | solution.py:748
  209.8 20.3 %collective-permute-start.18 = (bf16[4,64,1536]{2,1,0:T(8,128)(2,1)S(1)}, bf16[4,64,1536]{2,1,0:T(8,128)(2,1)S(1)}, u32[]{:S(2)}, u32[]{:S(2)}) collective-permute-start(bf16[4,64,1536]{2,1,0:T(8,128)(2,1)S(1)} %pad_maximum_fusion.3), channel_id=1, source_target_pairs={{0,12},{1,13},{2,14},{3,15},{4,0},{5,1},{6,2},{7,3},{8,4},{9,5},{1... | collective-permute-start | bytes 2359304 | tf_op jit(solution)/shard_map/ppermute | solution.py:594
  211.0 21.5 %collective-permute-start.16 = (bf16[4,64,1536]{2,1,0:T(8,128)(2,1)S(1)}, bf16[4,64,1536]{2,1,0:T(8,128)(2,1)S(1)}, u32[]{:S(2)}, u32[]{:S(2)}) collective-permute-start(bf16[4,64,1536]{2,1,0:T(8,128)(2,1)S(1)} %pad_maximum_fusion.2), channel_id=1, source_target_pairs={{0,4},{1,5},{2,6},{3,7},{4,8},{5,9},{6,10},{7,11},{8,12},{9,13},{1... | collective-permute-start | bytes 2359304 | tf_op jit(solution)/shard_map/ppermute | solution.py:594
  225.0 11.9 %collective-permute-start.26 = (bf16[64,1536]{1,0:T(8,128)(2,1)S(1)}, bf16[64,1536]{1,0:T(8,128)(2,1)S(1)}, u32[]{:S(2)}, u32[]{:S(2)}) collective-permute-start(bf16[64,1536]{1,0:T(8,128)(2,1)S(1)} %get-tuple-element.68), channel_id=1, source_target_pairs={{0,8},{1,9},{2,10},{3,11},{4,12},{5,13},{6,14},{7,15},{8,0},{9,1},... | collective-permute-start | bytes 589832 | tf_op jit(solution)/shard_map/ppermute | solution.py:594
  228.1 10.0 %collective-permute-start.28 = (bf16[64,1536]{1,0:T(8,128)(2,1)S(1)}, bf16[64,1536]{1,0:T(8,128)(2,1)S(1)}, u32[]{:S(2)}, u32[]{:S(2)}) collective-permute-start(bf16[64,1536]{1,0:T(8,128)(2,1)S(1)} %get-tuple-element.69), channel_id=1, source_target_pairs={{0,12},{1,13},{2,14},{3,15},{4,0},{5,1},{6,2},{7,3},{8,4},{9,5},{1... | collective-permute-start | bytes 589832 | tf_op jit(solution)/shard_map/ppermute | solution.py:594
  229.5 8.6 %collective-permute-start.27 = (bf16[64,1536]{1,0:T(8,128)(2,1)S(1)}, bf16[64,1536]{1,0:T(8,128)(2,1)S(1)}, u32[]{:S(2)}, u32[]{:S(2)}) collective-permute-start(bf16[64,1536]{1,0:T(8,128)(2,1)S(1)} %get-tuple-element.70), channel_id=1, source_target_pairs={{0,4},{1,5},{2,6},{3,7},{4,8},{5,9},{6,10},{7,11},{8,12},{9,13},{1... | collective-permute-start | bytes 589832 | tf_op jit(solution)/shard_map/ppermute | solution.py:594
  243.9 10.9 %collective-permute-start.29 = (bf16[48,768]{1,0:T(8,128)(2,1)S(1)}, bf16[48,768]{1,0:T(8,128)(2,1)S(1)}, u32[]{:S(2)}, u32[]{:S(2)}) collective-permute-start(bf16[48,768]{1,0:T(8,128)(2,1)S(1)} %slice.202), channel_id=1, source_target_pairs={{0,0},{16,1},{32,2},{48,3},{64,4},{80,5},{96,6},{112,7},{1,8},{17,... | collective-permute-start | bytes 221192 | tf_op jit(solution)/shard_map/ppermute | solution.py:756
  245.5 20.3 %all-to-all-start.1 = ((bf16[16,16,768]{2,1,0:T(8,128)(2,1)}), bf16[16,16,768]{2,1,0:T(8,128)(2,1)S(1)}, u32[]{:S(2)}, u32[]{:S(2)}) async-start(bf16[16,16,768]{2,1,0:T(8,128)(2,1)} %pad_maximum_fusion.7), calls=%async_computation.4 | async-start | bytes 786432 | tf_op jit(solution)/shard_map/all_to_all | solution.py:755
  (38 other events, 198.7 us)
Sparse Core Ops, SparseCore 0:
  12.2 98.8 all-gather.1
  132.2 63.6 reduce-scatter.3
  209.7 23.8 reduce-scatter.5
  238.3 30.6 reduce-scatter.7
